TPU v7x, 32 devices: a whole 2x2x4 slice. The times are simulated.
32 devices in a mesh: fsdp: 4 (over z), ctx: 2 (over x), tp: 4 (over y, core).
Axes of the slice: x: 2, y: 2, z: 4, core: 2. Of those that a mesh axis runs over, the one named last changes fastest.
Arguments:
- layer_input: float32 [12288, 1536], P(('fsdp', 'ctx')), may hold values from -6 to 6
- doc_lengths: int32 [4, 3], P('fsdp'), may hold values from 1 to 2048, 3072 in all within a row
- attention_gain: bfloat16 [1536], P('fsdp'), may hold values from 0.5 to 1.5
- query_weight: bfloat16 [1536, 1536], P('fsdp', 'tp'), may hold values from -0.15625 to 0.15625
- key_matrix: bfloat16 [1536, 768], P('fsdp', 'tp'), may hold values from -0.15625 to 0.15625
- value_matrix: bfloat16 [1536, 768], P('fsdp', 'tp'), may hold values from -0.15625 to 0.15625
- output_weight: bfloat16 [1536, 1536], P('tp', 'fsdp'), may hold values from -0.875 to 0.875
- feedforward_gain: bfloat16 [1536], P('fsdp'), may hold values from 0.5 to 1.5
- gate_weight: bfloat16 [1536, 4096], P('fsdp', 'tp'), may hold values from -0.15625 to 0.15625
- up_weight: bfloat16 [1536, 4096], P('fsdp', 'tp'), may hold values from -0.15625 to 0.15625
- down_weight: bfloat16 [4096, 1536], P('tp', 'fsdp'), may hold values from -0.09375 to 0.09375
- output_cotangent: float32 [12288, 1536], P(('fsdp', 'ctx')), may hold values from -6 to 6
Outputs:
- layer_output: float32 [12288, 1536], P(('fsdp', 'ctx'))
- input_gradient: float32 [12288, 1536], P(('fsdp', 'ctx'))
- attention_gain_gradient: float32 [1536], P('fsdp')
- query_gradient: float32 [1536, 1536], P('fsdp', 'tp')
- key_gradient: float32 [1536, 768], P('fsdp', 'tp')
- value_gradient: float32 [1536, 768], P('fsdp', 'tp')
- output_gradient: float32 [1536, 1536], P('tp', 'fsdp')
- feedforward_gain_gradient: float32 [1536], P('fsdp')
- gate_gradient: float32 [1536, 4096], P('fsdp', 'tp')
- up_gradient: float32 [1536, 4096], P('fsdp', 'tp')
- down_gradient: float32 [4096, 1536], P('tp', 'fsdp')
Inputs may be any that keep to these rules, and one draw needn't show every extreme that they name: `doc_lengths`: each row holds the lengths of the 3 documents packed in order into the 3072 tokens of one group; a row sums to 3072 and its longest document has exactly 2048 tokens.
All inputs are finite; a program needn't handle non-finite values.
Results may differ from a plain program's by a relative error of at most 0.014.
Values may be sent and summed in bfloat16 or wider, within the bound.
A program may use at most 256 MiB of HBM per device.

v0:
```python
import math

import jax
import jax.numpy as jnp
from jax import lax
from jax.sharding import PartitionSpec as P

HEAD_SIZE = 96


EPSILON = 1e-05
THETA = 100000.0
NEGATIVE = -1e30


def contract_rows(left, right):
    return lax.dot_general(
        left, right, (((0,), (0,)), ((), ())), preferred_element_type=jnp.float32
    )


def contract_cols(left, right):
    return lax.dot_general(
        left, right, (((1,), (1,)), ((), ())), preferred_element_type=jnp.float32
    )


def rms_forward(value_rows):
    factor = lax.rsqrt(jnp.mean(value_rows * value_rows, axis=-1, keepdims=True) + EPSILON)
    return (value_rows * factor, factor)


def rms_backward(grad_norm, normed, factor, gain):
    gain_term = jnp.sum(grad_norm * normed, axis=0)
    inner = grad_norm * gain
    grad_in = factor * (inner - normed * jnp.mean(inner * normed, axis=-1, keepdims=True))
    return (grad_in, gain_term)


def doc_positions(lengths, first, count):
    ends = jnp.cumsum(lengths)
    starts = ends - lengths
    index = first + jnp.arange(count, dtype=jnp.int32)
    document_list = jnp.sum((index[None, :] >= ends[:, None]).astype(jnp.int32), axis=0)
    chosen = document_list[None, :] == jnp.arange(lengths.shape[0], dtype=jnp.int32)[:, None]
    start_of = jnp.sum(jnp.where(chosen, starts[:, None], 0), axis=0)
    return (document_list, index - start_of)


def rotary_tables(positions, head_dim):
    half = head_dim // 2
    freqs = THETA ** (-(jnp.arange(half, dtype=jnp.float32) * 2.0 / head_dim))
    angles = positions.astype(jnp.float32)[:, None] * freqs[None, :]
    return (jnp.cos(angles), jnp.sin(angles))


def apply_rotary(value_rows, cosine_table, sine_table):
    half = value_rows.shape[-1] // 2
    first, second = (value_rows[..., :half], value_rows[..., half:])
    cosine_table, sine_table = (cosine_table[:, None, :], sine_table[:, None, :])
    return jnp.concatenate(
        [first * cosine_table - second * sine_table, second * cosine_table + first * sine_table],
        axis=-1,
    )


def unrotate(value_rows, cosine_table, sine_table):
    half = value_rows.shape[-1] // 2
    first, second = (value_rows[..., :half], value_rows[..., half:])
    cosine_table, sine_table = (cosine_table[:, None, :], sine_table[:, None, :])
    return jnp.concatenate(
        [first * cosine_table + second * sine_table, second * cosine_table - first * sine_table],
        axis=-1,
    )


def per_device(
    layer_input,
    doc_lengths,
    attention_gain,
    query_weight,
    key_matrix,
    value_matrix,
    output_weight,
    feedforward_gain,
    gate_weight,
    up_weight,
    down_weight,
    output_cotangent,
):
    tokens = layer_input.shape[0]
    head_dim = HEAD_SIZE
    query_heads = query_weight.shape[1] // head_dim
    kv_heads = key_matrix.shape[1] // head_dim
    group = query_heads // kv_heads
    piece = lax.axis_index("ctx")
    lengths = doc_lengths[0]
    scale = 1.0 / math.sqrt(head_dim)
    block = math.gcd(tokens, 512)
    blocks = tokens // block
    attn_set = (
        lax.all_gather(attention_gain, "fsdp", axis=0, tiled=True),
        lax.all_gather(query_weight, "fsdp", axis=0, tiled=True),
        lax.all_gather(key_matrix, "fsdp", axis=0, tiled=True),
        lax.all_gather(value_matrix, "fsdp", axis=0, tiled=True),
        lax.all_gather(output_weight, "fsdp", axis=1, tiled=True),
    )
    gain_one = attn_set[0].astype(jnp.float32)
    normed_one, factor_one = rms_forward(layer_input)
    branch_one = (normed_one * gain_one).astype(jnp.bfloat16)
    queries = jnp.dot(branch_one, attn_set[1], preferred_element_type=jnp.float32)
    keys_raw = jnp.dot(branch_one, attn_set[2], preferred_element_type=jnp.float32)
    values_raw = jnp.dot(branch_one, attn_set[3], preferred_element_type=jnp.float32)
    docs_query, positions = doc_positions(lengths, piece * tokens, tokens)
    cosine_table, sine_table = rotary_tables(positions, head_dim)
    rotated_queries = apply_rotary(
        queries.reshape(tokens, query_heads, head_dim), cosine_table, sine_table
    ).astype(jnp.bfloat16)
    rotated_keys = apply_rotary(
        keys_raw.reshape(tokens, kv_heads, head_dim), cosine_table, sine_table
    ).astype(jnp.bfloat16)
    lowered_values = values_raw.astype(jnp.bfloat16).reshape(tokens, kv_heads, head_dim)
    key_first = piece * 0
    all_keys, all_values = (
        lax.all_gather(rotated_keys, "ctx", axis=0, tiled=True),
        lax.all_gather(lowered_values, "ctx", axis=0, tiled=True),
    )
    key_count = all_keys.shape[0]
    docs_key, _ = doc_positions(lengths, key_first, key_count)
    key_index = jnp.arange(key_count, dtype=jnp.int32)
    query_grouped = rotated_queries.reshape(tokens, kv_heads, group, head_dim)

    def scores_of(index):
        start = index * block
        query_block = lax.dynamic_slice_in_dim(query_grouped, start, block, 0)
        raw = (
            jnp.einsum("qhgd,khd->hgqk", query_block, all_keys, preferred_element_type=jnp.float32)
            * scale
        )
        query_index = piece * tokens + start + jnp.arange(block, dtype=jnp.int32)
        doc_block = lax.dynamic_slice_in_dim(docs_query, start, block, 0)
        allowed = (
            (key_index[None, :] >= 0)
            & (key_index[None, :] <= query_index[:, None])
            & (docs_key[None, :] == doc_block[:, None])
        )
        return (jnp.where(allowed[None, None], raw, NEGATIVE), query_block)

    def forward_block(index):
        scores, _ = scores_of(index)
        highest = jnp.max(scores, axis=-1, keepdims=True)
        total = jnp.sum(jnp.exp(scores - highest), axis=-1, keepdims=True)
        logsum = highest + jnp.log(total)
        probs = jnp.exp(scores - logsum).astype(jnp.bfloat16)
        result = jnp.einsum("hgqk,khd->qhgd", probs, all_values, preferred_element_type=jnp.float32)
        return (result.reshape(block, query_heads * head_dim), logsum[..., 0])

    outputs, logsums = lax.map(forward_block, jnp.arange(blocks, dtype=jnp.int32))
    attended_rows = outputs.reshape(tokens, query_heads * head_dim).astype(jnp.bfloat16)
    attn_partial = jnp.dot(attended_rows, attn_set[4], preferred_element_type=jnp.float32)
    mlp_set = (
        lax.all_gather(feedforward_gain, "fsdp", axis=0, tiled=True),
        lax.all_gather(gate_weight, "fsdp", axis=0, tiled=True),
        lax.all_gather(up_weight, "fsdp", axis=0, tiled=True),
        lax.all_gather(down_weight, "fsdp", axis=1, tiled=True),
    )
    gain_two = mlp_set[0].astype(jnp.float32)
    middle = layer_input + lax.psum(attn_partial, "tp")
    normed_two, factor_two = rms_forward(middle)
    branch_two = (normed_two * gain_two).astype(jnp.bfloat16)
    gate = jnp.dot(branch_two, mlp_set[1], preferred_element_type=jnp.float32)
    up_value = jnp.dot(branch_two, mlp_set[2], preferred_element_type=jnp.float32)
    sigmoid = jax.nn.sigmoid(gate)
    activated = gate * sigmoid
    hidden = (activated * up_value).astype(jnp.bfloat16)
    mlp_partial = jnp.dot(hidden, mlp_set[3], preferred_element_type=jnp.float32)
    layer_output = middle + lax.psum(mlp_partial.astype(jnp.bfloat16), "tp").astype(jnp.float32)
    feed_grad = output_cotangent.astype(jnp.bfloat16)
    down_grad = contract_rows(hidden, feed_grad)
    hidden_grad = contract_cols(feed_grad, mlp_set[3])
    slope = sigmoid * (1.0 + gate * (1.0 - sigmoid))
    gate_grad = (hidden_grad * up_value * slope).astype(jnp.bfloat16)
    up_grad = (hidden_grad * activated).astype(jnp.bfloat16)
    gate_wgrad = contract_rows(branch_two, gate_grad)
    up_wgrad = contract_rows(branch_two, up_grad)
    normed_two_part = contract_cols(gate_grad, mlp_set[1]) + contract_cols(up_grad, mlp_set[2])
    normed_two_grad = lax.psum(normed_two_part, "tp")
    middle_norm_grad, gain_two_grad = rms_backward(
        normed_two_grad, normed_two, factor_two, gain_two
    )
    middle_grad = output_cotangent + middle_norm_grad
    branch_grad = middle_grad.astype(jnp.bfloat16)
    output_wgrad = contract_rows(attended_rows, branch_grad)
    attended_grad = contract_cols(branch_grad, attn_set[4]).astype(jnp.bfloat16)
    grad_grouped = attended_grad.reshape(tokens, kv_heads, group, head_dim)

    def backward_block(carry, index):
        key_acc, value_acc = carry
        scores, query_block = scores_of(index)
        probs = jnp.exp(scores - logsums[index][..., None])
        grad_block = lax.dynamic_slice_in_dim(grad_grouped, index * block, block, 0)
        prob_grad = jnp.einsum(
            "qhgd,khd->hgqk", grad_block, all_values, preferred_element_type=jnp.float32
        )
        inner = jnp.sum(probs * prob_grad, axis=-1, keepdims=True)
        score_grad = (probs * (prob_grad - inner)).astype(jnp.bfloat16)
        query_grad = (
            jnp.einsum("hgqk,khd->qhgd", score_grad, all_keys, preferred_element_type=jnp.float32)
            * scale
        )
        key_acc = (
            key_acc
            + jnp.einsum(
                "hgqk,qhgd->khd", score_grad, query_block, preferred_element_type=jnp.float32
            )
            * scale
        )
        value_acc = value_acc + jnp.einsum(
            "hgqk,qhgd->khd",
            probs.astype(jnp.bfloat16),
            grad_block,
            preferred_element_type=jnp.float32,
        )
        return ((key_acc, value_acc), query_grad)

    empty = jnp.zeros((key_count, kv_heads, head_dim), jnp.float32)
    (key_grad_all, value_grad_all), query_grads = lax.scan(
        backward_block, (empty, empty), jnp.arange(blocks, dtype=jnp.int32)
    )
    key_grad_own, value_grad_own = (
        lax.psum_scatter(key_grad_all, "ctx", scatter_dimension=0, tiled=True),
        lax.psum_scatter(value_grad_all, "ctx", scatter_dimension=0, tiled=True),
    )
    query_grad_raw = (
        unrotate(query_grads.reshape(tokens, query_heads, head_dim), cosine_table, sine_table)
        .reshape(tokens, query_heads * head_dim)
        .astype(jnp.bfloat16)
    )
    key_grad_raw = (
        unrotate(key_grad_own, cosine_table, sine_table)
        .reshape(tokens, kv_heads * head_dim)
        .astype(jnp.bfloat16)
    )
    value_grad_raw = value_grad_own.reshape(tokens, kv_heads * head_dim).astype(jnp.bfloat16)
    query_wgrad = contract_rows(branch_one, query_grad_raw)
    key_wgrad = contract_rows(branch_one, key_grad_raw)
    value_wgrad = contract_rows(branch_one, value_grad_raw)
    normed_one_part = (
        contract_cols(query_grad_raw, attn_set[1])
        + contract_cols(key_grad_raw, attn_set[2])
        + contract_cols(value_grad_raw, attn_set[3])
    )
    normed_one_grad = lax.psum(normed_one_part, "tp")
    input_norm_grad, gain_one_grad = rms_backward(normed_one_grad, normed_one, factor_one, gain_one)
    input_gradient = middle_grad + input_norm_grad
    owned = (
        lax.psum_scatter(gain_one_grad, "fsdp", scatter_dimension=0, tiled=True),
        lax.psum_scatter(query_wgrad, "fsdp", scatter_dimension=0, tiled=True),
        lax.psum_scatter(key_wgrad, "fsdp", scatter_dimension=0, tiled=True),
        lax.psum_scatter(value_wgrad, "fsdp", scatter_dimension=0, tiled=True),
        lax.psum_scatter(output_wgrad, "fsdp", scatter_dimension=1, tiled=True),
        lax.psum_scatter(gain_two_grad, "fsdp", scatter_dimension=0, tiled=True),
        lax.psum_scatter(gate_wgrad, "fsdp", scatter_dimension=0, tiled=True),
        lax.psum_scatter(up_wgrad, "fsdp", scatter_dimension=0, tiled=True),
        lax.psum_scatter(down_grad, "fsdp", scatter_dimension=1, tiled=True),
    )
    summed = lax.psum(
        (owned[0], owned[1], owned[2], owned[3], owned[4], owned[5], owned[6], owned[7], owned[8]),
        "ctx",
    )
    return (
        layer_output,
        input_gradient,
        summed[0],
        summed[1],
        summed[2],
        summed[3],
        summed[4],
        summed[5],
        summed[6],
        summed[7],
        summed[8],
    )


def solution(mesh):
    placed = (
        P(("fsdp", "ctx"), None),
        P("fsdp", None),
        P("fsdp"),
        P("fsdp", "tp"),
        P("fsdp", "tp"),
        P("fsdp", "tp"),
        P("tp", "fsdp"),
        P("fsdp"),
        P("fsdp", "tp"),
        P("fsdp", "tp"),
        P("tp", "fsdp"),
        P(("fsdp", "ctx"), None),
    )
    return jax.shard_map(
        per_device,
        mesh=mesh,
        in_specs=placed,
        out_specs=(
            P(("fsdp", "ctx"), None),
            P(("fsdp", "ctx"), None),
            P("fsdp"),
            P("fsdp", "tp"),
            P("fsdp", "tp"),
            P("fsdp", "tp"),
            P("tp", "fsdp"),
            P("fsdp"),
            P("fsdp", "tp"),
            P("fsdp", "tp"),
            P("tp", "fsdp"),
        ),
        check_vma=False,
    )
```

profile of v0, /device:TPU:0, one launch (start us, length us, event | category | flops | bytes accessed | tf_op | source)
XLA Modules:
  0.0 2159.1 jit_solution(7084426157221471808)
XLA Ops:
  26.8 24.4 %all_gather.37 = bf16[1536,192]{0,1:T(8,128)(2,1)S(1)} all-gather(bf16[384,192]{0,1:T(8,128)(2,1)S(1)} %copy-done.21), channel_id=1, replica_groups=mesh['fsdp'=4,'ctx'=2,'tp'=4] {'fsdp'}, dimensions={0}, use_global_device_ids=true | all-gather | bytes 737280 | tf_op jit(solution)/shard_map/all_gather | solution.py:105
  104.4 123.4 %while.34 = (s32[]{:T(128)}, bf16[3,512,384]{2,1,0:T(8,128)(2,1)}, f32[3,2,2,512]{3,2,1,0:T(2,128)}, s32[3]{0:T(128)S(1)}, s32[]{:T(128)}, /*index=5*/s32[3072]{...) while((s32[]{:T(128)}, bf16[3,512,384]{2,1,0:T(8,128)(2,1)}, ...), condition=%wide.region_8.9_spmd.clone.clone, body=%wide.region_5.8_spmd.clone.clone.sunk | while | flops 2489842176 | bytes 91314440 | solution.py:158
  250.4 155.9 %all-reduce.11.cloned.1.call-done = f32[1536,1536]{1,0:T(8,128)} async-done(((f32[1536,1536]{1,0:T(8,128)}), f32[1536,1536]{1,0:T(8,128)}) %all-reduce.11.cloned.1.call-update) | async-done | bytes 9437200 | tf_op jit(solution)/shard_map/psum | solution.py:168
  424.2 47.2 %all-gather.20.cloned.1.call-done = bf16[1536,1024]{1,0:T(8,128)(2,1)} async-done(((bf16[384,1024]{1,0:T(8,128)(2,1)}), bf16[1536,1024]{1,0:T(8,128)(2,1)}) %all-gather.20.cloned.1.call-update) | async-done | bytes 3145744 | tf_op jit(solution)/shard_map/all_gather | solution.py:164
  481.3 53.8 %all-gather.18.cloned.1.call-done = bf16[1536,1024]{1,0:T(8,128)(2,1)} async-done(((bf16[384,1024]{1,0:T(8,128)(2,1)}), bf16[1536,1024]{1,0:T(8,128)(2,1)}) %all-gather.18.cloned.1.call-update) | async-done | bytes 3145744 | tf_op jit(solution)/shard_map/all_gather | solution.py:163
  544.9 53.9 %all-gather.22.cloned.1.call-done = bf16[1024,1536]{1,0:T(8,128)(2,1)} async-done(((bf16[1024,384]{1,0:T(8,128)(2,1)}), bf16[1024,1536]{1,0:T(8,128)(2,1)}) %all-gather.22.cloned.1.call-update) | async-done | bytes 3145744 | tf_op jit(solution)/shard_map/all_gather | solution.py:165
  641.3 159.2 %all-reduce.15.cloned.1.call-done = f32[1536,1536]{1,0:T(8,128)} async-done(((f32[1536,1536]{1,0:T(8,128)}), f32[1536,1536]{1,0:T(8,128)}) %all-reduce.15.cloned.1.call-update) | async-done | bytes 9437200 | tf_op jit(solution)/shard_map/psum | solution.py:187
  808.7 88.3 %all-reduce.13.cloned.1.call-done = bf16[1536,1536]{1,0:T(8,128)(2,1)} async-done(((bf16[1536,1536]{1,0:T(8,128)(2,1)}), bf16[1536,1536]{1,0:T(8,128)(2,1)}) %all-reduce.13.cloned.1.call-update) | async-done | bytes 4718608 | tf_op jit(solution)/shard_map/psum | solution.py:177
  916.6 314.6 %while.35 = (s32[]{:T(128)}, f32[3072,2,96]{0,2,1:T(8,128)}, f32[3072,2,96]{0,2,1:T(8,128)}, f32[3,512,2,2,96]{1,0,4,3,2:T(4,128)}, s32[3]{0:T(128)S(1)}, /*inde...) while((s32[]{:T(128)}, f32[3072,2,96]{0,2,1:T(8,128)}, ...), condition=%wide.region_16.17_spmd.clone.clone, body=%wide.region_14.16_spmd.clone.clone.sunk | while | flops 6142032384 | bytes 235616640 | solution.py:227
  964.9 21.4 fusion.149
  1052.0 17.7 fusion.148
  1069.8 21.4 fusion.149
  1156.9 17.7 fusion.148
  1174.6 21.4 fusion.149
  1272.1 31.1 %reduce-scatter.10.cloned.1.call-done = f32[1536,2,96]{0,2,1:T(8,128)} async-done(((f32[3072,2,96]{0,2,1:T(8,128)}), f32[1536,2,96]{0,2,1:T(8,128)}) %reduce-scatter.10.cloned.1.call-update) | async-done | bytes 1179664 | tf_op jit(solution)/shard_map/reduce_scatter | solution.py:231
  1353.5 49.7 %reduce-scatter.20.cloned.1.call-done = f32[384,384]{1,0:T(8,128)} async-done(((f32[384,1536]{1,0:T(8,128)}), f32[384,384]{1,0:T(8,128)}) %reduce-scatter.20.cloned.1.call-update) | async-done | bytes 589840 | tf_op jit(solution)/shard_map/reduce_scatter | solution.py:261
  1403.3 31.4 %reduce-scatter.18.cloned.1.call-done = f32[384,192]{0,1:T(8,128)} async-done(((f32[1536,192]{0,1:T(8,128)}), f32[384,192]{0,1:T(8,128)}) %reduce-scatter.18.cloned.1.call-update) | async-done | bytes 294928 | tf_op jit(solution)/shard_map/reduce_scatter | solution.py:260
  1434.7 30.7 %reduce-scatter.16.cloned.1.call-done = f32[384,192]{0,1:T(8,128)} async-done(((f32[1536,192]{0,1:T(8,128)}), f32[384,192]{0,1:T(8,128)}) %reduce-scatter.16.cloned.1.call-update) | async-done | bytes 294928 | tf_op jit(solution)/shard_map/reduce_scatter | solution.py:259
  1465.4 111.7 %reduce-scatter.26.cloned.1.call-done = f32[1024,384]{1,0:T(8,128)} async-done(((f32[1024,1536]{1,0:T(8,128)}), f32[1024,384]{1,0:T(8,128)}) %reduce-scatter.26.cloned.1.call-update) | async-done | bytes 1572880 | tf_op jit(solution)/shard_map/reduce_scatter | solution.py:265
  1577.0 113.5 %reduce-scatter.24.cloned.1.call-done = f32[384,1024]{1,0:T(8,128)} async-done(((f32[1536,1024]{1,0:T(8,128)}), f32[384,1024]{1,0:T(8,128)}) %reduce-scatter.24.cloned.1.call-update) | async-done | bytes 1572880 | tf_op jit(solution)/shard_map/reduce_scatter | solution.py:264
  1690.5 113.6 %reduce-scatter.22.cloned.1.call-done = f32[384,1024]{1,0:T(8,128)} async-done(((f32[1536,1024]{1,0:T(8,128)}), f32[384,1024]{1,0:T(8,128)}) %reduce-scatter.22.cloned.1.call-update) | async-done | bytes 1572880 | tf_op jit(solution)/shard_map/reduce_scatter | solution.py:263
  1805.4 171.4 %all-reduce.17.cloned.1.call-done = f32[1536,1536]{1,0:T(8,128)} async-done(((f32[1536,1536]{1,0:T(8,128)}), f32[1536,1536]{1,0:T(8,128)}) %all-reduce.17.cloned.1.call-update) | async-done | bytes 9437200 | tf_op jit(solution)/shard_map/psum | solution.py:253
  1984.3 18.7 all-reduce.2
  2023.2 116.4 %all-reduce.19.cloned.1.call-done = (f32[384,384]{1,0:T(8,128)}, f32[384,192]{0,1:T(8,128)}, f32[384,192]{0,1:T(8,128)}, f32[384,384]{1,0:T(8,128)}, f32[384,102...) async-done(((f32[384,384]{1,0:T(8,128)}, f32[384,192]{0,1:T(8,128)}, f32[384,192]{0,1:T(8,128)}, f32[384,384]{1,0:T(8,128)}, f32[384,1024]{1,0:T(8,128)}, ...) | async-done | bytes 6488080 | tf_op jit(solution)/shard_map/psum | solution.py:267
  (275 shorter events, 662.0 us)
Async XLA Ops:
  7.2 75.0 %all-gather.10.cloned.1.call-start = ((), (), s32[]{:S(2)}) async-start(), calls=%async_computation.9 | async-start | bytes 1474560 | tf_op jit(solution)/shard_map/all_gather | solution.py:103
  7.9 79.5 %all-gather.14.cloned.1.call-start = ((), (), s32[]{:S(2)}) async-start(), calls=%async_computation.11 | async-start | bytes 1769472 | tf_op jit(solution)/shard_map/all_gather | solution.py:126
  56.7 47.7 %all-gather.12.cloned.1.call-start = ((), (), s32[]{:S(2)}) async-start(), calls=%async_computation.10 | async-start | bytes 1769472 | tf_op jit(solution)/shard_map/all_gather | solution.py:125
  81.4 146.4 %all-gather.16.cloned.1.call-start = ((), (), s32[]{:S(2)}) async-start(), calls=%async_computation.12 | async-start | bytes 1474560 | tf_op jit(solution)/shard_map/all_gather | solution.py:106
  82.0 324.3 %all-reduce.11.cloned.1.call-start = ((), (), s32[]{:S(2)}) async-start(), calls=%async_computation.13 | async-start | bytes 18874368 | tf_op jit(solution)/shard_map/psum | solution.py:168
  236.3 235.1 %all-gather.20.cloned.1.call-start = ((), (), s32[]{:S(2)}) async-start(), calls=%async_computation.15 | async-start | bytes 3932160 | tf_op jit(solution)/shard_map/all_gather | solution.py:164
  236.8 298.3 %all-gather.18.cloned.1.call-start = ((), (), s32[]{:S(2)}) async-start(), calls=%async_computation.14 | async-start | bytes 3932160 | tf_op jit(solution)/shard_map/all_gather | solution.py:163
  237.6 361.1 %all-gather.22.cloned.1.call-start = ((), (), s32[]{:S(2)}) async-start(), calls=%async_computation.16 | async-start | bytes 3932160 | tf_op jit(solution)/shard_map/all_gather | solution.py:165
  238.3 562.2 %all-reduce.15.cloned.1.call-start = ((), (), s32[]{:S(2)}) async-start(), calls=%async_computation.18 | async-start | bytes 18874368 | tf_op jit(solution)/shard_map/psum | solution.py:187
  632.0 265.0 %all-reduce.13.cloned.1.call-start = ((), (), s32[]{:S(2)}) async-start(), calls=%async_computation.17 | async-start | bytes 9437184 | tf_op jit(solution)/shard_map/psum | solution.py:177
  641.3 624.9 %reduce-scatter.12.cloned.1.call-start = ((), (), s32[]{:S(2)}) async-start(), calls=%async_computation.20 | async-start | bytes 3538944 | tf_op jit(solution)/shard_map/reduce_scatter | solution.py:232
  1231.2 71.9 %reduce-scatter.10.cloned.1.call-start = ((), (), s32[]{:S(2)}) async-start(), calls=%async_computation.19 | async-start | bytes 3538944 | tf_op jit(solution)/shard_map/reduce_scatter | solution.py:231
  1231.8 121.8 %reduce-scatter.14.cloned.1.call-start = ((), (), s32[]{:S(2)}) async-start(), calls=%async_computation.22 | async-start | bytes 2949120 | tf_op jit(solution)/shard_map/reduce_scatter | solution.py:258
  1243.3 160.0 %reduce-scatter.20.cloned.1.call-start = ((), (), s32[]{:S(2)}) async-start(), calls=%async_computation.25 | async-start | bytes 2949120 | tf_op jit(solution)/shard_map/reduce_scatter | solution.py:261
  1250.5 184.2 %reduce-scatter.18.cloned.1.call-start = ((), (), s32[]{:S(2)}) async-start(), calls=%async_computation.24 | async-start | bytes 1474560 | tf_op jit(solution)/shard_map/reduce_scatter | solution.py:260
  1272.0 193.3 %reduce-scatter.16.cloned.1.call-start = ((), (), s32[]{:S(2)}) async-start(), calls=%async_computation.23 | async-start | bytes 1474560 | tf_op jit(solution)/shard_map/reduce_scatter | solution.py:259
  1309.1 267.9 %reduce-scatter.26.cloned.1.call-start = ((), (), s32[]{:S(2)}) async-start(), calls=%async_computation.28 | async-start | bytes 7864320 | tf_op jit(solution)/shard_map/reduce_scatter | solution.py:265
  1320.8 369.7 %reduce-scatter.24.cloned.1.call-start = ((), (), s32[]{:S(2)}) async-start(), calls=%async_computation.27 | async-start | bytes 7864320 | tf_op jit(solution)/shard_map/reduce_scatter | solution.py:264
  1330.8 473.3 %reduce-scatter.22.cloned.1.call-start = ((), (), s32[]{:S(2)}) async-start(), calls=%async_computation.26 | async-start | bytes 7864320 | tf_op jit(solution)/shard_map/reduce_scatter | solution.py:263
  1340.9 635.8 %all-reduce.17.cloned.1.call-start = ((), (), s32[]{:S(2)}) async-start(), calls=%async_computation.21 | async-start | bytes 18874368 | tf_op jit(solution)/shard_map/psum | solution.py:253
  1351.6 452.5 %copy-start.32 = (u32[32]{0:T(128)S(1)}, u32[32]{0:T(128)}, u32[]{:S(2)}) copy-start(u32[32]{0:T(128)} %constant.129) | copy-start | bytes 388
  1351.6 625.1 %copy-start.24 = (f32[1536]{0:T(1024)S(1)}, f32[1536]{0:T(1024)}, u32[]{:S(2)}) copy-start(f32[1536]{0:T(1024)} %copy-done.23) | copy-start | bytes 18436
  1351.6 625.1 %copy-start.26 = (f32[1536]{0:T(1024)S(1)}, f32[1536]{0:T(1024)}, u32[]{:S(2)}) copy-start(f32[1536]{0:T(1024)} %copy-done.25) | copy-start | bytes 18436
  1351.7 788.0 %all-reduce.19.cloned.1.call-start = ((), (), s32[]{:S(2)}) async-start(), calls=%async_computation.29 | async-start | bytes 12976128 | tf_op jit(solution)/shard_map/psum | solution.py:267
  (39 other events, 691.8 us)
Sparse Core Ops, SparseCore 0:
  9.6 42.5 all-gather.9
  56.8 22.5 all-gather.13
  81.5 22.7 all-gather.11
  105.8 30.1 all-gather.15
  236.4 169.8 all-reduce.10
  407.7 63.6 all-gather.19
  472.9 62.1 all-gather.17
  536.7 61.9 all-gather.21
  632.1 168.3 all-reduce.14
  802.8 94.1 all-reduce.12
  1231.3 34.8 reduce-scatter.11
  1268.4 34.6 reduce-scatter.9
  1305.4 48.0 reduce-scatter.13
  1355.7 47.5 reduce-scatter.19
  1406.0 28.6 reduce-scatter.17
  1437.4 27.8 reduce-scatter.15
  1467.5 109.4 reduce-scatter.25
  1579.2 111.2 reduce-scatter.23
  1692.8 111.2 reduce-scatter.21
  1806.4 170.3 all-reduce.16
  1979.9 159.7 all-reduce.18
where the time goes:
time: 2170 us; the launch traced here: 2160 us
  waiting for transfers between devices  1370 us (63%)
  matrix products  399 us (18%)
  other arithmetic  189 us (9%)
  blocking collectives  90.6 us (4%)
  local copies, waits for them, and re-layouts  86.8 us (4%)
    psum x1, waiting for transfers between devices, per_device(): normed_one_grad = lax.psum(normed_one_part, 'tp')  171 us
    psum x1, waiting for transfers between devices, per_device(): normed_two_grad = lax.psum(normed_two_part, 'tp')  159 us
    psum x1, waiting for transfers between devices, per_device(): middle = layer_input + lax.psum(attn_partial, 'tp')  156 us
    psum x1, waiting for transfers between devices, per_device(): lax.psum((owned[0], owned[1], owned[2], owned[3], owned[4], owned[5], own...  116 us
    reduce_scatter x1, waiting for transfers between devices, per_device(): lax.psum_scatter(gate_wgrad, 'fsdp', scatter_dimension=0, tiled=True)  114 us
    reduce_scatter x1, waiting for transfers between devices, per_device(): lax.psum_scatter(up_wgrad, 'fsdp', scatter_dimension=0, tiled=True)  113 us
    reduce_scatter x1, waiting for transfers between devices, per_device(): lax.psum_scatter(down_grad, 'fsdp', scatter_dimension=1, tiled=True)  112 us
    psum x1, waiting for transfers between devices, per_device(): lax.psum(mlp_partial.astype(jnp.bfloat16), 'tp').astype(jnp.float32)  88.3 us
  transfers between devices with their start and end apart: 21, of which 18 were waited for; matrix products, arithmetic and copies ran while one was open for 14% of the time, Pallas kernels for 0%

commit v1 on v0

v1 whole, which is shorter than its diff:
```python
import functools
import math

import jax
import jax.numpy as jnp
from jax import lax
from jax.experimental import pallas as pl
from jax.experimental.pallas import tpu as pltpu
from jax.sharding import PartitionSpec as P

HEAD_SIZE = 96
EPSILON = 1e-05
THETA = 100000.0
NEGATIVE = -1e30
LOG2E = 1.4426950408889634
LANES = 128
F32 = jnp.float32
BF16 = jnp.bfloat16
NN = (((1,), (0,)), ((), ()))
NT = (((1,), (1,)), ((), ()))
TN = (((0,), (0,)), ((), ()))


def dot(left, right, dims=NN):
    return lax.dot_general(left, right, dims, preferred_element_type=F32)


def select_rotary(heads, head_dim):
    shape = (heads * LANES, heads * head_dim)
    row = lax.broadcasted_iota(jnp.int32, shape, 0)
    col = lax.broadcasted_iota(jnp.int32, shape, 1)
    half = head_dim // 2
    within = col % head_dim
    want = (col // head_dim) * LANES + jnp.where(within < half, within, within - half + LANES // 2)
    return (row == want).astype(BF16)


def select_value(heads, head_dim):
    shape = (heads * LANES, heads * head_dim)
    row = lax.broadcasted_iota(jnp.int32, shape, 0)
    col = lax.broadcasted_iota(jnp.int32, shape, 1)
    return (row == (col // head_dim) * LANES + col % head_dim).astype(BF16)


def rotary_lanes(positions, head_dim):
    half = head_dim // 2
    freqs = THETA ** (-(jnp.arange(half, dtype=F32) * 2.0 / head_dim))
    angles = positions.astype(F32)[:, None] * freqs[None, :]
    cos, sin = jnp.cos(angles), jnp.sin(angles)
    pad = jnp.zeros((positions.shape[0], LANES // 2 - half), F32)
    return (
        jnp.concatenate([cos, pad, cos, pad], axis=1),
        jnp.concatenate([-sin, pad, sin, pad], axis=1),
    )


def doc_positions(lengths, first, count):
    ends = jnp.cumsum(lengths)
    starts = ends - lengths
    index = first + jnp.arange(count, dtype=jnp.int32)
    document = jnp.sum((index[None, :] >= ends[:, None]).astype(jnp.int32), axis=0)
    chosen = document[None, :] == jnp.arange(lengths.shape[0], dtype=jnp.int32)[:, None]
    start_of = jnp.sum(jnp.where(chosen, starts[:, None], 0), axis=0)
    return index - start_of


def doc_start(ends_ref, base, rows):
    start = base if jnp.ndim(rows) == 0 else jnp.zeros_like(rows) + base
    for j in range(ends_ref.shape[0]):
        end = ends_ref[j]
        start = jnp.where(rows >= end, jnp.maximum(start, end), start)
    return start


def put_lanes(rows, column, lane):
    at = lax.broadcasted_iota(jnp.int32, rows.shape, 1)
    high = column.astype(BF16).astype(F32)
    rest = column - high
    mid = rest.astype(BF16).astype(F32)
    low = rest - mid
    wide = rows.astype(F32)
    wide = jnp.where(at == lane, high, wide)
    wide = jnp.where(at == lane + 1, mid, wide)
    return jnp.where(at == lane + 2, low, wide).astype(BF16)


def block_ranges(first_row, rows, block, low, last_low, key_base, key_count):
    begin = (jnp.maximum(low, key_base) - key_base) // block
    stop = jnp.minimum((first_row + rows - key_base + block - 1) // block, key_count // block)
    inner = jnp.minimum(jnp.maximum((last_low - key_base + block - 1) // block, begin), stop)
    diagonal = jnp.minimum(jnp.maximum((first_row - key_base) // block, inner), stop)
    return begin, inner, diagonal, stop


def stack_heads(ref, kv, group):
    parts = [ref[:, (kv * group + g) * LANES : (kv * group + g + 1) * LANES] for g in range(group)]
    return jnp.concatenate(parts, axis=0)


def row_marks(ends_ref, base, first_row, bq, group):
    rows = lax.broadcasted_iota(jnp.int32, (1, bq), 1) + first_row
    starts = doc_start(ends_ref, base, rows)
    return jnp.concatenate([rows] * group, axis=1), jnp.concatenate([starts] * group, axis=1)


def attention_forward_kernel(
    first, key_base, tokens, bq, bk, head_dim, group, ends_ref, base_ref, q_ref, kv_ref, *rest
):
    if first:
        max_ref, acc_ref = rest
    else:
        sel_ref, max_in, acc_in, o_ref, qa_ref, max_ref, acc_ref = rest
    first_row = tokens + pl.program_id(0) * bq
    base = base_ref[0]
    low = doc_start(ends_ref, base, first_row)
    last_low = doc_start(ends_ref, base, first_row + bq - 1)
    rows, starts = row_marks(ends_ref, base, first_row, bq, group)
    kv_heads = kv_ref.shape[1] // LANES // 2
    unit = LOG2E / math.sqrt(head_dim)
    queries = [stack_heads(q_ref, h, group) for h in range(kv_heads)]
    if first:
        max_ref[...] = jnp.full(max_ref.shape, NEGATIVE, F32)
        acc_ref[...] = jnp.zeros(acc_ref.shape, F32)
    else:
        max_ref[...] = max_in[...]
        acc_ref[...] = acc_in[...]

    def body(masked, index, carry):
        at = pl.multiple_of(index * bk, bk)
        if masked:
            keys = lax.broadcasted_iota(jnp.int32, (bk, group * bq), 0) + (at + key_base)
            keep = (keys <= rows) & (keys >= starts)
        for h in range(kv_heads):
            key = kv_ref[pl.ds(at, bk), h * LANES : (h + 1) * LANES]
            value = kv_ref[pl.ds(at, bk), (kv_heads + h) * LANES : (kv_heads + h + 1) * LANES]
            scores = dot(key, queries[h], NT)
            if masked:
                scores = jnp.where(keep, scores, NEGATIVE)
            old = max_ref[0, h]
            new = jnp.maximum(old, jnp.max(scores, axis=0, keepdims=True))
            probs = jnp.exp2((scores - new) * unit)
            if masked:
                probs = jnp.where(keep, probs, 0.0)
            acc_ref[0, h] = acc_ref[0, h] * jnp.exp2((old - new) * unit) + dot(
                value, probs.astype(BF16), TN
            )
            max_ref[0, h] = new
        return carry

    begin, inner, diagonal, stop = block_ranges(
        first_row, bq, bk, low, last_low, key_base, kv_ref.shape[0]
    )
    lax.fori_loop(begin, inner, functools.partial(body, True), 0)
    lax.fori_loop(inner, diagonal, functools.partial(body, False), 0)
    lax.fori_loop(diagonal, stop, functools.partial(body, True), 0)
    if first:
        return
    outs = []
    for h in range(kv_heads):
        acc = acc_ref[0, h]
        total = acc[head_dim : head_dim + 1, :]
        out = jnp.transpose(acc * (1.0 / total)).astype(BF16)
        logsum = jnp.broadcast_to(max_ref[0, h] + jnp.log2(total) * (1.0 / unit), (8, group * bq))
        marked = put_lanes(queries[h], jnp.transpose(logsum)[:, :1], head_dim // 2)
        for g in range(group):
            head = h * group + g
            qa_ref[:, head * LANES : (head + 1) * LANES] = marked[g * bq : (g + 1) * bq]
            outs.append(out[g * bq : (g + 1) * bq])
    o_ref[...] = dot(jnp.concatenate(outs, axis=1), sel_ref[...]).astype(BF16)


def attention_forward(ends, base, q, kv, head_dim, key_base, state=None, select=None):
    tokens, width = q.shape
    kv_heads = kv.shape[1] // LANES // 2
    group = width // LANES // kv_heads
    bq = bk = math.gcd(tokens, 512)
    steps = tokens // bq
    whole = lambda a: pl.BlockSpec(a.shape, lambda i, *_: (0, 0))
    row = lambda w: pl.BlockSpec((bq, w), lambda i, *_: (i, 0))
    shapes = [(steps, kv_heads, 1, group * bq), (steps, kv_heads, LANES, group * bq)]
    kept = [pl.BlockSpec((1,) + a[1:], lambda i, *_: (i, 0, 0, 0)) for a in shapes]
    pairs = tokens * tokens * group * kv_heads // 2
    if state is None:
        in_specs, operands = [row(width), whole(kv)], (q, kv)
        out_specs, out_shape = kept, [jax.ShapeDtypeStruct(a, F32) for a in shapes]
        scratch = []
    else:
        in_specs, operands = [row(width), whole(kv), whole(select)] + kept, (q, kv, select) + tuple(state)
        out_specs = [row(select.shape[1]), row(width)]
        out_shape = [
            jax.ShapeDtypeStruct((tokens, select.shape[1]), BF16),
            jax.ShapeDtypeStruct(q.shape, BF16),
        ]
        scratch = [pltpu.VMEM((1,) + a[1:], F32) for a in shapes]
    return pl.pallas_call(
        functools.partial(
            attention_forward_kernel, state is None, key_base, tokens, bq, bk, head_dim, group
        ),
        grid_spec=pltpu.PrefetchScalarGridSpec(
            num_scalar_prefetch=2, grid=(steps,), in_specs=in_specs, out_specs=out_specs,
            scratch_shapes=scratch,
        ),
        out_shape=out_shape,
        compiler_params=pltpu.CompilerParams(vmem_limit_bytes=40 << 20),
        cost_estimate=pl.CostEstimate(
            flops=pairs * 1024, bytes_accessed=8 << 20, transcendentals=pairs
        ),
        name="attention_forward",
    )(ends, base, *operands)


def attention_backward_kernel(
    first, key_base, tokens, bq, bk, head_dim, group,
    ends_ref, base_ref, qa_ref, do_ref, o_ref, kv_ref, spread_ref, *rest
):
    if first:
        dq_ref, dkv_ref, dk_acc, dv_acc, dq_acc = rest
    else:
        part_ref, cos_ref, sin_ref, sel_ref, dq_ref, dkv_ref, dk_acc, dv_acc, dq_acc = rest
    step = pl.program_id(0)
    first_row = tokens + step * bq
    base = base_ref[0]
    low = doc_start(ends_ref, base, first_row)
    last_low = doc_start(ends_ref, base, first_row + bq - 1)
    kv_heads = kv_ref.shape[1] // LANES // 2
    scale = 1.0 / math.sqrt(head_dim)
    unit = LOG2E * scale
    begin, inner, diagonal, stop = block_ranges(
        first_row, bq, bk, low, last_low, key_base, kv_ref.shape[0]
    )

    @pl.when(step == 0)
    def _():
        dk_acc[...] = jnp.zeros(dk_acc.shape, F32)
        dv_acc[...] = jnp.zeros(dv_acc.shape, F32)

    if first:
        dq_acc[...] = jnp.zeros(dq_acc.shape, F32)
    else:
        for h in range(kv_heads):
            dq_acc[h] = stack_heads(part_ref, h, group)

    @pl.when(begin < stop)
    def _():
        rows, starts = row_marks(ends_ref, base, first_row, bq, group)
        grads_wide = dot(do_ref[...], spread_ref[...])
        outs_wide = dot(o_ref[...], spread_ref[...])
        queries, grads = [], []
        for h in range(kv_heads):
            queries.append(stack_heads(qa_ref, h, group))
            grad = stack_heads(grads_wide, h, group)
            inner_sum = jnp.sum(grad * stack_heads(outs_wide, h, group), axis=1, keepdims=True)
            grads.append(put_lanes(grad, -inner_sum, head_dim))

        def body(masked, index, carry):
            at = pl.multiple_of(index * bk, bk)
            if masked:
                keys = lax.broadcasted_iota(jnp.int32, (bk, group * bq), 0) + (at + key_base)
                keep = (keys <= rows) & (keys >= starts)
            for h in range(kv_heads):
                key = kv_ref[pl.ds(at, bk), h * LANES : (h + 1) * LANES]
                value = kv_ref[pl.ds(at, bk), (kv_heads + h) * LANES : (kv_heads + h + 1) * LANES]
                probs = jnp.exp2(dot(key, queries[h], NT) * unit)
                if masked:
                    probs = jnp.where(keep, probs, 0.0)
                slope = (probs * dot(value, grads[h], NT)).astype(BF16)
                dv_acc[h, pl.ds(at, bk), :] += dot(probs.astype(BF16), grads[h])
                dk_acc[h, pl.ds(at, bk), :] += dot(slope, queries[h])
                dq_acc[h] += dot(slope, key, TN)
            return carry

        lax.fori_loop(begin, inner, functools.partial(body, True), 0)
        lax.fori_loop(inner, diagonal, functools.partial(body, False), 0)
        lax.fori_loop(diagonal, stop, functools.partial(body, True), 0)

    outs = []
    for h in range(kv_heads):
        for g in range(group):
            grad = dq_acc[h, g * bq : (g + 1) * bq, :]
            if first:
                dq_ref[:, (h * group + g) * LANES : (h * group + g + 1) * LANES] = grad
            else:
                grad = grad * scale
                outs.append(
                    (grad * cos_ref[...] - pltpu.roll(grad, LANES // 2, 1) * sin_ref[...]).astype(BF16)
                )
    if not first:
        dq_ref[...] = dot(jnp.concatenate(outs, axis=1), sel_ref[...]).astype(BF16)

    @pl.when(step == pl.num_programs(0) - 1)
    def _():
        for h in range(kv_heads):
            dkv_ref[:, h * LANES : (h + 1) * LANES] = (dk_acc[h] * scale).astype(dkv_ref.dtype)
            dkv_ref[:, (kv_heads + h) * LANES : (kv_heads + h + 1) * LANES] = dv_acc[h].astype(dkv_ref.dtype)


def attention_backward(ends, base, qa, grad, out, kv, spread, head_dim, key_base, rest=None):
    tokens, width = qa.shape
    keys = kv.shape[0]
    kv_heads = kv.shape[1] // LANES // 2
    group = width // LANES // kv_heads
    bq = bk = math.gcd(tokens, 512)
    whole = lambda a: pl.BlockSpec(a.shape, lambda i, *_: (0, 0))
    row = lambda w: pl.BlockSpec((bq, w), lambda i, *_: (i, 0))
    pairs = tokens * tokens * group * kv_heads // 2
    in_specs = [row(width), row(grad.shape[1]), row(out.shape[1]), whole(kv), whole(spread)]
    operands = (qa, grad, out, kv, spread)
    if rest is None:
        dq_width, dq_type, dkv_type = width, F32, BF16
    else:
        part, cos, sin, select = rest
        in_specs += [row(width), row(LANES), row(LANES), whole(select)]
        operands += (part, cos, sin, select)
        dq_width, dq_type, dkv_type = select.shape[1], BF16, F32
    return pl.pallas_call(
        functools.partial(
            attention_backward_kernel, rest is None, key_base, tokens, bq, bk, head_dim, group
        ),
        grid_spec=pltpu.PrefetchScalarGridSpec(
            num_scalar_prefetch=2,
            grid=(tokens // bq,),
            in_specs=in_specs,
            out_specs=[row(dq_width), whole(kv)],
            scratch_shapes=[
                pltpu.VMEM((kv_heads, keys, LANES), F32),
                pltpu.VMEM((kv_heads, keys, LANES), F32),
                pltpu.VMEM((kv_heads, group * bq, LANES), F32),
            ],
        ),
        out_shape=[
            jax.ShapeDtypeStruct((tokens, dq_width), dq_type),
            jax.ShapeDtypeStruct(kv.shape, dkv_type),
        ],
        compiler_params=pltpu.CompilerParams(vmem_limit_bytes=48 << 20),
        cost_estimate=pl.CostEstimate(
            flops=pairs * 2560, bytes_accessed=12 << 20, transcendentals=pairs
        ),
        name="attention_backward",
    )(ends, base, qa, grad, out, kv, spread, *operands[5:])


MESH = pl.DeviceIdType.MESH


class Ranks:
    def __init__(self, count):
        self.count, self.chips = count, count // 2
        self.me = lax.axis_index("tp")
        self.chip, self.core = self.me // 2, self.me % 2

    def peer(self, k, j):
        return lax.rem(self.chip + k + self.chips, self.chips) * 2 + lax.rem(self.core + j, 2)

    def others(self):
        return [(k, j) for k in range(self.chips) for j in range(2) if k or j]

    def barrier(self):
        sem = pltpu.get_barrier_semaphore()
        for k, j in self.others():
            pl.semaphore_signal(sem, inc=1, device_id={"tp": self.peer(k, j)}, device_id_type=MESH)
        pl.semaphore_wait(sem, self.count - 1)


def remote(src, dst, send, recv, rank):
    return pltpu.make_async_remote_copy(
        src_ref=src, dst_ref=dst, send_sem=send, recv_sem=recv, device_id={"tp": rank},
        device_id_type=MESH,
    )


def row_mean(x):
    return jnp.sum(x, axis=-1, keepdims=True) * (1.0 / x.shape[-1])


class GatherRows:
    def __init__(self, ranks, rows_ref, out_ref, send, recv, local):
        own = rows_ref.shape[0]
        self.ranks, self.send, self.recv = ranks, send, recv
        self.at = lambda rank: out_ref.at[pl.ds(pl.multiple_of(rank * own, own), own)]
        self.keep = pltpu.make_async_copy(rows_ref, self.at(ranks.me), local)
        self.copies = []
        for k in list(range(1, ranks.chips)) + [0]:
            peer = ranks.peer(k, 0) if k else ranks.peer(0, 1)
            self.copies.append(remote(rows_ref, self.at(ranks.me), send.at[0, k], recv.at[0, k], peer))

    def start(self):
        for copy in self.copies:
            copy.start()
        self.keep.start()

    def finish(self):
        ranks, passed = self.ranks, []
        for k, copy in zip(range(1, ranks.chips), self.copies):
            copy.wait_recv()
            held = self.at(ranks.peer(-k, 0))
            passed.append(
                remote(held, held, self.send.at[1, k], self.recv.at[1, k], ranks.peer(0, 1))
            )
            passed[-1].start()
        self.copies[-1].wait_recv()
        for copy in self.copies:
            copy.wait_send()
        for copy in passed:
            copy.wait()
        self.keep.wait()


def both_cores(ranks, blocks, out_ref, send, recv, local):
    own = blocks[0].shape[0]
    copies = []
    for k, block in enumerate(blocks):
        there = out_ref.at[pl.ds(pl.multiple_of(ranks.peer(-k, 0) * own, own), own)]
        copies.append(remote(block, there, send.at[k], recv.at[k], ranks.peer(0, 1)))
        copies.append(pltpu.make_async_copy(block, there, local.at[k]))
    return copies


def mix_kernel(count, att_ref, x_ref, gain_ref, *rest):
    chips = count // 2
    blocks, rest = rest[:chips], rest[chips:]
    (
        n2_ref, mid_ref, other_ref, heads, rows_in, rows_out, others, a_send, a_recv, b_send, b_recv,
        g_send, g_recv, local,
    ) = rest
    ranks = Ranks(count)
    own = rows_in.shape[0]
    mine_at = pl.ds(pl.multiple_of(ranks.me * own, own), own)
    fetch = pltpu.make_async_copy(x_ref.at[mine_at], rows_in, local.at[0])
    fetch.start()
    mine = pltpu.make_async_copy(att_ref.at[mine_at], heads.at[0], local.at[1])
    mine.start()
    ranks.barrier()
    copies = {}
    for k, j in ranks.others()[::-1]:
        peer, slot = ranks.peer(k, j), 2 * k + j
        copies[slot] = remote(
            att_ref.at[pl.ds(pl.multiple_of(peer * own, own), own)], heads.at[slot],
            a_send.at[slot], a_recv.at[slot], peer,
        )
        copies[slot].start()
    swaps = [
        remote(blocks[k], others.at[k], b_send.at[k], b_recv.at[k], ranks.peer(0, 1))
        for k in range(chips)
    ]
    for copy in swaps:
        copy.start()
    fetch.wait()
    mine.wait()
    mid_ref[...] = rows_in[...] + dot(heads[0], blocks[0][...], NT)
    keeps = []
    for slot in range(1, count):
        k = slot // 2
        if slot % 2:
            swaps[k].wait_recv()
            keeps.append(pltpu.make_async_copy(others.at[k], other_ref.at[k], local.at[2 + k]))
            keeps[-1].start()
        copies[slot].wait_recv()
        mid_ref[...] += dot(heads[slot], others[k] if slot % 2 else blocks[k][...], NT)
    mid = mid_ref[...]
    factor = lax.rsqrt(row_mean(mid * mid) + EPSILON)
    rows_out[...] = (mid * factor * gain_ref[...]).astype(BF16)
    gather = GatherRows(ranks, rows_out, n2_ref, g_send, g_recv, local.at[0])
    gather.start()
    for slot in range(1, count):
        copies[slot].wait_send()
    for copy in swaps:
        copy.wait_send()
    for copy in keeps:
        copy.wait()
    gather.finish()


def mix(count, attended, layer_input, gain, blocks):
    tokens, model = layer_input.shape
    own = tokens // count
    chips = count // 2
    width = attended.shape[1]
    vmem, hbm = pl.BlockSpec(memory_space=pltpu.VMEM), pl.BlockSpec(memory_space=pl.ANY)
    sem = pltpu.SemaphoreType.DMA
    return pl.pallas_call(
        functools.partial(mix_kernel, count),
        in_specs=[hbm, hbm, vmem] + [vmem] * chips,
        out_specs=[hbm, vmem, hbm],
        out_shape=[
            jax.ShapeDtypeStruct((tokens, model), BF16),
            jax.ShapeDtypeStruct((own, model), F32),
            jax.ShapeDtypeStruct((chips, model, width), BF16),
        ],
        scratch_shapes=[
            pltpu.VMEM((count, own, width), BF16),
            pltpu.VMEM((own, model), F32),
            pltpu.VMEM((own, model), BF16),
            pltpu.VMEM((chips, model, width), BF16),
            sem((count,)), sem((count,)), sem((chips,)), sem((chips,)), sem((2, chips)),
            sem((2, chips)), sem((2 + chips,)),
        ],
        compiler_params=pltpu.CompilerParams(
            vmem_limit_bytes=40 << 20, collective_id=1, has_side_effects=True
        ),
        cost_estimate=pl.CostEstimate(
            flops=2 * tokens * model * model, bytes_accessed=150 << 20, transcendentals=0
        ),
        name="mix_heads",
    )(attended, layer_input, gain, *blocks)


def scatter_order(ranks, halves, own, i):
    k = lax.rem(i // halves + 1, ranks.chips)
    half = lax.rem(i, halves)
    rows = own // halves
    at = lambda j: pl.multiple_of(ranks.peer(k, j) * own + half * rows, rows)
    return k, half, at(0), at(1)


def half_rows(shard, which, half):
    return pl.ds(pl.multiple_of((shard * 2 + which) * half, half), half)


def swap_halves(src, dst, send, recv, shards):
    piece = lax.axis_index("ctx")
    half = src.shape[0] // (2 * shards)
    return [
        pltpu.make_async_remote_copy(
            src_ref=src.at[half_rows(s, 1 - piece, half)], dst_ref=dst.at[pl.ds(s * half, half)],
            send_sem=send.at[s], recv_sem=recv.at[s], device_id={"ctx": 1 - piece},
            device_id_type=MESH,
        )
        for s in range(shards)
    ]


def signal_piece(count):
    ranks = Ranks(count)
    sem = pltpu.get_barrier_semaphore()
    for k, j in ranks.others():
        pl.semaphore_signal(sem, inc=1, device_id={"tp": ranks.peer(k, j)}, device_id_type=MESH)
    pl.semaphore_signal(sem, inc=1, device_id={"ctx": 1 - lax.axis_index("ctx")}, device_id_type=MESH)
    pl.semaphore_wait(sem, count)


def feedforward_kernel(count, n2_ref, cot_ref, mid_ref, gain_ref, other_ref, weight_ref, *rest):
    blocks, rest = rest[: count // 2], rest[count // 2 :]
    (
        ffb_ref, mg_ref, bg_ref, gain_grad_ref, da_ref, grad_ref, grads_ref,
        gate_w, up_w, down_w, n2, fg, hid, gu, rows_in, ffb_out,
        c_send, c_recv, y_send, y_recv, f_send, f_recv, heads,
        w_sem, in_sem, out_sem, cs, cr, ys, yr, fs, fr, hs, hr, local,
    ) = rest
    ranks = Ranks(count)
    own = mg_ref.shape[0]
    halves = 2
    rows = own // halves
    steps = ranks.chips * halves
    width = gate_w.shape[1]
    model = n2.shape[1]
    loads = [pltpu.make_async_copy(n2_ref, n2, w_sem.at[3])] + [
        pltpu.make_async_copy(weight_ref.at[:, pl.ds(w * width, width)], full, w_sem.at[w])
        for w, full in enumerate((gate_w, up_w, down_w))
    ]
    for load in loads:
        load.start()

    def read(at, slot):
        return pltpu.make_async_copy(cot_ref.at[pl.ds(at, rows)], rows_in.at[slot], in_sem.at[slot])

    def tile(at, slot, begin):
        here = pl.ds(at, rows)

        def ready(n):
            if begin is not None:
                @pl.when(begin)
                def _():
                    loads[n].wait()

        ready(0)
        ready(1)
        n = n2[here, :]
        grad = rows_in[slot].astype(BF16)
        fg[here, :] = grad
        gate = dot(n, gate_w[...])
        ready(2)
        up = dot(n, up_w[...])
        ready(3)
        back = dot(grad, down_w[...])
        sig = 1.0 / (1.0 + jnp.exp(-gate))
        act = gate * sig
        hidden = (act * up).astype(BF16)
        hid[here, :] = hidden
        gg = (back * up * (sig * (1.0 + gate * (1.0 - sig)))).astype(BF16)
        gu[here, :width] = gg
        ug = (back * act).astype(BF16)
        gu[here, width:] = ug
        return dot(gg, gate_w[...], NT) + dot(ug, up_w[...], NT), dot(hidden, down_w[...], NT)

    read(scatter_order(ranks, halves, own, 0)[3], 0).start()
    ranks.barrier()
    neighbour = ranks.peer(0, 1)

    def to_core(i):
        slot = lax.rem(i, 2)
        return [
            remote(c_send.at[slot], c_recv.at[slot], cs.at[slot], cr.at[slot], neighbour),
            remote(f_send.at[slot], f_recv.at[slot], fs.at[slot], fr.at[slot], neighbour),
        ]

    def to_chip(i, k):
        return remote(y_send.at[i], y_recv.at[i], ys.at[i], yr.at[i], ranks.peer(k, 0))

    def ffb_write(i):
        return pltpu.make_async_copy(ffb_out, ffb_ref.at[i], out_sem.at[0])

    def step(i, carry):
        k, u, at_mine, at_other = scatter_order(ranks, halves, own, i)
        slot = lax.rem(i, 2)
        read(at_mine, 1).start()
        read(at_other, 0).wait()
        grad, forward = tile(at_other, 0, i == 0)

        @pl.when(i + 1 < steps)
        def _():
            read(scatter_order(ranks, halves, own, i + 1)[3], 0).start()

        @pl.when(i > 1)
        def _():
            for copy in to_core(i):
                copy.wait_send()

        c_send[slot] = grad.astype(BF16)
        f_send[slot] = forward.astype(BF16)
        for copy in to_core(i):
            copy.start()
        read(at_mine, 1).wait()
        grad, forward = tile(at_mine, 1, None)

        @pl.when(i > 0)
        def _():
            ffb_write(i).wait()

        for copy in to_core(i):
            copy.wait_recv()
        grad = grad + c_recv[slot].astype(F32)
        ffb_out[...] = (forward + f_recv[slot].astype(F32)).astype(BF16)
        ffb_write(i).start()

        @pl.when(k != 0)
        def _():
            y_send[i] = grad.astype(BF16)
            to_chip(i, k).start()

        @pl.when(k == 0)
        def _():
            mg_ref[pl.ds(pl.multiple_of(u * rows, rows), rows), :] = grad

        return carry

    lax.fori_loop(0, steps, step, 0)
    mine_at = pl.multiple_of(ranks.me * own, own)
    fetch = lambda u: [
        pltpu.make_async_copy(mid_ref.at[pl.ds(u * rows, rows)], rows_in.at[0], in_sem.at[0]),
        read(mine_at + u * rows, 1),
    ]
    for copy in fetch(0):
        copy.start()
    cols = math.gcd(model, 384)
    writes = []

    def product(left, right, full, dst, n):
        for d in range(model // cols):
            full[d * cols : (d + 1) * cols, :] = dot(
                left[:, d * cols : (d + 1) * cols], right, TN
            ).astype(BF16)
        writes.append(pltpu.make_async_copy(full, dst, out_sem.at[1 + n]))
        writes[-1].start()

    product(n2, gu[:, :width], gate_w, grad_ref, 0)
    gain = gain_ref[...]
    gain_total = None
    for u in range(halves):
        here = slice(u * rows, (u + 1) * rows)
        total = mg_ref[here, :]
        for k in range(1, ranks.chips):
            i = (k - 1) * halves + u
            to_chip(i, k).wait_recv()
            total = total + y_recv[i].astype(F32)
        for copy in fetch(u):
            copy.wait()
        mid = rows_in[0]
        factor = lax.rsqrt(row_mean(mid * mid) + EPSILON)
        hat = mid * factor
        term = jnp.sum(total * hat, axis=0, keepdims=True)
        gain_total = term if gain_total is None else gain_total + term
        inner = total * gain
        grad = rows_in[1] + factor * (inner - hat * row_mean(inner * hat))
        mg_ref[here, :] = grad
        bg_ref[here, :] = grad.astype(BF16)
        if u + 1 < halves:
            for copy in fetch(u + 1):
                copy.start()
    gain_grad_ref[...] = gain_total
    back = []
    for k, j in ranks.others()[::-1]:
        slot, peer = 2 * k + j, ranks.peer(-k, j)
        heads[slot] = dot(bg_ref[...], other_ref[k] if j else blocks[k][...]).astype(BF16)
        back.append(
            remote(heads.at[slot], da_ref.at[pl.ds(mine_at, own)], hs.at[slot], hr.at[slot], peer)
        )
        back[-1].start()
    heads[0] = dot(bg_ref[...], blocks[0][...]).astype(BF16)
    keep = pltpu.make_async_copy(heads.at[0], da_ref.at[pl.ds(mine_at, own)], local.at[0])
    keep.start()
    product(n2, gu[:, width:], up_w, grads_ref.at[:, pl.ds(0, width)], 1)
    product(fg, hid[...], down_w, grads_ref.at[:, pl.ds(width, width)], 2)
    for i in (steps - 2, steps - 1):
        for copy in to_core(i):
            copy.wait_send()
    for i in range(steps - halves):
        to_chip(i, i // halves + 1).wait_send()
    ffb_write(steps - 1).wait()
    for copy in back:
        copy.wait()
    keep.wait()
    for copy in writes:
        copy.wait()


def feedforward(count, n2, cotangent, middle, gain, weights, blocks, others):
    tokens, model = n2.shape
    own = tokens // count
    hidden = weights.shape[1] // 3
    width = blocks[0].shape[1]
    rows, steps = own // 2, count
    vmem, hbm = pl.BlockSpec(memory_space=pltpu.VMEM), pl.BlockSpec(memory_space=pl.ANY)
    sem = pltpu.SemaphoreType.DMA
    return pl.pallas_call(
        functools.partial(feedforward_kernel, count),
        in_specs=[hbm, hbm, hbm, vmem, vmem, hbm] + [vmem] * (count // 2),
        out_specs=[hbm, vmem, vmem, vmem, hbm, hbm, hbm],
        out_shape=[
            jax.ShapeDtypeStruct((steps, rows, model), BF16),
            jax.ShapeDtypeStruct((own, model), F32),
            jax.ShapeDtypeStruct((own, model), BF16),
            jax.ShapeDtypeStruct((1, model), F32),
            jax.ShapeDtypeStruct((tokens, width), BF16),
            jax.ShapeDtypeStruct((model, hidden), BF16),
            jax.ShapeDtypeStruct((model, 2 * hidden), BF16),
        ],
        scratch_shapes=[pltpu.VMEM((model, hidden), BF16)] * 3
        + [
            pltpu.VMEM((tokens, model), BF16),
            pltpu.VMEM((tokens, model), BF16),
            pltpu.VMEM((tokens, hidden), BF16),
            pltpu.VMEM((tokens, 2 * hidden), BF16),
            pltpu.VMEM((2, rows, model), F32),
            pltpu.VMEM((rows, model), BF16),
        ]
        + [pltpu.VMEM((2, rows, model), BF16)] * 2
        + [pltpu.VMEM((steps - 2, rows, model), BF16)] * 2
        + [pltpu.VMEM((2, rows, model), BF16)] * 2
        + [
            pltpu.VMEM((count, own, width), BF16),
            sem((4,)), sem((2,)), sem((4,)),
            sem((2,)), sem((2,)), sem((steps - 2,)), sem((steps - 2,)),
            sem((2,)), sem((2,)), sem((count,)), sem((count,)), sem((1,)),
        ],
        compiler_params=pltpu.CompilerParams(
            vmem_limit_bytes=63 << 20, collective_id=2, has_side_effects=True
        ),
        cost_estimate=pl.CostEstimate(
            flops=2 * tokens * model * hidden * 9, bytes_accessed=280 << 20,
            transcendentals=tokens * hidden,
        ),
        name="feed_forward",
    )(n2, cotangent, middle, gain, others, weights, *blocks)


def shard_copy(src, dst, send, recv, axis, index):
    return pltpu.make_async_remote_copy(
        src_ref=src, dst_ref=dst, send_sem=send, recv_sem=recv, device_id={axis: index},
        device_id_type=MESH,
    )


def begin_kernel(
    shards, x_ref, qkv_ref, wo_ref, gains_ref, n_ref, qkv_full_ref, wo_full_ref, gain_out_ref,
    qkv_full, wo_full, normed, rows_in, gain_buf, zs, zr, xs, xr, gs, gr, own_sem, in_sem, out_sem,
):
    me, piece = lax.axis_index("fsdp"), lax.axis_index("ctx")
    fulls, sources = (qkv_full, wo_full), (qkv_ref, wo_ref)
    shard = qkv_ref.shape[0]
    half = shard // 2
    tokens = normed.shape[0]
    rows = rows_in.shape[1]
    steps = tokens // rows

    def read(i):
        return pltpu.make_async_copy(
            x_ref.at[pl.ds(i * rows, rows)], rows_in.at[i % 2], in_sem.at[i % 2]
        )

    read(0).start()
    keeps = [
        pltpu.make_async_copy(src, full.at[pl.ds(pl.multiple_of(me * shard, shard), shard)], own_sem.at[a])
        for a, (src, full) in enumerate(zip(sources, fulls))
    ]
    for copy in keeps:
        copy.start()
    keep_gain = pltpu.make_async_copy(gains_ref, gain_buf.at[me], own_sem.at[2])
    keep_gain.start()
    barrier = pltpu.get_barrier_semaphore()
    for k in range(1, shards):
        pl.semaphore_signal(
            barrier, inc=1, device_id={"fsdp": lax.rem(me + k, shards)}, device_id_type=MESH
        )
    pl.semaphore_signal(barrier, inc=1, device_id={"ctx": 1 - piece}, device_id_type=MESH)
    pl.semaphore_wait(barrier, shards)

    def place(a, s, which):
        return fulls[a].at[half_rows(s, which, half)]

    def own_half(a):
        return sources[a].at[pl.ds(pl.multiple_of(piece * half, half), half)]

    def along(a, s, step, mine):
        way = 0 if step > 0 else 1
        src = own_half(a) if mine else place(a, s, piece)
        return shard_copy(
            src, place(a, s, piece), zs.at[a, way, s], zr.at[a, s], "fsdp",
            lax.rem(me + step + shards, shards),
        )

    def across(a, s):
        return shard_copy(
            place(a, s, piece), place(a, s, piece), xs.at[a, s], xr.at[a, s], "ctx", 1 - piece
        )

    gain_copies = [
        shard_copy(
            gains_ref, gain_buf.at[me], gs.at[k], gr.at[k], "fsdp", lax.rem(me + k, shards)
        )
        for k in range(1, shards)
    ]
    for copy in gain_copies:
        copy.start()
    for a in range(2):
        for step, there in ((1, me < shards - 1), (-1, me > 0)):
            @pl.when(there)
            def _():
                along(a, me, step, True).start()

    for copy in gain_copies:
        copy.wait()
    keep_gain.wait()
    gain_out_ref[...] = jnp.concatenate([gain_buf[s] for s in range(shards)], axis=1)
    for i in range(steps):
        if i + 1 < steps:
            read(i + 1).start()
        read(i).wait()
        x = rows_in[i % 2]
        factor = lax.rsqrt(row_mean(x * x) + EPSILON)
        normed[i * rows : (i + 1) * rows, :] = (x * factor * gain_out_ref[0:1, :]).astype(BF16)
    write_normed = pltpu.make_async_copy(normed, n_ref, out_sem.at[0])
    write_normed.start()

    def arrival(d, step):
        s = me - step * d
        there = (s >= 0) & (s <= shards - 1)
        s = jnp.minimum(jnp.maximum(s, 0), shards - 1)
        onward = (me < shards - 1) if step > 0 else (me > 0)

        @pl.when(there)
        def _():
            for a in range(2):
                along(a, s, step, False).wait_recv()
                across(a, s).start()

        @pl.when(there & onward)
        def _():
            for a in range(2):
                along(a, s, step, False).start()

    for d in range(1, shards):
        arrival(d, 1)
        arrival(d, -1)
    for copy in keeps:
        copy.wait()
    for k in range(1, shards):
        s = lax.rem(me + k, shards)
        for a in range(2):
            across(a, s).wait_recv()
    writes = [
        pltpu.make_async_copy(qkv_full, qkv_full_ref, out_sem.at[1]),
        pltpu.make_async_copy(wo_full, wo_full_ref, out_sem.at[2]),
    ]
    for copy in writes:
        copy.start()
    for a in range(2):
        for s in range(shards):
            @pl.when((me >= s) & (me < shards - 1))
            def _():
                along(a, s, 1, False).wait_send()

            @pl.when((me <= s) & (me > 0))
            def _():
                along(a, s, -1, False).wait_send()

        for k in range(1, shards):
            across(a, lax.rem(me + k, shards)).wait_send()
    write_normed.wait()
    for copy in writes:
        copy.wait()


def begin(shards, x, qkv, wo, gains):
    tokens, model = x.shape
    rows = math.gcd(tokens, 256)
    vmem, hbm = pl.BlockSpec(memory_space=pltpu.VMEM), pl.BlockSpec(memory_space=pl.ANY)
    sem = pltpu.SemaphoreType.DMA
    return pl.pallas_call(
        functools.partial(begin_kernel, shards),
        in_specs=[hbm, vmem, vmem, vmem],
        out_specs=[hbm, hbm, hbm, vmem],
        out_shape=[
            jax.ShapeDtypeStruct((tokens, model), BF16),
            jax.ShapeDtypeStruct((model, qkv.shape[1]), BF16),
            jax.ShapeDtypeStruct((model, wo.shape[1]), BF16),
            jax.ShapeDtypeStruct((gains.shape[0], model), F32),
        ],
        scratch_shapes=[
            pltpu.VMEM((model, qkv.shape[1]), BF16),
            pltpu.VMEM((model, wo.shape[1]), BF16),
            pltpu.VMEM((tokens, model), BF16),
            pltpu.VMEM((2, rows, model), F32),
            pltpu.VMEM((shards,) + gains.shape, F32),
            sem((2, 2, shards)), sem((2, shards)), sem((2, shards)), sem((2, shards)),
            sem((shards,)), sem((shards,)), sem((3,)), sem((2,)), sem((3,)),
        ],
        compiler_params=pltpu.CompilerParams(
            vmem_limit_bytes=48 << 20, collective_id=4, has_side_effects=True
        ),
        cost_estimate=pl.CostEstimate(flops=0, bytes_accessed=120 << 20, transcendentals=0),
        name="norm_and_gather",
    )(x, qkv, wo, gains)


def project_kernel(
    q_heads, n_ref, qkv_ref, spread_ref, cos_ref, sin_ref, krow_ref, vrow_ref, q_ref, kv_ref, wide
):
    @pl.when(pl.program_id(0) == 0)
    def _():
        model = qkv_ref.shape[0]
        block = math.gcd(model, 512)
        for r in range(0, model, block):
            wide[r : r + block, :] = dot(qkv_ref[r : r + block, :], spread_ref[...]).astype(BF16)

    kv_heads = kv_ref.shape[1] // LANES // 2
    cos, sin = cos_ref[...], sin_ref[...]
    out = dot(n_ref[...], wide[...])
    for h in range(q_heads + 2 * kv_heads):
        part = out[:, h * LANES : (h + 1) * LANES]
        if h < q_heads + kv_heads:
            part = part * cos + pltpu.roll(part, LANES // 2, 1) * sin
        if h < q_heads:
            q_ref[:, h * LANES : (h + 1) * LANES] = part.astype(BF16)
        else:
            part = part + (krow_ref[...] if h < q_heads + kv_heads else vrow_ref[...])
            kv_ref[:, (h - q_heads) * LANES : (h - q_heads + 1) * LANES] = part.astype(BF16)


def project(normed, qkv, spread, cos, sin, krow, vrow, q_heads, kv_heads):
    tokens, model = normed.shape
    wide = spread.shape[1]
    bm = math.gcd(tokens, 256)
    whole = lambda a: pl.BlockSpec(a.shape, lambda i: (0, 0))
    row = lambda w: pl.BlockSpec((bm, w), lambda i: (i, 0))
    return pl.pallas_call(
        functools.partial(project_kernel, q_heads),
        grid=(tokens // bm,),
        in_specs=[row(model), whole(qkv), whole(spread), row(LANES), row(LANES), whole(krow), whole(vrow)],
        out_specs=[row(q_heads * LANES), row(2 * kv_heads * LANES)],
        out_shape=[
            jax.ShapeDtypeStruct((tokens, q_heads * LANES), BF16),
            jax.ShapeDtypeStruct((tokens, 2 * kv_heads * LANES), BF16),
        ],
        scratch_shapes=[pltpu.VMEM((model, wide), BF16)],
        compiler_params=pltpu.CompilerParams(vmem_limit_bytes=40 << 20),
        cost_estimate=pl.CostEstimate(
            flops=2 * tokens * model * wide, bytes_accessed=16 << 20, transcendentals=0
        ),
        name="project_qkv",
    )(normed, qkv, spread, cos, sin, krow, vrow)


def dense_kernel(
    chips, dq_ref, dkv_ref, after_ref, cos_ref, sin_ref, rotk_ref, valk_ref, att_ref, n_ref, *rest
):
    blocks, rest = rest[:chips], rest[chips:]
    dense_ref, grad_ref, normed, branch, send, recv, local = rest
    ranks = Ranks(2 * chips)
    fetch = pltpu.make_async_copy(n_ref, normed, local.at[chips])
    fetch.start()
    sem = pltpu.get_barrier_semaphore()
    pl.semaphore_signal(sem, inc=1, device_id={"tp": ranks.peer(0, 1)}, device_id_type=MESH)
    pl.semaphore_wait(sem, 1)
    copies = both_cores(ranks, blocks, branch, send, recv, local)
    for copy in copies:
        copy.start()
    width = dense_ref.shape[1]
    lanes = dkv_ref.shape[1] // 2
    cos, sin = cos_ref[...], sin_ref[...]
    turned = []
    for h in range(lanes // LANES):
        at = slice(h * LANES, (h + 1) * LANES)
        key = dkv_ref[:, at] + after_ref[:, at].astype(F32)
        turned.append((key * cos - pltpu.roll(key, LANES // 2, 1) * sin).astype(BF16))
    dk = dot(jnp.concatenate(turned, axis=1), rotk_ref[...]).astype(BF16)
    dv = (dkv_ref[:, lanes:] + after_ref[:, lanes:].astype(F32)).astype(BF16)
    dv = dot(dv, valk_ref[...]).astype(BF16)
    dense_ref[...] = jnp.concatenate([dq_ref[...], dk, dv], axis=1)
    fetch.wait()
    model = normed.shape[1]
    cols = math.gcd(model, 384)
    for d in range(0, model, cols):
        grad_ref[d : d + cols, :width] = dot(
            normed[:, d : d + cols], dense_ref[...], TN
        ).astype(BF16)
    for copy in copies:
        copy.wait()
    for d in range(0, model, cols):
        grad_ref[d : d + cols, width:] = dot(branch[:, d : d + cols], att_ref[...], TN).astype(BF16)


def dense_gradients(dq, dkv, after, cos, sin, rot_k, val_k, attended, normed, blocks):
    tokens, model = normed.shape
    chips = len(blocks)
    width = dq.shape[1] + 2 * rot_k.shape[1]
    total = width + attended.shape[1]
    vmem, hbm = pl.BlockSpec(memory_space=pltpu.VMEM), pl.BlockSpec(memory_space=pl.ANY)
    sem = pltpu.SemaphoreType.DMA
    return pl.pallas_call(
        functools.partial(dense_kernel, chips),
        in_specs=[vmem] * 8 + [hbm] * (1 + chips),
        out_specs=[vmem, vmem],
        out_shape=[
            jax.ShapeDtypeStruct((tokens, width), BF16),
            jax.ShapeDtypeStruct((model, total), BF16),
        ],
        scratch_shapes=[
            pltpu.VMEM((tokens, model), BF16),
            pltpu.VMEM((tokens, model), BF16),
            sem((chips,)), sem((chips,)), sem((chips + 1,)),
        ],
        compiler_params=pltpu.CompilerParams(
            vmem_limit_bytes=48 << 20, collective_id=5, has_side_effects=True
        ),
        cost_estimate=pl.CostEstimate(
            flops=2 * tokens * model * total, bytes_accessed=24 << 20, transcendentals=0
        ),
        name="dense_gradients",
    )(dq, dkv, after, cos, sin, rot_k, val_k, attended, normed, *blocks)


def close_kernel(
    count, shards, dense_ref, w_ref, x_ref, mg_ref, gain_ref, gain_two_ref, grad_ref, gate_ref, *rest
):
    layers, rest = rest[: count // 2], rest[count // 2 :]
    (
        out_ref, gain_grad_ref, half_ref, lay_ref, gate_out_ref, rows_in, rows_out, sums, c_send, c_recv, y_send,
        y_recv, x_mine, x_recv, gate_mine, gate_recv, t_send, t_recv, cs, cr, ys, yr, g_send, g_recv, xs, xr, x_sem,
        ls, lr, lay_sem, ts, tr, gate_sem, local,
    ) = rest
    ranks = Ranks(count)
    own = rows_in.shape[0]
    halves = 2
    rows = own // halves
    steps = ranks.chips * halves
    fetch = pltpu.make_async_copy(
        x_ref.at[pl.ds(pl.multiple_of(ranks.me * own, own), own)], rows_in, local.at[0]
    )
    fetch.start()
    def tile(at):
        return dot(dense_ref[pl.ds(at, rows), :], w_ref[...], NT)

    piece = lax.axis_index("ctx")
    half = grad_ref.shape[0] // (2 * shards)
    keeps = [
        pltpu.make_async_copy(
            grad_ref.at[half_rows(s, piece, half)], x_mine.at[pl.ds(s * half, half)], x_sem.at[s]
        )
        for s in range(shards)
    ]
    keeps.append(pltpu.make_async_copy(gate_ref, gate_mine, gate_sem.at[0]))
    for copy in keeps:
        copy.start()
    me = lax.axis_index("fsdp")
    barrier = pltpu.get_barrier_semaphore()
    for k, j in ranks.others():
        pl.semaphore_signal(barrier, inc=1, device_id={"tp": ranks.peer(k, j)}, device_id_type=MESH)
    for k in range(1, shards):
        pl.semaphore_signal(
            barrier, inc=1, device_id={"fsdp": lax.rem(me + k, shards)}, device_id_type=MESH
        )
    pl.semaphore_signal(barrier, inc=1, device_id={"ctx": 1 - piece}, device_id_type=MESH)
    pl.semaphore_wait(barrier, count + shards - 1)
    swaps = swap_halves(grad_ref, x_recv, xs, xr, shards)
    swaps.append(
        pltpu.make_async_remote_copy(
            src_ref=gate_ref, dst_ref=gate_recv, send_sem=gate_sem.at[1], recv_sem=gate_sem.at[2],
            device_id={"ctx": 1 - piece}, device_id_type=MESH,
        )
    )
    for copy in swaps:
        copy.start()
    forward = both_cores(ranks, layers, lay_ref, ls, lr, lay_sem)
    for copy in forward:
        copy.start()
    neighbour = ranks.peer(0, 1)

    def to_core(i):
        return remote(c_send.at[i], c_recv.at[i], cs.at[i], cr.at[i], neighbour)

    def to_chip(i, k):
        return remote(y_send.at[i], y_recv.at[i], ys.at[i], yr.at[i], ranks.peer(k, 0))

    def send_step(i, carry):
        k, u, at_mine, at_other = scatter_order(ranks, halves, own, i)
        c_send[i] = tile(at_other).astype(BF16)
        to_core(i).start()
        return carry

    def sum_step(i, carry):
        k, u, at_mine, at_other = scatter_order(ranks, halves, own, i)
        grad = tile(at_mine)
        to_core(i).wait_recv()
        grad = grad + c_recv[i].astype(F32)

        @pl.when(k != 0)
        def _():
            y_send[i] = grad.astype(BF16)
            to_chip(i, k).start()

        @pl.when(k == 0)
        def _():
            sums[u] = grad

        return carry

    lax.fori_loop(0, steps, send_step, 0)
    lax.fori_loop(0, steps, sum_step, 0)
    fetch.wait()
    gain = gain_ref[...]
    gain_total = None
    for u in range(halves):
        total = sums[u]
        for k in range(1, ranks.chips):
            i = (k - 1) * halves + u
            to_chip(i, k).wait_recv()
            total = total + y_recv[i].astype(F32)
        x = rows_in[u * rows : (u + 1) * rows]
        factor = lax.rsqrt(row_mean(x * x) + EPSILON)
        hat = x * factor
        term = jnp.sum(total * hat, axis=0, keepdims=True)
        gain_total = term if gain_total is None else gain_total + term
        inner = total * gain
        grad = mg_ref[u * rows : (u + 1) * rows] + factor * (inner - hat * row_mean(inner * hat))
        rows_out[u * rows : (u + 1) * rows] = grad.astype(BF16)
    gather = GatherRows(ranks, rows_out, out_ref, g_send, g_recv, local.at[0])
    gather.start()
    total = jnp.concatenate([gain_total, gain_two_ref[...], jnp.zeros((6, gain_total.shape[1]), F32)], axis=0)
    hops = [[{"tp": ranks.peer(0, 1)}], [{"tp": ranks.peer(k, 0)} for k in range(1, ranks.chips)]]
    hops += [[{"ctx": 1 - piece}], [{"fsdp": lax.rem(me + k, shards)} for k in range(1, shards)]]
    slot, sent = 0, []
    for n, peers in enumerate(hops):
        t_send[n] = total
        copies = []
        for peer in peers:
            copies.append(
                pltpu.make_async_remote_copy(
                    src_ref=t_send.at[n], dst_ref=t_recv.at[slot], send_sem=ts.at[slot],
                    recv_sem=tr.at[slot], device_id=peer, device_id_type=MESH,
                )
            )
            copies[-1].start()
            slot += 1
        for copy, at in zip(copies, range(slot - len(copies), slot)):
            copy.wait_recv()
            total = total + t_recv[at]
        sent += copies
    gain_grad_ref[...] = total
    for copy in sent:
        copy.wait_send()
    gather.finish()
    for copy in forward:
        copy.wait()
    for s in range(shards):
        keeps[s].wait()
        swaps[s].wait_recv()
        here = slice(s * half, (s + 1) * half)
        half_ref[here, :] = (x_mine[here, :].astype(F32) + x_recv[here, :].astype(F32)).astype(BF16)
    keeps[shards].wait()
    swaps[shards].wait_recv()
    gate_out_ref[...] = gate_mine[...].astype(F32) + gate_recv[...].astype(F32)
    for copy in swaps:
        copy.wait_send()
    for i in range(steps):
        to_core(i).wait_send()
    for i in range(steps - halves):
        to_chip(i, i // halves + 1).wait_send()


def close(count, shards, dense, weight, layer_input, middle_grad, gain, gain_two, grad, gate, layers):
    tokens, model = layer_input.shape
    own = tokens // count
    rows, steps, chips = own // 2, count, count // 2
    vmem, hbm = pl.BlockSpec(memory_space=pltpu.VMEM), pl.BlockSpec(memory_space=pl.ANY)
    sem = pltpu.SemaphoreType.DMA
    return pl.pallas_call(
        functools.partial(close_kernel, count, shards),
        in_specs=[vmem, vmem, hbm, vmem, vmem, vmem, hbm, hbm] + [hbm] * chips,
        out_specs=[hbm, vmem, vmem, hbm, vmem],
        out_shape=[
            jax.ShapeDtypeStruct((tokens, model), BF16),
            jax.ShapeDtypeStruct((8, model), F32),
            jax.ShapeDtypeStruct((model // 2, grad.shape[1]), BF16),
            jax.ShapeDtypeStruct((tokens, model), BF16),
            jax.ShapeDtypeStruct(gate.shape, F32),
        ],
        scratch_shapes=[
            pltpu.VMEM((own, model), F32),
            pltpu.VMEM((own, model), BF16),
            pltpu.VMEM((2, rows, model), F32),
        ]
        + [pltpu.VMEM((steps, rows, model), BF16)] * 2
        + [pltpu.VMEM((steps - 2, rows, model), BF16)] * 2
        + [pltpu.VMEM((model // 2, grad.shape[1]), BF16)] * 2
        + [
            pltpu.VMEM(gate.shape, BF16),
            pltpu.VMEM(gate.shape, BF16),
            pltpu.VMEM((4, 8, model), F32),
            pltpu.VMEM((chips + shards, 8, model), F32),
            sem((steps,)), sem((steps,)), sem((steps - 2,)), sem((steps - 2,)),
            sem((2, chips)), sem((2, chips)), sem((shards,)), sem((shards,)), sem((shards,)),
            sem((chips,)), sem((chips,)), sem((chips,)), sem((chips + shards,)),
            sem((chips + shards,)), sem((3,)), sem((2,)),
        ],
        compiler_params=pltpu.CompilerParams(
            vmem_limit_bytes=48 << 20, collective_id=3, has_side_effects=True
        ),
        cost_estimate=pl.CostEstimate(
            flops=2 * tokens * model * dense.shape[1], bytes_accessed=200 << 20, transcendentals=0
        ),
        name="close_layer",
    )(dense, weight, layer_input, middle_grad, gain, gain_two, grad, gate, *layers)


def per_device(
    sizes,
    layer_input,
    doc_lengths,
    attention_gain,
    query_weight,
    key_matrix,
    value_matrix,
    output_weight,
    feedforward_gain,
    gate_weight,
    up_weight,
    down_weight,
    output_cotangent,
):
    shards, pieces, ranks = sizes
    assert pieces == 2 and ranks % 2 == 0
    chips = ranks // 2
    tokens, model = layer_input.shape
    own = tokens // ranks
    head_dim = HEAD_SIZE
    q_heads = query_weight.shape[1] // head_dim
    kv_heads = key_matrix.shape[1] // head_dim
    q_width, kv_width = q_heads * head_dim, kv_heads * head_dim
    piece = lax.axis_index("ctx")
    rank = lax.axis_index("tp")
    chip, core = rank // 2, rank % 2
    me = lax.axis_index("fsdp")
    scale = 1.0 / math.sqrt(head_dim)

    swap_x = [(0, 1), (1, 0)]
    swap_core = [(i, i ^ 1) for i in range(ranks)]

    def chip_shift(k):
        return [(i, (i + 2 * k) % ranks) for i in range(ranks)]

    def shard_shift(k):
        return [(i, (i + k) % shards) for i in range(shards)]

    def pick(array, index, axis=0):
        return lax.dynamic_index_in_dim(array, index, axis, keepdims=False)

    def half_of(shard):
        rows = shard.shape[0] // 2
        return lax.dynamic_slice_in_dim(shard, piece * rows, rows, 0)

    both_axes = ("fsdp", "ctx")

    def reduce_fsdp(part):
        return lax.psum_scatter(part, "fsdp", scatter_dimension=0, tiled=True)

    def add_pieces(mine):
        return mine.astype(F32) + lax.ppermute(mine, "ctx", swap_x).astype(F32)

    def whole_shard(mine):
        other = lax.ppermute(mine, "ctx", swap_x)
        pair = jnp.where(
            piece == 0, jnp.concatenate([mine, other], 0), jnp.concatenate([other, mine], 0)
        )
        return pair.astype(F32)

    ff_half = half_of(jnp.concatenate([gate_weight, up_weight, down_weight.T], axis=1))
    gain_shard = jnp.stack([attention_gain, feedforward_gain]).astype(F32)
    gain_shard = jnp.pad(gain_shard, ((0, 6), (0, 0)))
    qkv_shard = jnp.concatenate([query_weight, key_matrix, value_matrix], axis=1)
    positions = doc_positions(doc_lengths[0], piece * tokens, tokens)
    cos, sin = rotary_lanes(positions, head_dim)
    lane = lax.broadcasted_iota(jnp.int32, (1, LANES), 1)
    krow = jnp.where((lane >= head_dim // 2) & (lane < head_dim // 2 + 3), -1.0, 0.0)
    vrow = jnp.where((lane >= head_dim) & (lane < head_dim + 3), 1.0, 0.0)
    spread = jnp.zeros((q_width + 2 * kv_width, (q_heads + 2 * kv_heads) * LANES), BF16)
    rot_q, rot_k = select_rotary(q_heads, head_dim), select_rotary(kv_heads, head_dim)
    val_q, val_k = select_value(q_heads, head_dim), select_value(kv_heads, head_dim)
    spread = spread.at[:q_width, : q_heads * LANES].set(rot_q.T)
    spread = spread.at[q_width : q_width + kv_width, q_heads * LANES : (q_heads + kv_heads) * LANES].set(rot_k.T)
    spread = spread.at[q_width + kv_width :, (q_heads + kv_heads) * LANES :].set(val_k.T)

    normed_one, qkv_full, out_own, gains_full = begin(
        shards, layer_input, qkv_shard, output_weight.T, gain_shard
    )
    queries, keys_values = project(
        normed_one, qkv_full, spread, cos, sin, krow, vrow, q_heads, kv_heads
    )
    ff_half, gains_full = lax.optimization_barrier((ff_half, gains_full))
    ff_full = lax.all_gather(ff_half, both_axes, axis=0, tiled=True)
    gain_one, gain_two = gains_full[0:1], gains_full[1:2]
    before = lax.ppermute(keys_values, "ctx", [(0, 1)])
    base = -(piece - 1) * tokens
    ends = jnp.cumsum(doc_lengths[0]).astype(jnp.int32) + base
    base = base.astype(jnp.int32).reshape(1)
    state = attention_forward(ends, base, queries, keys_values, head_dim, tokens)
    attended, marked = attention_forward(
        ends, base, queries, before, head_dim, 0, state, val_q
    )
    wo = [out_own] + [lax.ppermute(out_own, "tp", chip_shift(k)) for k in range(1, chips)]
    normed_two, middle, wo_others = mix(ranks, attended, layer_input, gain_two, wo)
    (
        feed_sums, middle_grad, branch_grad, gain_two_grad, attended_grad, gate_part, feed_part,
    ) = feedforward(
        ranks, normed_two, output_cotangent, middle, gain_two, ff_full, wo, wo_others
    )
    gate_own, feed_own = reduce_fsdp(gate_part), reduce_fsdp(feed_part)
    cut = feed_sums.reshape(chips, own, model)
    feed_sums = [lax.ppermute(cut[k - 1], "tp", chip_shift(k)) for k in range(1, chips)]
    dq_part, dkv_before = attention_backward(
        ends, base, marked, attended_grad, attended, before, val_q.T, head_dim, 0
    )
    after = lax.ppermute(dkv_before, "ctx", [(1, 0)])
    dq, dkv = attention_backward(
        ends, base, marked, attended_grad, attended, keys_values, val_q.T, head_dim, tokens,
        (dq_part, cos, sin, rot_q),
    )

    feed_sums, dq = lax.optimization_barrier((feed_sums, dq))
    layer_rows = middle + cut[chips - 1].astype(F32)
    for block in feed_sums:
        layer_rows = layer_rows + block.astype(F32)
    layer_rows = layer_rows.astype(BF16)

    def from_chips(rows):
        return [rows] + [lax.ppermute(rows, "tp", chip_shift(k)) for k in range(1, chips)]

    dqkv, attention_part = dense_gradients(
        dq, dkv, after, cos, sin, rot_k, val_k, attended, normed_one, from_chips(branch_grad)
    )
    input_gradient, gains, attention_half, layer_output, gate = close(
        ranks, shards, dqkv, qkv_full, layer_input, middle_grad, gain_one, gain_two_grad,
        attention_part, gate_own, from_chips(layer_rows),
    )
    attention_half, feed_own = lax.optimization_barrier((attention_half, feed_own))
    attention = whole_shard(reduce_fsdp(attention_half))
    feed = add_pieces(feed_own)
    layer_output, input_gradient = layer_output.astype(F32), input_gradient.astype(F32)
    ff_width = gate_weight.shape[1]
    gains = lax.dynamic_slice_in_dim(gains, me * gain_shard.shape[1], gain_shard.shape[1], 1)

    return (
        layer_output,
        input_gradient,
        gains[0],
        attention[:, :q_width],
        attention[:, q_width : q_width + kv_width],
        attention[:, q_width + kv_width : q_width + 2 * kv_width],
        attention[:, q_width + 2 * kv_width :].T,
        gains[1],
        gate,
        feed[:, :ff_width],
        feed[:, ff_width:].T,
    )


def solution(mesh):
    rows = P(("fsdp", "ctx"), None)
    into, out_of = P("fsdp", "tp"), P("tp", "fsdp")
    sizes = (mesh.shape["fsdp"], mesh.shape["ctx"], mesh.shape["tp"])
    return jax.shard_map(
        functools.partial(per_device, sizes),
        mesh=mesh,
        in_specs=(
            rows, P("fsdp", None), P("fsdp"), into, into, into, out_of, P("fsdp"), into, into,
            out_of, rows,
        ),
        out_specs=(
            rows, rows, P("fsdp"), into, into, into, out_of, P("fsdp"), into, into, out_of,
        ),
        check_vma=False,
    )
```

time: 2170 us -> 526 us (0.24)
  waiting for transfers between devices: 1370 us -> 102 us
  matrix products: 399 us -> 0 us
  Pallas kernels: 0 us -> 330 us
  other arithmetic: 189 us -> 25.5 us
  blocking collectives: 90.6 us -> 0 us
  local copies, waits for them, and re-layouts: 86.8 us -> 34.3 us
    psum x5 -> x0, waiting for transfers between devices: 691 us -> none  [the longest x1 171 us: per_device(): normed_one_grad = lax.psum(normed_one_part, 'tp')]
    reduce_scatter x9 -> x3, waiting for transfers between devices: 499 us -> 26 us  [reduce_fsdp(): return lax.psum_scatter(part, 'fsdp', scatter_dimension=0, tiled=True)]
    dot_general x42 -> x0, matrix products: 399 us -> none  [the longest x6 70.1 us: scores_of(): jnp.einsum('qhgd,khd->hgqk', query_block, all_keys, preferred_element_typ...]
    pallas_call x0 -> x10, Pallas kernels: none -> 330 us  [the longest x1 93.8 us: close(): pl.pallas_call(functools.partial(close_kernel, count, shards), in_specs=[...]
    all_gather x7 -> x1, waiting for transfers between devices: 172 us -> 22 us  [per_device(): ff_full = lax.all_gather(ff_half, both_axes, axis=0, tiled=True)]
    reduce_sum x7 -> x0, other arithmetic: 67.5 us -> none  [the longest x3 36.1 us: forward_block(): total = jnp.sum(jnp.exp(scores - highest), axis=-1, keepdims=True)]
    all_gather x4 -> x0, blocking collectives: 66.3 us -> none  [the longest x1 24.4 us: per_device(): lax.all_gather(value_matrix, 'fsdp', axis=0, tiled=True)]
    dynamic_update_slice x12 -> x0, local copies, waits for them, and re-layouts: 56.5 us -> none  [the longest x6 53.5 us: per_device(): lax.scan(backward_block, (empty, empty), jnp.arange(blocks, dtype=jnp.int...]
  transfers between devices with their start and end apart: 21 -> 12, of which waited for: 18 -> 6; matrix products, arithmetic and copies ran while one was open for 14% -> 6% of each run, Pallas kernels for 0% -> 40%
where the time goes in v1:
time: 526 us; the launch traced here: 518 us
  Pallas kernels  330 us (63%)
  waiting for transfers between devices  102 us (19%)
  local copies, waits for them, and re-layouts  34.3 us (7%)
  other arithmetic  25.5 us (5%)
  between operations  14.6 us (3%)
  starting transfers between devices  12 us (2%)
    pallas_call x1, Pallas kernels, close(): pl.pallas_call(functools.partial(close_kernel, count, shards), in_specs=[...  93.8 us
    pallas_call x1, Pallas kernels, feedforward(): pl.pallas_call(functools.partial(feedforward_kernel, count), in_specs=[hb...  79.1 us
    pallas_call x1, Pallas kernels, mix(): pl.pallas_call(functools.partial(mix_kernel, count), in_specs=[hbm, hbm,...  48 us
    pallas_call x1, Pallas kernels, begin(): pl.pallas_call(functools.partial(begin_kernel, shards), in_specs=[hbm, vm...  44.7 us
    ppermute x2, waiting for transfers between devices, from_chips(): lax.ppermute(rows, 'tp', chip_shift(k))  28.9 us
    pallas_call x2, Pallas kernels, attention_backward(): pl.pallas_call(functools.partial(attention_backward_kernel, rest is None,...  28.6 us
    unnamed x79, local copies, waits for them, and re-layouts  27.3 us
    reduce_scatter x3, waiting for transfers between devices, reduce_fsdp(): return lax.psum_scatter(part, 'fsdp', scatter_dimension=0, tiled=True)  26 us
  transfers between devices with their start and end apart: 12, of which 6 were waited for; matrix products, arithmetic and copies ran while one was open for 6% of the time, Pallas kernels for 40%

profile of v1, /device:TPU:0, one launch (start us, length us, event | category | flops | bytes accessed | tf_op | source)
XLA Modules:
  0.0 518.2 jit_solution(4364674813764479856)
XLA Ops:
  13.3 44.7 %norm_and_gather.1 = (bf16[1536,1536]{1,0:T(8,128)(2,1)}, bf16[1536,768]{1,0:T(8,128)(2,1)S(1)}, bf16[1536,384]{1,0:T(8,128)(2,1)S(1)}, f32[8,1536]{1,0:T(8,128)S(1)}) custom-call(f32[1536,1536]{1,0:T(8,128)} %x_ref.5, bf16[384,768]{1,0:T(8,128)(2,1)S(1)} %pad_maximum_fusion.4.qkv_ref, bf16[384,384]{1,0:T(8,128)(2,1)S(1)} %bitcast.17, ...), custom_call_target="tpu_custom_call" | custom-call | bytes 125829120 | tf_op jit(solution)/shard_map/norm_and_gather/pallas_call | solution.py:918
  62.9 2.8 fusion.21
  66.6 3.0 copy-done.12
  69.7 9.0 %project_qkv.1 = (bf16[1536,512]{1,0:T(8,128)(2,1)S(1)}, bf16[1536,512]{1,0:T(8,128)(2,1)S(1)}) custom-call(bf16[1536,1536]{1,0:T(8,128)(2,1)S(1)} %copy-done.12, bf16[1536,768]{1,0:T(8,128)(2,1)S(1)} %get-tuple-element.85.qkv_ref.w_ref, bf16[768,1024]{1,0:T(8,128)(2,1)S(1)} %fusion.28.spread_ref, f32[1536,128]{1,0:T(8,128)S(1)} %get-tuple-element.154.cos_ref.rest_1_, ...), custom_call_target="tpu_custom_call" | custom-call | flops 4831838208 | bytes 16777216 | tf_op jit(solution)/shard_map/project_qkv/pallas_call | solution.py:975
  78.7 3.2 collective-permute-start
  84.5 9.1 %attention_forward.2 = (f32[3,2,1,1024]{3,2,1,0:T(1,128)S(1)}, f32[3,2,128,1024]{3,2,1,0:T(8,128)S(1)}) custom-call(s32[3]{0:T(128)S(1)} %get-tuple-element.167.ends_ref, s32[1]{0:T(128)} %bitcast.2.base_ref, bf16[1536,512]{1,0:T(8,128)(2,1)S(1)} %get-tuple-element.86.q_ref, bf16[1536,512]{1,0:T(8,128)(2,1)S(1)} %get-tuple-element.87.kv_ref), custom_call_target="tpu_custom_call" | custom-call | flops 4831838208 | bytes 8388608 | tf_op jit(solution)/shard_map/attention_forward/pallas_call | solution.py:195
  93.6 21.1 %collective-permute-done.kv_ref = bf16[1536,512]{1,0:T(8,128)(2,1)S(1)} collective-permute-done((bf16[1536,512]{1,0:T(8,128)(2,1)S(1)}, bf16[1536,512]{1,0:T(8,128)(2,1)S(1)}, u32[]{:S(2)}, u32[]{:S(2)}) %collective-permute-start) | collective-permute-done | bytes 1572896 | tf_op jit(solution)/shard_map/ppermute | solution.py:1341
  114.7 4.4 attention_forward.3
  120.2 48.0 %mix_heads.1 = (bf16[1536,1536]{1,0:T(8,128)(2,1)S(1)}, f32[384,1536]{1,0:T(8,128)S(1)}, bf16[2,1536,384]{2,1,0:T(8,128)(2,1)S(1)}) custom-call(bf16[1536,384]{1,0:T(8,128)(2,1)S(1)} %get-tuple-element.90.att_ref.o_ref, f32[1536,1536]{1,0:T(8,128)} %x_ref.5, f32[1,1536]{1,0:T(1,128)S(1)} %get-tuple-element.156.gain_ref, bf16[1536,384]{1,0:T(8,128)(2,1)S(1)} %copy-done.16, ...), custom_call_target="tpu_custom_call" | custom-call | flops 7247757312 | bytes 157286400 | tf_op jit(solution)/shard_map/mix_heads/pallas_call | solution.py:480
  171.8 2.2 copy-done.21
  175.4 22.0 %all-gather.2.cloned.1.call-done.weight_ref = bf16[1536,3072]{1,0:T(8,128)(2,1)} async-done(((bf16[192,3072]{1,0:T(8,128)(2,1)}), bf16[1536,3072]{1,0:T(8,128)(2,1)}) %all-gather.2.cloned.1.call-update) | async-done | bytes 9437200 | tf_op jit(solution)/shard_map/all_gather | solution.py:1339
  197.3 79.1 %feed_forward.1 = (bf16[4,192,1536]{2,1,0:T(8,128)(2,1)}, f32[384,1536]{1,0:T(8,128)}, bf16[384,1536]{1,0:T(8,128)(2,1)}, f32[1,1536]{1,0:T(1,128)}, bf16[1536,3...) custom-call(bf16[1536,1536]{1,0:T(8,128)(2,1)} %copy-done.21, f32[1536,1536]{1,0:T(8,128)} %cot_ref.1, ...), custom_call_target="tpu_custom_call" | custom-call | flops 43486543872 | bytes 293601280 | tf_op jit(solution)/shard_map/feed_forward/pallas_call | solution.py:734
  280.5 5.1 attention_backward.2
  288.3 23.5 %attention_backward.3 = (bf16[1536,384]{1,0:T(8,128)(2,1)S(1)}, f32[1536,512]{1,0:T(8,128)}) custom-call(s32[3]{0:T(128)S(1)} %get-tuple-element.167.ends_ref, s32[1]{0:T(128)} %bitcast.2.base_ref, bf16[1536,512]{1,0:T(8,128)(2,1)} %copy-done.22, bf16[1536,384]{1,0:T(8,128)(2,1)S(1)} %copy-done.25, bf16[1536,384]{1,0:T(8,128)(2,1)S(1)} %copy-done.20, ...), custom_call_target="tpu_custom_call" | custom-call | flops 12079595520 | bytes 12582912 | tf_op jit(solution)/shard_map/attention_backward/pallas_call | solution.py:315
  314.5 19.1 %collective-permute-done.4.rest_1_ = bf16[384,1536]{1,0:T(8,128)(2,1)} collective-permute-done((bf16[384,1536]{1,0:T(8,128)(2,1)S(1)}, bf16[384,1536]{1,0:T(8,128)(2,1)}, u32[]{:S(2)}, u32[]{:S(2)}) %collective-permute-start.4) | collective-permute-done | bytes 1179680 | tf_op jit(solution)/shard_map/ppermute | solution.py:1375
  333.5 13.5 %dense_gradients.1 = (bf16[1536,768]{1,0:T(8,128)(2,1)}, bf16[1536,1152]{1,0:T(8,128)(2,1)}) custom-call(bf16[1536,384]{1,0:T(8,128)(2,1)S(1)} %get-tuple-element.103.dq_ref, f32[1536,512]{1,0:T(8,128)} %get-tuple-element.104.dkv_ref, bf16[1536,512]{1,0:T(8,128)(2,1)} %collective-permute-done.3.after_ref, f32[1536,128]{1,0:T(8,128)S(1)} %copy-done.7, ...), custom_call_target="tpu_custom_call" | custom-call | flops 5435817984 | bytes 25165824 | tf_op jit(solution)/shard_map/dense_gradients/pallas_call | solution.py:1039
  347.0 9.8 %collective-permute-done.5.rest_1_ = bf16[384,1536]{1,0:T(8,128)(2,1)S(1)} collective-permute-done((bf16[384,1536]{1,0:T(8,128)(2,1)S(1)}, bf16[384,1536]{1,0:T(8,128)(2,1)S(1)}, u32[]{:S(2)}, u32[]{:S(2)}) %collective-permute-start.5) | collective-permute-done | bytes 1179680 | tf_op jit(solution)/shard_map/ppermute | solution.py:1375
  360.3 93.8 %close_layer.1 = (bf16[1536,1536]{1,0:T(8,128)(2,1)}, f32[8,1536]{1,0:T(8,128)S(1)}, bf16[768,1152]{1,0:T(8,128)(2,1)}, bf16[1536,1536]{1,0:T(8,128)(2,1)}, f32[384,1024]{1,0:T(8,128)S(1)}) custom-call(bf16[1536,768]{1,0:T(8,128)(2,1)} %get-tuple-element.107.dense_ref, bf16[1536,768]{1,0:T(8,128)(2,1)} %copy-done, f32[1536,1536]{1,0:T(8,128)} %x_ref.5, ...), custom_call_target="tpu_custom_call" | custom-call | flops 3623878656 | bytes 209715200 | tf_op jit(solution)/shard_map/close_layer/pallas_call | solution.py:1216
  454.9 7.6 %convert_element_type.73 = f32[1536,1536]{1,0:T(8,128)} convert(bf16[1536,1536]{1,0:T(8,128)(2,1)} %get-tuple-element.113) | non-fusion elementwise | flops 2359296 | bytes 14155776 | tf_op jit(solution)/shard_map/convert_element_type | solution.py:1387
  462.5 5.1 convert_element_type.74
  468.3 26.0 %reduce-scatter.8.cloned.1.call-done = bf16[192,1152]{1,0:T(8,128)(2,1)} async-done(((bf16[768,1152]{1,0:T(8,128)(2,1)}), bf16[192,1152]{1,0:T(8,128)(2,1)}) %reduce-scatter.8.cloned.1.call-update) | async-done | bytes 442384 | tf_op jit(solution)/shard_map/reduce_scatter | solution.py:1304
  495.8 2.5 convert_add_fusion
  500.1 3.1 copy.38
  503.2 3.0 collective-permute-done.6
  (133 shorter events, 43.2 us)
Async XLA Ops:
  7.2 190.1 %all-gather.2.cloned.1.call-start = ((), (), s32[]{:S(2)}) async-start(), calls=%async_computation.3 | async-start | bytes 10616832 | tf_op jit(solution)/shard_map/all_gather | solution.py:1339
  13.3 45.8 %copy-start.26 = (bf16[1024,384]{0,1:T(8,128)(2,1)S(1)}, bf16[1024,384]{0,1:T(8,128)(2,1)}, u32[]{:S(2)}) copy-start(bf16[1024,384]{0,1:T(8,128)(2,1)} %copy.34) | copy-start | bytes 2359300
  13.3 45.8 %copy-start.28 = (bf16[384,1024]{1,0:T(8,128)(2,1)S(1)}, bf16[384,1024]{1,0:T(8,128)(2,1)}, u32[]{:S(2)}) copy-start(bf16[384,1024]{1,0:T(8,128)(2,1)} %param.26) | copy-start | bytes 2359300
  13.3 45.7 %copy-start.29 = (bf16[384,1024]{1,0:T(8,128)(2,1)S(1)}, bf16[384,1024]{1,0:T(8,128)(2,1)}, u32[]{:S(2)}) copy-start(bf16[384,1024]{1,0:T(8,128)(2,1)} %param.27) | copy-start | bytes 2359300
  60.4 297.5 %reduce-scatter.4.cloned.1.call-start = ((), (), s32[]{:S(2)}) async-start(), calls=%async_computation.4 | async-start | bytes 3932160 | tf_op jit(solution)/shard_map/reduce_scatter | solution.py:1304
  66.6 12.0 %copy-start.6 = (f32[1536,128]{1,0:T(8,128)}, f32[1536,128]{1,0:T(8,128)S(1)}, u32[]{:S(2)}) copy-start(f32[1536,128]{1,0:T(8,128)S(1)} %get-tuple-element.154.cos_ref.rest_1_) | copy-start | bytes 2359300
  69.7 12.2 %copy-start.16 = (bf16[1536,384]{1,0:T(8,128)(2,1)S(1)}, bf16[1536,384]{1,0:T(8,128)(2,1)}, u32[]{:S(2)}) copy-start(bf16[1536,384]{1,0:T(8,128)(2,1)} %copy-done.15) | copy-start | bytes 3538948
  78.7 14.9 %copy-start.13 = (bf16[1536,512]{1,0:T(8,128)(2,1)}, bf16[1536,512]{1,0:T(8,128)(2,1)S(1)}, u32[]{:S(2)}) copy-start(bf16[1536,512]{1,0:T(8,128)(2,1)S(1)} %get-tuple-element.87.kv_ref) | copy-start | bytes 4718596
  78.7 36.0 %collective-permute-start = (bf16[1536,512]{1,0:T(8,128)(2,1)S(1)}, bf16[1536,512]{1,0:T(8,128)(2,1)S(1)}, u32[]{:S(2)}, u32[]{:S(2)}) collective-permute-start(bf16[1536,512]{1,0:T(8,128)(2,1)S(1)} %get-tuple-element.87.kv_ref), channel_id=1, source_target_pairs={{0,4},{1,5},{2,6},{3,7},{8,12},{9,13},{10,14},{11,15},{16,20},{17,... | collective-permute-start | bytes 4718600 | tf_op jit(solution)/shard_map/ppermute | solution.py:1341
  81.9 38.3 %collective-permute-start.1 = (bf16[1536,384]{1,0:T(8,128)(2,1)S(1)}, bf16[1536,384]{1,0:T(8,128)(2,1)S(1)}, u32[]{:S(2)}, u32[]{:S(2)}) collective-permute-start(bf16[1536,384]{1,0:T(8,128)(2,1)S(1)} %copy-done.16), channel_id=1, source_target_pairs={{0,2},{1,3},{2,0},{3,1},{4,6},{5,7},{6,4},{7,5},{8,10},{9,11},{10,... | collective-permute-start | bytes 3538952 | tf_op jit(solution)/shard_map/ppermute | solution.py:1349
  83.5 36.7 %copy-start.11 = (f32[1,1536]{1,0:T(1,128)}, f32[1,1536]{1,0:T(1,128)S(1)}, u32[]{:S(2)}) copy-start(f32[1,1536]{1,0:T(1,128)S(1)} %get-tuple-element.156.gain_ref) | copy-start | bytes 18436
  276.4 177.7 %reduce-scatter.6.cloned.1.call-start = ((), (), s32[]{:S(2)}) async-start(), calls=%async_computation.5 | async-start | bytes 7864320 | tf_op jit(solution)/shard_map/reduce_scatter | solution.py:1304
  277.2 217.1 %reduce-scatter.8.cloned.1.call-start = ((), (), s32[]{:S(2)}) async-start(), calls=%async_computation.6 | async-start | bytes 2211840 | tf_op jit(solution)/shard_map/reduce_scatter | solution.py:1304
  279.2 32.6 %collective-permute-start.2 = (bf16[384,1536]{1,0:T(8,128)(2,1)S(1)}, bf16[384,1536]{1,0:T(8,128)(2,1)}, u32[]{:S(2)}, u32[]{:S(2)}) collective-permute-start(bf16[384,1536]{1,0:T(8,128)(2,1)S(1)} %bitcast.21), channel_id=1, source_target_pairs={{0,2},{1,3},{2,0},{3,1},{4,6},{5,7},{6,4},{7,5},{8,10},{9,11},{10,... | collective-permute-start | bytes 3538952 | tf_op jit(solution)/shard_map/ppermute | solution.py:1358
  280.5 7.8 %copy-start.7 = (f32[1536,128]{1,0:T(8,128)S(1)}, f32[1536,128]{1,0:T(8,128)}, u32[]{:S(2)}) copy-start(f32[1536,128]{1,0:T(8,128)} %copy-done.6) | copy-start | bytes 2359300
  280.5 7.8 %copy-start.9 = (bf16[512,384]{1,0:T(8,128)(2,1)S(1)}, bf16[512,384]{1,0:T(8,128)(2,1)}, u32[]{:S(2)}) copy-start(bf16[512,384]{1,0:T(8,128)(2,1)} %get-tuple-element.157.rest_3_) | copy-start | bytes 1179652
  285.6 48.0 %collective-permute-start.3 = (bf16[1536,512]{1,0:T(8,128)(2,1)S(1)}, bf16[1536,512]{1,0:T(8,128)(2,1)}, u32[]{:S(2)}, u32[]{:S(2)}) collective-permute-start(bf16[1536,512]{1,0:T(8,128)(2,1)S(1)} %get-tuple-element.105), channel_id=1, source_target_pairs={{4,0},{5,1},{6,2},{7,3},{12,8},{13,9},{14,10},{15,11},{20,16},{21,... | collective-permute-start | bytes 4718600 | tf_op jit(solution)/shard_map/ppermute | solution.py:1362
  286.9 46.7 %collective-permute-start.4 = (bf16[384,1536]{1,0:T(8,128)(2,1)S(1)}, bf16[384,1536]{1,0:T(8,128)(2,1)}, u32[]{:S(2)}, u32[]{:S(2)}) collective-permute-start(bf16[384,1536]{1,0:T(8,128)(2,1)S(1)} %copy-done.17), channel_id=1, source_target_pairs={{0,2},{1,3},{2,0},{3,1},{4,6},{5,7},{6,4},{7,5},{8,10},{9,11},{10,... | collective-permute-start | bytes 3538952 | tf_op jit(solution)/shard_map/ppermute | solution.py:1375
  288.3 23.6 %copy-start.2 = (f32[384,1536]{1,0:T(8,128)S(1)}, f32[384,1536]{1,0:T(8,128)}, u32[]{:S(2)}) copy-start(f32[384,1536]{1,0:T(8,128)} %copy-done.1) | copy-start | bytes 7077892
  313.6 43.3 %collective-permute-start.5 = (bf16[384,1536]{1,0:T(8,128)(2,1)S(1)}, bf16[384,1536]{1,0:T(8,128)(2,1)S(1)}, u32[]{:S(2)}, u32[]{:S(2)}) collective-permute-start(bf16[384,1536]{1,0:T(8,128)(2,1)S(1)} %fusion.1.rest_0_), channel_id=1, source_target_pairs={{0,2},{1,3},{2,0},{3,1},{4,6},{5,7},{6,4},{7,5},{8,10},{9,11},{10,... | collective-permute-start | bytes 3538952 | tf_op jit(solution)/shard_map/ppermute | solution.py:1375
  333.5 24.3 %copy-start.10 = (f32[1,1536]{1,0:T(1,128)S(1)}, f32[1,1536]{1,0:T(1,128)}, u32[]{:S(2)}) copy-start(f32[1,1536]{1,0:T(1,128)} %get-tuple-element.109.gain_two_ref) | copy-start | bytes 18436
  454.1 8.4 %slice-start = ((s8[4718592]{0:T(1024)(128)(4,1)}), s8[524288]{0:T(1024)(128)(4,1)S(1)}, s32[]{:S(2)}) async-start(s8[4718592]{0:T(1024)(128)(4,1)} %bitcast.18), calls=%async_computation.7 | async-start | bytes 1048576
  454.1 41.6 %collective-permute-start.7 = (bf16[384,2048]{1,0:T(8,128)(2,1)}, bf16[384,2048]{1,0:T(8,128)(2,1)}, u32[]{:S(2)}, u32[]{:S(2)}) collective-permute-start(bf16[384,2048]{1,0:T(8,128)(2,1)} %reduce-scatter.6.cloned.1.call-done), channel_id=1, source_target_pairs={{0,4},{4,0},{1,5},{5,1},{2,6},{6,2},{3,7},{7,3},{8,12},{12,8},{9,1... | collective-permute-start | bytes 4718600 | tf_op jit(solution)/shard_map/ppermute | solution.py:1307
  494.3 12.0 %collective-permute-start.6 = (bf16[192,1152]{1,0:T(8,128)(2,1)}, bf16[192,1152]{1,0:T(8,128)(2,1)S(1)}, u32[]{:S(2)}, u32[]{:S(2)}) collective-permute-start(bf16[192,1152]{1,0:T(8,128)(2,1)} %reduce-scatter.8.cloned.1.call-done), channel_id=1, source_target_pairs={{0,4},{4,0},{1,5},{5,1},{2,6},{6,2},{3,7},{7,3},{8,12},{12,8},{9,1... | collective-permute-start | bytes 1327112 | tf_op jit(solution)/shard_map/ppermute | solution.py:1310
  (23 other events, 72.8 us)
Sparse Core Ops, SparseCore 0:
  60.5 136.7 all-gather.1
  276.5 58.1 reduce-scatter.3
  337.0 113.9 reduce-scatter.5
  454.2 39.9 reduce-scatter.7

commit v2 on v1

--- a/solution.py
+++ b/solution.py
@@ -538,13 +538,13 @@
     pl.semaphore_wait(sem, count)
 
 
-def feedforward_kernel(count, n2_ref, cot_ref, mid_ref, gain_ref, other_ref, weight_ref, *rest):
+def feedforward_kernel(count, shards, n2_ref, cot_ref, mid_ref, gain_ref, other_ref, weight_ref, *rest):
     blocks, rest = rest[: count // 2], rest[count // 2 :]
     (
-        ffb_ref, mg_ref, bg_ref, gain_grad_ref, da_ref, grad_ref, grads_ref,
+        ffb_ref, mg_ref, bg_ref, gain_grad_ref, da_ref, gate_ref, up_ref, down_ref,
         gate_w, up_w, down_w, n2, fg, hid, gu, rows_in, ffb_out,
-        c_send, c_recv, y_send, y_recv, f_send, f_recv, heads,
-        w_sem, in_sem, out_sem, cs, cr, ys, yr, fs, fr, hs, hr, local,
+        c_send, c_recv, y_send, y_recv, f_send, f_recv, heads, x_recv,
+        w_sem, in_sem, out_sem, cs, cr, ys, yr, fs, fr, hs, hr, xs, xr, local,
     ) = rest
     ranks = Ranks(count)
     own = mg_ref.shape[0]
@@ -593,7 +593,7 @@
         return dot(gg, gate_w[...], NT) + dot(ug, up_w[...], NT), dot(hidden, down_w[...], NT)
 
     read(scatter_order(ranks, halves, own, 0)[3], 0).start()
-    ranks.barrier()
+    signal_piece(count)
     neighbour = ranks.peer(0, 1)
 
     def to_core(i):
@@ -664,15 +664,24 @@
     cols = math.gcd(model, 384)
     writes = []
 
-    def product(left, right, full, dst, n):
+    def product(left, right, full, pairs):
         for d in range(model // cols):
             full[d * cols : (d + 1) * cols, :] = dot(
                 left[:, d * cols : (d + 1) * cols], right, TN
             ).astype(BF16)
-        writes.append(pltpu.make_async_copy(full, dst, out_sem.at[1 + n]))
-        writes[-1].start()
-
-    product(n2, gu[:, :width], gate_w, grad_ref, 0)
+        for src, dst in pairs:
+            writes.append(pltpu.make_async_copy(src, dst, out_sem.at[1 + len(writes)]))
+            writes[-1].start()
+
+    swaps = swap_halves(gate_w, x_recv, xs, xr, shards)
+    per_shard = model // shards
+    for d in range(model // cols):
+        gate_w[d * cols : (d + 1) * cols, :] = dot(
+            n2[:, d * cols : (d + 1) * cols], gu[:, :width], TN
+        ).astype(BF16)
+        for s in range(shards):
+            if d * cols < (s + 1) * per_shard <= (d + 1) * cols:
+                swaps[s].start()
     gain = gain_ref[...]
     gain_total = None
     for u in range(halves):
@@ -708,8 +717,8 @@
     heads[0] = dot(bg_ref[...], blocks[0][...]).astype(BF16)
     keep = pltpu.make_async_copy(heads.at[0], da_ref.at[pl.ds(mine_at, own)], local.at[0])
     keep.start()
-    product(n2, gu[:, width:], up_w, grads_ref.at[:, pl.ds(0, width)], 1)
-    product(fg, hid[...], down_w, grads_ref.at[:, pl.ds(width, width)], 2)
+    product(n2, gu[:, width:], up_w, [(up_w, up_ref)])
+    product(fg, hid[...], down_w, [(down_w, down_ref)])
     for i in (steps - 2, steps - 1):
         for copy in to_core(i):
             copy.wait_send()
@@ -719,11 +728,21 @@
     for copy in back:
         copy.wait()
     keep.wait()
+    half = per_shard // 2
+    piece = lax.axis_index("ctx")
+    for s in range(shards):
+        swaps[s].wait_recv()
+        here = slice(s * half, (s + 1) * half)
+        gate_ref[here, :] = (
+            gate_w[half_rows(s, piece, half), :].astype(F32) + x_recv[here, :].astype(F32)
+        ).astype(BF16)
+    for copy in swaps:
+        copy.wait_send()
     for copy in writes:
         copy.wait()
 
 
-def feedforward(count, n2, cotangent, middle, gain, weights, blocks, others):
+def feedforward(count, shards, n2, cotangent, middle, gain, weights, blocks, others):
     tokens, model = n2.shape
     own = tokens // count
     hidden = weights.shape[1] // 3
@@ -732,17 +751,18 @@
     vmem, hbm = pl.BlockSpec(memory_space=pltpu.VMEM), pl.BlockSpec(memory_space=pl.ANY)
     sem = pltpu.SemaphoreType.DMA
     return pl.pallas_call(
-        functools.partial(feedforward_kernel, count),
+        functools.partial(feedforward_kernel, count, shards),
         in_specs=[hbm, hbm, hbm, vmem, vmem, hbm] + [vmem] * (count // 2),
-        out_specs=[hbm, vmem, vmem, vmem, hbm, hbm, hbm],
+        out_specs=[hbm, vmem, vmem, vmem, hbm, vmem, hbm, hbm],
         out_shape=[
             jax.ShapeDtypeStruct((steps, rows, model), BF16),
             jax.ShapeDtypeStruct((own, model), F32),
             jax.ShapeDtypeStruct((own, model), BF16),
             jax.ShapeDtypeStruct((1, model), F32),
             jax.ShapeDtypeStruct((tokens, width), BF16),
+            jax.ShapeDtypeStruct((model // 2, hidden), BF16),
             jax.ShapeDtypeStruct((model, hidden), BF16),
-            jax.ShapeDtypeStruct((model, 2 * hidden), BF16),
+            jax.ShapeDtypeStruct((model, hidden), BF16),
         ],
         scratch_shapes=[pltpu.VMEM((model, hidden), BF16)] * 3
         + [
@@ -758,9 +778,11 @@
         + [pltpu.VMEM((2, rows, model), BF16)] * 2
         + [
             pltpu.VMEM((count, own, width), BF16),
-            sem((4,)), sem((2,)), sem((4,)),
+            pltpu.VMEM((model // 2, hidden), BF16),
+            sem((4,)), sem((2,)), sem((3,)),
             sem((2,)), sem((2,)), sem((steps - 2,)), sem((steps - 2,)),
-            sem((2,)), sem((2,)), sem((count,)), sem((count,)), sem((1,)),
+            sem((2,)), sem((2,)), sem((count,)), sem((count,)), sem((shards,)), sem((shards,)),
+            sem((1,)),
         ],
         compiler_params=pltpu.CompilerParams(
             vmem_limit_bytes=63 << 20, collective_id=2, has_side_effects=True
@@ -1060,13 +1082,14 @@
 
 
 def close_kernel(
-    count, shards, dense_ref, w_ref, x_ref, mg_ref, gain_ref, gain_two_ref, grad_ref, gate_ref, *rest
+    count, shards, dense_ref, w_ref, x_ref, mg_ref, gain_ref, gain_two_ref, grad_ref, up_ref, gate_ref, *rest
 ):
     layers, rest = rest[: count // 2], rest[count // 2 :]
     (
-        out_ref, gain_grad_ref, half_ref, lay_ref, gate_out_ref, rows_in, rows_out, sums, c_send, c_recv, y_send,
-        y_recv, x_mine, x_recv, gate_mine, gate_recv, t_send, t_recv, cs, cr, ys, yr, g_send, g_recv, xs, xr, x_sem,
-        ls, lr, lay_sem, ts, tr, gate_sem, local,
+        out_ref, gain_grad_ref, att_ref, lay_ref, up_out_ref, gate_out_ref, rows_in, rows_out, sums, c_send, c_recv, y_send,
+        y_recv, x_mine, x_recv, up_mine, up_recv, gate_mine, gate_recv, l_own, l_send, l_recv, last_send,
+        last_recv, t_send, t_recv, cs, cr, ys, yr, g_send, g_recv, xs, xr, x_sem,
+        ls, lr, lay_sem, ts, tr, up_sem, gate_sem, lines, liner, last_sem, local,
     ) = rest
     ranks = Ranks(count)
     own = rows_in.shape[0]
@@ -1088,6 +1111,7 @@
         )
         for s in range(shards)
     ]
+    keeps.append(pltpu.make_async_copy(up_ref, up_mine, up_sem.at[0]))
     keeps.append(pltpu.make_async_copy(gate_ref, gate_mine, gate_sem.at[0]))
     for copy in keeps:
         copy.start()
@@ -1102,12 +1126,8 @@
     pl.semaphore_signal(barrier, inc=1, device_id={"ctx": 1 - piece}, device_id_type=MESH)
     pl.semaphore_wait(barrier, count + shards - 1)
     swaps = swap_halves(grad_ref, x_recv, xs, xr, shards)
-    swaps.append(
-        pltpu.make_async_remote_copy(
-            src_ref=gate_ref, dst_ref=gate_recv, send_sem=gate_sem.at[1], recv_sem=gate_sem.at[2],
-            device_id={"ctx": 1 - piece}, device_id_type=MESH,
-        )
-    )
+    swaps.append(shard_copy(up_ref, up_recv, up_sem.at[1], up_sem.at[2], "ctx", 1 - piece))
+    swaps.append(shard_copy(gate_ref, gate_recv, gate_sem.at[1], gate_sem.at[2], "ctx", 1 - piece))
     for copy in swaps:
         copy.start()
     forward = both_cores(ranks, layers, lay_ref, ls, lr, lay_sem)
@@ -1188,17 +1208,78 @@
     gain_grad_ref[...] = total
     for copy in sent:
         copy.wait_send()
+    for s in range(shards):
+        keeps[s].wait()
+        swaps[s].wait_recv()
+        here = slice(s * half, (s + 1) * half)
+        l_own[s] = x_mine[here, :].astype(F32) + x_recv[here, :].astype(F32)
+
+    def line(way, s, step):
+        return shard_copy(
+            l_send.at[way, s], l_recv.at[way, s], lines.at[way, s], liner.at[way, s], "fsdp",
+            lax.rem(me + step + shards, shards),
+        )
+
+    def toward(way, s, step, there, follows):
+        @pl.when(there & follows)
+        def _():
+            line(way, s, step).wait_recv()
+            l_send[way, s] = (l_own[s] + l_recv[way, s].astype(F32)).astype(BF16)
+            line(way, s, step).start()
+
+        @pl.when(there & jnp.logical_not(follows))
+        def _():
+            l_send[way, s] = l_own[s].astype(BF16)
+            line(way, s, step).start()
+
+    for d in range(shards - 1):
+        toward(0, shards - 1 - d, 1, me < shards - 1 - d, me > 0)
+        toward(1, d, -1, me > d, me < shards - 1)
     gather.finish()
     for copy in forward:
         copy.wait()
     for s in range(shards):
-        keeps[s].wait()
-        swaps[s].wait_recv()
-        here = slice(s * half, (s + 1) * half)
-        half_ref[here, :] = (x_mine[here, :].astype(F32) + x_recv[here, :].astype(F32)).astype(BF16)
+        @pl.when(me == s)
+        def _():
+            if s > 0:
+                line(0, s, 1).wait_recv()
+                l_own[s] += l_recv[0, s].astype(F32)
+            if s < shards - 1:
+                line(1, s, -1).wait_recv()
+                l_own[s] += l_recv[1, s].astype(F32)
+            last_send[...] = l_own[s].astype(BF16)
+
+    last = shard_copy(last_send, last_recv, last_sem.at[0], last_sem.at[1], "ctx", 1 - piece)
+    last.start()
     keeps[shards].wait()
     swaps[shards].wait_recv()
-    gate_out_ref[...] = gate_mine[...].astype(F32) + gate_recv[...].astype(F32)
+    up_out_ref[...] = up_mine[...].astype(F32) + up_recv[...].astype(F32)
+    keeps[shards + 1].wait()
+    swaps[shards + 1].wait_recv()
+    last.wait_recv()
+    for n, (dst, pair) in enumerate(((gate_out_ref, (gate_mine, gate_recv)), (att_ref, (last_send, last_recv)))):
+        rows_half = pair[0].shape[0]
+
+        @pl.when(piece == 0)
+        def _():
+            dst[:rows_half, :] = pair[0][...].astype(F32)
+            dst[rows_half:, :] = pair[1][...].astype(F32)
+
+        @pl.when(piece == 1)
+        def _():
+            dst[:rows_half, :] = pair[1][...].astype(F32)
+            dst[rows_half:, :] = pair[0][...].astype(F32)
+
+    for d in range(shards - 1):
+        @pl.when(me < shards - 1 - d)
+        def _():
+            line(0, shards - 1 - d, 1).wait_send()
+
+        @pl.when(me > d)
+        def _():
+            line(1, d, -1).wait_send()
+
+    last.wait_send()
     for copy in swaps:
         copy.wait_send()
     for i in range(steps):
@@ -1207,7 +1288,7 @@
         to_chip(i, i // halves + 1).wait_send()
 
 
-def close(count, shards, dense, weight, layer_input, middle_grad, gain, gain_two, grad, gate, layers):
+def close(count, shards, dense, weight, layer_input, middle_grad, gain, gain_two, grad, up, gate, layers):
     tokens, model = layer_input.shape
     own = tokens // count
     rows, steps, chips = own // 2, count, count // 2
@@ -1215,14 +1296,15 @@
     sem = pltpu.SemaphoreType.DMA
     return pl.pallas_call(
         functools.partial(close_kernel, count, shards),
-        in_specs=[vmem, vmem, hbm, vmem, vmem, vmem, hbm, hbm] + [hbm] * chips,
-        out_specs=[hbm, vmem, vmem, hbm, vmem],
+        in_specs=[vmem, vmem, hbm, vmem, vmem, vmem, hbm, hbm, hbm] + [hbm] * chips,
+        out_specs=[hbm, vmem, vmem, hbm, vmem, vmem],
         out_shape=[
             jax.ShapeDtypeStruct((tokens, model), BF16),
             jax.ShapeDtypeStruct((8, model), F32),
-            jax.ShapeDtypeStruct((model // 2, grad.shape[1]), BF16),
+            jax.ShapeDtypeStruct((model // shards, grad.shape[1]), F32),
             jax.ShapeDtypeStruct((tokens, model), BF16),
-            jax.ShapeDtypeStruct(gate.shape, F32),
+            jax.ShapeDtypeStruct(up.shape, F32),
+            jax.ShapeDtypeStruct(up.shape, F32),
         ],
         scratch_shapes=[
             pltpu.VMEM((own, model), F32),
@@ -1233,14 +1315,22 @@
         + [pltpu.VMEM((steps - 2, rows, model), BF16)] * 2
         + [pltpu.VMEM((model // 2, grad.shape[1]), BF16)] * 2
         + [
+            pltpu.VMEM(up.shape, BF16),
+            pltpu.VMEM(up.shape, BF16),
             pltpu.VMEM(gate.shape, BF16),
             pltpu.VMEM(gate.shape, BF16),
+            pltpu.VMEM((shards, gate.shape[0], grad.shape[1]), F32),
+            pltpu.VMEM((2, shards, gate.shape[0], grad.shape[1]), BF16),
+            pltpu.VMEM((2, shards, gate.shape[0], grad.shape[1]), BF16),
+            pltpu.VMEM((gate.shape[0], grad.shape[1]), BF16),
+            pltpu.VMEM((gate.shape[0], grad.shape[1]), BF16),
             pltpu.VMEM((4, 8, model), F32),
             pltpu.VMEM((chips + shards, 8, model), F32),
             sem((steps,)), sem((steps,)), sem((steps - 2,)), sem((steps - 2,)),
             sem((2, chips)), sem((2, chips)), sem((shards,)), sem((shards,)), sem((shards,)),
             sem((chips,)), sem((chips,)), sem((chips,)), sem((chips + shards,)),
-            sem((chips + shards,)), sem((3,)), sem((2,)),
+            sem((chips + shards,)), sem((3,)), sem((3,)), sem((2, shards)), sem((2, shards)), sem((2,)),
+            sem((2,)),
         ],
         compiler_params=pltpu.CompilerParams(
             vmem_limit_bytes=48 << 20, collective_id=3, has_side_effects=True
@@ -1249,7 +1339,7 @@
             flops=2 * tokens * model * dense.shape[1], bytes_accessed=200 << 20, transcendentals=0
         ),
         name="close_layer",
-    )(dense, weight, layer_input, middle_grad, gain, gain_two, grad, gate, *layers)
+    )(dense, weight, layer_input, middle_grad, gain, gain_two, grad, up, gate, *layers)
 
 
 def per_device(
@@ -1306,13 +1396,6 @@
     def add_pieces(mine):
         return mine.astype(F32) + lax.ppermute(mine, "ctx", swap_x).astype(F32)
 
-    def whole_shard(mine):
-        other = lax.ppermute(mine, "ctx", swap_x)
-        pair = jnp.where(
-            piece == 0, jnp.concatenate([mine, other], 0), jnp.concatenate([other, mine], 0)
-        )
-        return pair.astype(F32)
-
     ff_half = half_of(jnp.concatenate([gate_weight, up_weight, down_weight.T], axis=1))
     gain_shard = jnp.stack([attention_gain, feedforward_gain]).astype(F32)
     gain_shard = jnp.pad(gain_shard, ((0, 6), (0, 0)))
@@ -1349,11 +1432,13 @@
     wo = [out_own] + [lax.ppermute(out_own, "tp", chip_shift(k)) for k in range(1, chips)]
     normed_two, middle, wo_others = mix(ranks, attended, layer_input, gain_two, wo)
     (
-        feed_sums, middle_grad, branch_grad, gain_two_grad, attended_grad, gate_part, feed_part,
+        feed_sums, middle_grad, branch_grad, gain_two_grad, attended_grad, gate_half, up_part, down_part,
     ) = feedforward(
-        ranks, normed_two, output_cotangent, middle, gain_two, ff_full, wo, wo_others
+        ranks, shards, normed_two, output_cotangent, middle, gain_two, ff_full, wo, wo_others
     )
-    gate_own, feed_own = reduce_fsdp(gate_part), reduce_fsdp(feed_part)
+    gate_own = reduce_fsdp(gate_half)
+    up_own = reduce_fsdp(up_part)
+    down_own = reduce_fsdp(down_part)
     cut = feed_sums.reshape(chips, own, model)
     feed_sums = [lax.ppermute(cut[k - 1], "tp", chip_shift(k)) for k in range(1, chips)]
     dq_part, dkv_before = attention_backward(
@@ -1377,15 +1462,13 @@
     dqkv, attention_part = dense_gradients(
         dq, dkv, after, cos, sin, rot_k, val_k, attended, normed_one, from_chips(branch_grad)
     )
-    input_gradient, gains, attention_half, layer_output, gate = close(
+    input_gradient, gains, attention, layer_output, up, gate = close(
         ranks, shards, dqkv, qkv_full, layer_input, middle_grad, gain_one, gain_two_grad,
-        attention_part, gate_own, from_chips(layer_rows),
+        attention_part, up_own, gate_own, from_chips(layer_rows),
     )
-    attention_half, feed_own = lax.optimization_barrier((attention_half, feed_own))
-    attention = whole_shard(reduce_fsdp(attention_half))
-    feed = add_pieces(feed_own)
+    down_own, gains = lax.optimization_barrier((down_own, gains))
+    down = add_pieces(down_own)
     layer_output, input_gradient = layer_output.astype(F32), input_gradient.astype(F32)
-    ff_width = gate_weight.shape[1]
     gains = lax.dynamic_slice_in_dim(gains, me * gain_shard.shape[1], gain_shard.shape[1], 1)
 
     return (
@@ -1398,8 +1481,8 @@
         attention[:, q_width + 2 * kv_width :].T,
         gains[1],
         gate,
-        feed[:, :ff_width],
-        feed[:, ff_width:].T,
+        up,
+        down.T,
     )
 
 

time: 526 us -> 566 us (1.076)
  Pallas kernels: 330 us -> 381 us
  waiting for transfers between devices: 102 us -> 86.1 us
    pallas_call x1, Pallas kernels: 93.8 us -> 131 us  [close(): pl.pallas_call(functools.partial(close_kernel, count, shards), in_specs=[...]
    pallas_call x1, Pallas kernels: 79.1 us -> 92.1 us  [feedforward(): pl.pallas_call(functools.partial(feedforward_kernel, count, shards), in_s...]
    reduce_scatter x3, waiting for transfers between devices: 26 us -> 13.8 us  [reduce_fsdp(): return lax.psum_scatter(part, 'fsdp', scatter_dimension=0, tiled=True)]
    unnamed x79 -> x82, local copies, waits for them, and re-layouts: 27.3 us -> 31.9 us
  transfers between devices with their start and end apart: 12 -> 11, of which waited for: 6 -> 5; matrix products, arithmetic and copies ran while one was open for 6% -> 5% of each run, Pallas kernels for 40% -> 44%
where the time goes in v2:
time: 566 us; the launch traced here: 557 us
  Pallas kernels  381 us (67%)
  waiting for transfers between devices  86.1 us (15%)
  local copies, waits for them, and re-layouts  39.3 us (7%)
  other arithmetic  25.6 us (5%)
  between operations  14.7 us (3%)
  starting transfers between devices  11.1 us (2%)
    pallas_call x1, Pallas kernels, close(): pl.pallas_call(functools.partial(close_kernel, count, shards), in_specs=[...  131 us
    pallas_call x1, Pallas kernels, feedforward(): pl.pallas_call(functools.partial(feedforward_kernel, count, shards), in_s...  92.1 us
    pallas_call x1, Pallas kernels, mix(): pl.pallas_call(functools.partial(mix_kernel, count), in_specs=[hbm, hbm,...  48 us
    pallas_call x1, Pallas kernels, begin(): pl.pallas_call(functools.partial(begin_kernel, shards), in_specs=[hbm, vm...  44.7 us
    unnamed x82, local copies, waits for them, and re-layouts  31.9 us
    pallas_call x2, Pallas kernels, attention_backward(): pl.pallas_call(functools.partial(attention_backward_kernel, rest is None,...  28.5 us
    ppermute x2, waiting for transfers between devices, from_chips(): lax.ppermute(rows, 'tp', chip_shift(k))  27.7 us
    all_gather x1, waiting for transfers between devices, per_device(): ff_full = lax.all_gather(ff_half, both_axes, axis=0, tiled=True)  22.1 us
  transfers between devices with their start and end apart: 11, of which 5 were waited for; matrix products, arithmetic and copies ran while one was open for 5% of the time, Pallas kernels for 44%

profile of v2, /device:TPU:0, one launch (start us, length us, event | category | flops | bytes accessed | tf_op | source)
XLA Modules:
  0.0 557.4 jit_solution(5272983471308204184)
XLA Ops:
  13.3 44.7 %norm_and_gather.1 = (bf16[1536,1536]{1,0:T(8,128)(2,1)}, bf16[1536,768]{1,0:T(8,128)(2,1)S(1)}, bf16[1536,384]{1,0:T(8,128)(2,1)S(1)}, f32[8,1536]{1,0:T(8,128)S(1)}) custom-call(f32[1536,1536]{1,0:T(8,128)} %x_ref.5, bf16[384,768]{1,0:T(8,128)(2,1)S(1)} %pad_maximum_fusion.4.qkv_ref, bf16[384,384]{1,0:T(8,128)(2,1)S(1)} %bitcast.17, ...), custom_call_target="tpu_custom_call" | custom-call | bytes 125829120 | tf_op jit(solution)/shard_map/norm_and_gather/pallas_call | solution.py:940
  62.8 2.8 fusion.20
  66.6 3.0 copy-done.13
  69.6 9.0 %project_qkv.1 = (bf16[1536,512]{1,0:T(8,128)(2,1)S(1)}, bf16[1536,512]{1,0:T(8,128)(2,1)S(1)}) custom-call(bf16[1536,1536]{1,0:T(8,128)(2,1)S(1)} %copy-done.13, bf16[1536,768]{1,0:T(8,128)(2,1)S(1)} %get-tuple-element.87.qkv_ref.w_ref, bf16[768,1024]{1,0:T(8,128)(2,1)S(1)} %fusion.27.spread_ref, f32[1536,128]{1,0:T(8,128)S(1)} %get-tuple-element.156.cos_ref.rest_1_, ...), custom_call_target="tpu_custom_call" | custom-call | flops 4831838208 | bytes 16777216 | tf_op jit(solution)/shard_map/project_qkv/pallas_call | solution.py:997
  78.7 2.9 collective-permute-start
  84.2 9.1 %attention_forward.2 = (f32[3,2,1,1024]{3,2,1,0:T(1,128)S(1)}, f32[3,2,128,1024]{3,2,1,0:T(8,128)S(1)}) custom-call(s32[3]{0:T(128)S(1)} %get-tuple-element.169.ends_ref, s32[1]{0:T(128)} %bitcast.2.base_ref, bf16[1536,512]{1,0:T(8,128)(2,1)S(1)} %get-tuple-element.88.q_ref, bf16[1536,512]{1,0:T(8,128)(2,1)S(1)} %get-tuple-element.89.kv_ref), custom_call_target="tpu_custom_call" | custom-call | flops 4831838208 | bytes 8388608 | tf_op jit(solution)/shard_map/attention_forward/pallas_call | solution.py:195
  93.3 21.3 %collective-permute-done.kv_ref = bf16[1536,512]{1,0:T(8,128)(2,1)S(1)} collective-permute-done((bf16[1536,512]{1,0:T(8,128)(2,1)S(1)}, bf16[1536,512]{1,0:T(8,128)(2,1)S(1)}, u32[]{:S(2)}, u32[]{:S(2)}) %collective-permute-start) | collective-permute-done | bytes 1572896 | tf_op jit(solution)/shard_map/ppermute | solution.py:1424
  114.7 4.4 attention_forward.3
  120.2 48.0 %mix_heads.1 = (bf16[1536,1536]{1,0:T(8,128)(2,1)S(1)}, f32[384,1536]{1,0:T(8,128)S(1)}, bf16[2,1536,384]{2,1,0:T(8,128)(2,1)S(1)}) custom-call(bf16[1536,384]{1,0:T(8,128)(2,1)S(1)} %get-tuple-element.92.att_ref.o_ref, f32[1536,1536]{1,0:T(8,128)} %x_ref.5, f32[1,1536]{1,0:T(1,128)S(1)} %get-tuple-element.158.gain_ref, bf16[1536,384]{1,0:T(8,128)(2,1)S(1)} %copy-done.17, ...), custom_call_target="tpu_custom_call" | custom-call | flops 7247757312 | bytes 157286400 | tf_op jit(solution)/shard_map/mix_heads/pallas_call | solution.py:480
  175.2 22.1 %all-gather.2.cloned.1.call-done.weight_ref = bf16[1536,3072]{1,0:T(8,128)(2,1)} async-done(((bf16[192,3072]{1,0:T(8,128)(2,1)}), bf16[1536,3072]{1,0:T(8,128)(2,1)}) %all-gather.2.cloned.1.call-update) | async-done | bytes 9437200 | tf_op jit(solution)/shard_map/all_gather | solution.py:1422
  197.3 92.1 %feed_forward.1 = (bf16[4,192,1536]{2,1,0:T(8,128)(2,1)}, f32[384,1536]{1,0:T(8,128)}, bf16[384,1536]{1,0:T(8,128)(2,1)}, f32[1,1536]{1,0:T(1,128)}, bf16[1536,3...) custom-call(bf16[1536,1536]{1,0:T(8,128)(2,1)} %copy-done.22, ...), custom_call_target="tpu_custom_call" | custom-call | flops 43486543872 | bytes 293601280 | tf_op jit(solution)/shard_map/feed_forward/pallas_call | solution.py:753
  290.8 3.0 fusion.40
  295.4 5.0 attention_backward.2
  302.5 23.6 %attention_backward.3 = (bf16[1536,384]{1,0:T(8,128)(2,1)S(1)}, f32[1536,512]{1,0:T(8,128)}) custom-call(s32[3]{0:T(128)S(1)} %get-tuple-element.169.ends_ref, s32[1]{0:T(128)} %bitcast.2.base_ref, bf16[1536,512]{1,0:T(8,128)(2,1)} %copy-done.23, bf16[1536,384]{1,0:T(8,128)(2,1)S(1)} %copy-done.26, bf16[1536,384]{1,0:T(8,128)(2,1)S(1)} %copy-done.21, ...), custom_call_target="tpu_custom_call" | custom-call | flops 12079595520 | bytes 12582912 | tf_op jit(solution)/shard_map/attention_backward/pallas_call | solution.py:315
  330.2 18.2 %collective-permute-done.4.rest_1_ = bf16[384,1536]{1,0:T(8,128)(2,1)} collective-permute-done((bf16[384,1536]{1,0:T(8,128)(2,1)S(1)}, bf16[384,1536]{1,0:T(8,128)(2,1)}, u32[]{:S(2)}, u32[]{:S(2)}) %collective-permute-start.4) | collective-permute-done | bytes 1179680 | tf_op jit(solution)/shard_map/ppermute | solution.py:1460
  348.3 13.4 %dense_gradients.1 = (bf16[1536,768]{1,0:T(8,128)(2,1)}, bf16[1536,1152]{1,0:T(8,128)(2,1)}) custom-call(bf16[1536,384]{1,0:T(8,128)(2,1)S(1)} %get-tuple-element.105.dq_ref, f32[1536,512]{1,0:T(8,128)} %get-tuple-element.106.dkv_ref, bf16[1536,512]{1,0:T(8,128)(2,1)} %collective-permute-done.3.after_ref, f32[1536,128]{1,0:T(8,128)S(1)} %copy-done.7, ...), custom_call_target="tpu_custom_call" | custom-call | flops 5435817984 | bytes 25165824 | tf_op jit(solution)/shard_map/dense_gradients/pallas_call | solution.py:1061
  361.8 9.5 %collective-permute-done.5.rest_1_ = bf16[384,1536]{1,0:T(8,128)(2,1)S(1)} collective-permute-done((bf16[384,1536]{1,0:T(8,128)(2,1)S(1)}, bf16[384,1536]{1,0:T(8,128)(2,1)S(1)}, u32[]{:S(2)}, u32[]{:S(2)}) %collective-permute-start.5) | collective-permute-done | bytes 1179680 | tf_op jit(solution)/shard_map/ppermute | solution.py:1460
  372.3 13.8 %reduce-scatter.4.cloned.1.call-done.up_ref = bf16[384,1024]{1,0:T(8,128)(2,1)} async-done(((bf16[1536,1024]{1,0:T(8,128)(2,1)}), bf16[384,1024]{1,0:T(8,128)(2,1)}) %reduce-scatter.4.cloned.1.call-update) | async-done | bytes 786448 | tf_op jit(solution)/shard_map/reduce_scatter | solution.py:1394
  389.5 131.4 %close_layer.1 = (bf16[1536,1536]{1,0:T(8,128)(2,1)}, f32[8,1536]{1,0:T(8,128)S(1)}, f32[384,1152]{1,0:T(8,128)}, bf16[1536,1536]{1,0:T(8,128)(2,1)}, f32[384,1024]{1,0:T(8,128)S(1)}, /*index=5*/f32[384,1024]{1,0:T(8,128)}) custom-call(bf16[1536,768]{1,0:T(8,128)(2,1)} %get-tuple-element.109.dense_ref, bf16[1536,768]{1,0:T(8,128)(2,1)} %copy-done, ...), custom_call_target="tpu_custom_call" | custom-call | flops 3623878656 | bytes 209715200 | tf_op jit(solution)/shard_map/close_layer/pallas_call | solution.py:1297
  522.4 7.6 %convert_element_type.70 = f32[1536,1536]{1,0:T(8,128)} convert(bf16[1536,1536]{1,0:T(8,128)(2,1)} %get-tuple-element.116) | non-fusion elementwise | flops 2359296 | bytes 14155776 | tf_op jit(solution)/shard_map/convert_element_type | solution.py:1471
  530.0 5.1 convert_element_type.71
  540.8 2.8 add_bitcast_fusion
  543.6 3.0 copy.38
  546.6 2.7 copy.43
  (131 shorter events, 44.3 us)
Async XLA Ops:
  7.2 190.1 %all-gather.2.cloned.1.call-start = ((), (), s32[]{:S(2)}) async-start(), calls=%async_computation.3 | async-start | bytes 10616832 | tf_op jit(solution)/shard_map/all_gather | solution.py:1422
  13.3 45.8 %copy-start.28 = (bf16[1024,384]{0,1:T(8,128)(2,1)S(1)}, bf16[1024,384]{0,1:T(8,128)(2,1)}, u32[]{:S(2)}) copy-start(bf16[1024,384]{0,1:T(8,128)(2,1)} %copy.34) | copy-start | bytes 2359300
  13.3 45.8 %copy-start.32 = (bf16[384,1024]{1,0:T(8,128)(2,1)S(1)}, bf16[384,1024]{1,0:T(8,128)(2,1)}, u32[]{:S(2)}) copy-start(bf16[384,1024]{1,0:T(8,128)(2,1)} %param.26) | copy-start | bytes 2359300
  13.3 45.8 %copy-start.33 = (bf16[384,1024]{1,0:T(8,128)(2,1)S(1)}, bf16[384,1024]{1,0:T(8,128)(2,1)}, u32[]{:S(2)}) copy-start(bf16[384,1024]{1,0:T(8,128)(2,1)} %param.27) | copy-start | bytes 2359300
  59.1 7.5 %copy-start = (bf16[1536,768]{1,0:T(8,128)(2,1)}, bf16[1536,768]{1,0:T(8,128)(2,1)S(1)}, u32[]{:S(2)}) copy-start(bf16[1536,768]{1,0:T(8,128)(2,1)S(1)} %get-tuple-element.87.qkv_ref.w_ref) | copy-start | bytes 7077892
  60.4 311.9 %reduce-scatter.6.cloned.1.call-start = ((), (), s32[]{:S(2)}) async-start(), calls=%async_computation.5 | async-start | bytes 1966080 | tf_op jit(solution)/shard_map/reduce_scatter | solution.py:1394
  66.6 12.0 %copy-start.6 = (f32[1536,128]{1,0:T(8,128)}, f32[1536,128]{1,0:T(8,128)S(1)}, u32[]{:S(2)}) copy-start(f32[1536,128]{1,0:T(8,128)S(1)} %get-tuple-element.156.cos_ref.rest_1_) | copy-start | bytes 2359300
  69.6 12.0 %copy-start.17 = (bf16[1536,384]{1,0:T(8,128)(2,1)S(1)}, bf16[1536,384]{1,0:T(8,128)(2,1)}, u32[]{:S(2)}) copy-start(bf16[1536,384]{1,0:T(8,128)(2,1)} %copy-done.16) | copy-start | bytes 3538948
  78.6 14.7 %copy-start.14 = (bf16[1536,512]{1,0:T(8,128)(2,1)}, bf16[1536,512]{1,0:T(8,128)(2,1)S(1)}, u32[]{:S(2)}) copy-start(bf16[1536,512]{1,0:T(8,128)(2,1)S(1)} %get-tuple-element.89.kv_ref) | copy-start | bytes 4718596
  78.7 36.0 %collective-permute-start = (bf16[1536,512]{1,0:T(8,128)(2,1)S(1)}, bf16[1536,512]{1,0:T(8,128)(2,1)S(1)}, u32[]{:S(2)}, u32[]{:S(2)}) collective-permute-start(bf16[1536,512]{1,0:T(8,128)(2,1)S(1)} %get-tuple-element.89.kv_ref), channel_id=1, source_target_pairs={{0,4},{1,5},{2,6},{3,7},{8,12},{9,13},{10,14},{11,15},{16,20},{17,... | collective-permute-start | bytes 4718600 | tf_op jit(solution)/shard_map/ppermute | solution.py:1424
  81.6 38.6 %collective-permute-start.1 = (bf16[1536,384]{1,0:T(8,128)(2,1)S(1)}, bf16[1536,384]{1,0:T(8,128)(2,1)S(1)}, u32[]{:S(2)}, u32[]{:S(2)}) collective-permute-start(bf16[1536,384]{1,0:T(8,128)(2,1)S(1)} %copy-done.17), channel_id=1, source_target_pairs={{0,2},{1,3},{2,0},{3,1},{4,6},{5,7},{6,4},{7,5},{8,10},{9,11},{10,... | collective-permute-start | bytes 3538952 | tf_op jit(solution)/shard_map/ppermute | solution.py:1432
  83.2 37.0 %copy-start.12 = (f32[1,1536]{1,0:T(1,128)}, f32[1,1536]{1,0:T(1,128)S(1)}, u32[]{:S(2)}) copy-start(f32[1,1536]{1,0:T(1,128)S(1)} %get-tuple-element.158.gain_ref) | copy-start | bytes 18436
  289.5 96.6 %reduce-scatter.4.cloned.1.call-start = ((), (), s32[]{:S(2)}) async-start(), calls=%async_computation.4 | async-start | bytes 3932160 | tf_op jit(solution)/shard_map/reduce_scatter | solution.py:1394
  290.2 230.7 %reduce-scatter.8.cloned.1.call-start = ((), (), s32[]{:S(2)}) async-start(), calls=%async_computation.6 | async-start | bytes 3932160 | tf_op jit(solution)/shard_map/reduce_scatter | solution.py:1394
  293.8 32.3 %collective-permute-start.2 = (bf16[384,1536]{1,0:T(8,128)(2,1)}, bf16[384,1536]{1,0:T(8,128)(2,1)S(1)}, u32[]{:S(2)}, u32[]{:S(2)}) collective-permute-start(bf16[384,1536]{1,0:T(8,128)(2,1)} %bitcast.6), channel_id=1, source_target_pairs={{0,2},{1,3},{2,0},{3,1},{4,6},{5,7},{6,4},{7,5},{8,10},{9,11},{10,... | collective-permute-start | bytes 3538952 | tf_op jit(solution)/shard_map/ppermute | solution.py:1443
  295.3 7.2 %copy-start.7 = (f32[1536,128]{1,0:T(8,128)S(1)}, f32[1536,128]{1,0:T(8,128)}, u32[]{:S(2)}) copy-start(f32[1536,128]{1,0:T(8,128)} %copy-done.6) | copy-start | bytes 2359300
  295.3 7.2 %copy-start.9 = (bf16[512,384]{1,0:T(8,128)(2,1)S(1)}, bf16[512,384]{1,0:T(8,128)(2,1)}, u32[]{:S(2)}) copy-start(bf16[512,384]{1,0:T(8,128)(2,1)} %get-tuple-element.159.rest_3_) | copy-start | bytes 1179652
  300.3 48.0 %collective-permute-start.3 = (bf16[1536,512]{1,0:T(8,128)(2,1)S(1)}, bf16[1536,512]{1,0:T(8,128)(2,1)}, u32[]{:S(2)}, u32[]{:S(2)}) collective-permute-start(bf16[1536,512]{1,0:T(8,128)(2,1)S(1)} %get-tuple-element.107), channel_id=1, source_target_pairs={{4,0},{5,1},{6,2},{7,3},{12,8},{13,9},{14,10},{15,11},{20,16},{21,... | collective-permute-start | bytes 4718600 | tf_op jit(solution)/shard_map/ppermute | solution.py:1447
  301.6 46.7 %collective-permute-start.4 = (bf16[384,1536]{1,0:T(8,128)(2,1)S(1)}, bf16[384,1536]{1,0:T(8,128)(2,1)}, u32[]{:S(2)}, u32[]{:S(2)}) collective-permute-start(bf16[384,1536]{1,0:T(8,128)(2,1)S(1)} %copy-done.18), channel_id=1, source_target_pairs={{0,2},{1,3},{2,0},{3,1},{4,6},{5,7},{6,4},{7,5},{8,10},{9,11},{10,... | collective-permute-start | bytes 3538952 | tf_op jit(solution)/shard_map/ppermute | solution.py:1460
  302.5 24.6 %copy-start.2 = (f32[384,1536]{1,0:T(8,128)S(1)}, f32[384,1536]{1,0:T(8,128)}, u32[]{:S(2)}) copy-start(f32[384,1536]{1,0:T(8,128)} %copy-done.1) | copy-start | bytes 7077892
  328.9 42.4 %collective-permute-start.5 = (bf16[384,1536]{1,0:T(8,128)(2,1)S(1)}, bf16[384,1536]{1,0:T(8,128)(2,1)S(1)}, u32[]{:S(2)}, u32[]{:S(2)}) collective-permute-start(bf16[384,1536]{1,0:T(8,128)(2,1)S(1)} %fusion.1.rest_0_), channel_id=1, source_target_pairs={{0,2},{1,3},{2,0},{3,1},{4,6},{5,7},{6,4},{7,5},{8,10},{9,11},{10,... | collective-permute-start | bytes 3538952 | tf_op jit(solution)/shard_map/ppermute | solution.py:1460
  348.3 37.7 %copy-start.11 = (f32[1,1536]{1,0:T(1,128)S(1)}, f32[1,1536]{1,0:T(1,128)}, u32[]{:S(2)}) copy-start(f32[1,1536]{1,0:T(1,128)} %get-tuple-element.111.gain_two_ref) | copy-start | bytes 18436
  520.9 19.9 %collective-permute-start.6 = (bf16[384,1024]{1,0:T(8,128)(2,1)}, bf16[384,1024]{1,0:T(8,128)(2,1)}, u32[]{:S(2)}, u32[]{:S(2)}) collective-permute-start(bf16[384,1024]{1,0:T(8,128)(2,1)} %reduce-scatter.8.cloned.1.call-done), channel_id=1, source_target_pairs={{0,4},{4,0},{1,5},{5,1},{2,6},{6,2},{3,7},{7,3},{8,12},{12,8},{9,1... | collective-permute-start | bytes 2359304 | tf_op jit(solution)/shard_map/ppermute | solution.py:1397
  522.4 7.6 %copy-start.27 = (bf16[1536,1536]{1,0:T(8,128)(2,1)S(1)}, bf16[1536,1536]{1,0:T(8,128)(2,1)}, u32[]{:S(2)}) copy-start(bf16[1536,1536]{1,0:T(8,128)(2,1)} %get-tuple-element.117) | copy-start | bytes 14155780
  (23 other events, 63.6 us)
Sparse Core Ops, SparseCore 0:
  60.5 136.7 all-gather.1
  289.6 34.8 reduce-scatter.5
  326.8 59.2 reduce-scatter.3
  388.2 60.2 reduce-scatter.7

commit v3 on v1

--- a/solution.py
+++ b/solution.py
@@ -3,6 +3,8 @@
 
 import jax
 import jax.numpy as jnp
+import ml_dtypes
+import numpy as np
 from jax import lax
 from jax.experimental import pallas as pl
 from jax.experimental.pallas import tpu as pltpu
@@ -26,20 +28,20 @@
 
 
 def select_rotary(heads, head_dim):
-    shape = (heads * LANES, heads * head_dim)
-    row = lax.broadcasted_iota(jnp.int32, shape, 0)
-    col = lax.broadcasted_iota(jnp.int32, shape, 1)
+    col = np.arange(heads * head_dim)
     half = head_dim // 2
     within = col % head_dim
-    want = (col // head_dim) * LANES + jnp.where(within < half, within, within - half + LANES // 2)
-    return (row == want).astype(BF16)
+    lane = np.where(within < half, within, within - half + LANES // 2)
+    return select_lanes(heads, (col // head_dim) * LANES + lane)
 
 
 def select_value(heads, head_dim):
-    shape = (heads * LANES, heads * head_dim)
-    row = lax.broadcasted_iota(jnp.int32, shape, 0)
-    col = lax.broadcasted_iota(jnp.int32, shape, 1)
-    return (row == (col // head_dim) * LANES + col % head_dim).astype(BF16)
+    col = np.arange(heads * head_dim)
+    return select_lanes(heads, (col // head_dim) * LANES + col % head_dim)
+
+
+def select_lanes(heads, want):
+    return (np.arange(heads * LANES)[:, None] == want[None, :]).astype(ml_dtypes.bfloat16)
 
 
 def rotary_lanes(positions, head_dim):
@@ -103,13 +105,23 @@
     return jnp.concatenate([rows] * group, axis=1), jnp.concatenate([starts] * group, axis=1)
 
 
+def widen(dense_ref, spread_ref, mark_ref, wide_ref):
+    @pl.when(pl.program_id(0) == 0)
+    def _():
+        wide = dot(dense_ref[...], spread_ref[...]) + mark_ref[...]
+        wide_ref[...] = wide.astype(BF16)
+
+    return wide_ref
+
+
 def attention_forward_kernel(
     first, key_base, tokens, bq, bk, head_dim, group, ends_ref, base_ref, q_ref, kv_ref, *rest
 ):
     if first:
         max_ref, acc_ref = rest
     else:
-        sel_ref, max_in, acc_in, o_ref, qa_ref, max_ref, acc_ref = rest
+        spread_ref, mark_ref, sel_ref, max_in, acc_in, o_ref, qa_ref, max_ref, acc_ref, wide = rest
+        kv_ref = widen(kv_ref, spread_ref, mark_ref, wide)
     first_row = tokens + pl.program_id(0) * bq
     base = base_ref[0]
     low = doc_start(ends_ref, base, first_row)
@@ -169,9 +181,9 @@
     o_ref[...] = dot(jnp.concatenate(outs, axis=1), sel_ref[...]).astype(BF16)
 
 
-def attention_forward(ends, base, q, kv, head_dim, key_base, state=None, select=None):
+def attention_forward(ends, base, q, kv, head_dim, key_base, state=None, extra=None):
     tokens, width = q.shape
-    kv_heads = kv.shape[1] // LANES // 2
+    kv_heads = (kv if state is None else extra[0]).shape[1] // LANES // 2
     group = width // LANES // kv_heads
     bq = bk = math.gcd(tokens, 512)
     steps = tokens // bq
@@ -185,13 +197,16 @@
         out_specs, out_shape = kept, [jax.ShapeDtypeStruct(a, F32) for a in shapes]
         scratch = []
     else:
-        in_specs, operands = [row(width), whole(kv), whole(select)] + kept, (q, kv, select) + tuple(state)
+        select = extra[2]
+        in_specs = [row(width), whole(kv)] + [whole(a) for a in extra] + kept
+        operands = (q, kv) + tuple(extra) + tuple(state)
         out_specs = [row(select.shape[1]), row(width)]
         out_shape = [
             jax.ShapeDtypeStruct((tokens, select.shape[1]), BF16),
             jax.ShapeDtypeStruct(q.shape, BF16),
         ]
         scratch = [pltpu.VMEM((1,) + a[1:], F32) for a in shapes]
+        scratch.append(pltpu.VMEM((tokens, extra[0].shape[1]), BF16))
     return pl.pallas_call(
         functools.partial(
             attention_forward_kernel, state is None, key_base, tokens, bq, bk, head_dim, group
@@ -214,7 +229,8 @@
     ends_ref, base_ref, qa_ref, do_ref, o_ref, kv_ref, spread_ref, *rest
 ):
     if first:
-        dq_ref, dkv_ref, dk_acc, dv_acc, dq_acc = rest
+        widen_ref, mark_ref, dq_ref, dkv_ref, dk_acc, dv_acc, dq_acc, wide = rest
+        kv_ref = widen(kv_ref, widen_ref, mark_ref, wide)
     else:
         part_ref, cos_ref, sin_ref, sel_ref, dq_ref, dkv_ref, dk_acc, dv_acc, dq_acc = rest
     step = pl.program_id(0)
@@ -294,10 +310,11 @@
             dkv_ref[:, (kv_heads + h) * LANES : (kv_heads + h + 1) * LANES] = dv_acc[h].astype(dkv_ref.dtype)
 
 
-def attention_backward(ends, base, qa, grad, out, kv, spread, head_dim, key_base, rest=None):
+def attention_backward(ends, base, qa, grad, out, kv, spread, head_dim, key_base, rest=None, extra=None):
     tokens, width = qa.shape
     keys = kv.shape[0]
-    kv_heads = kv.shape[1] // LANES // 2
+    kv_lanes = (kv if rest is not None else extra[0]).shape[1]
+    kv_heads = kv_lanes // LANES // 2
     group = width // LANES // kv_heads
     bq = bk = math.gcd(tokens, 512)
     whole = lambda a: pl.BlockSpec(a.shape, lambda i, *_: (0, 0))
@@ -305,7 +322,11 @@
     pairs = tokens * tokens * group * kv_heads // 2
     in_specs = [row(width), row(grad.shape[1]), row(out.shape[1]), whole(kv), whole(spread)]
     operands = (qa, grad, out, kv, spread)
+    scratch = []
     if rest is None:
+        in_specs += [whole(a) for a in extra]
+        operands += tuple(extra)
+        scratch = [pltpu.VMEM((keys, kv_lanes), BF16)]
         dq_width, dq_type, dkv_type = width, F32, BF16
     else:
         part, cos, sin, select = rest
@@ -320,16 +341,17 @@
             num_scalar_prefetch=2,
             grid=(tokens // bq,),
             in_specs=in_specs,
-            out_specs=[row(dq_width), whole(kv)],
+            out_specs=[row(dq_width), pl.BlockSpec((keys, kv_lanes), lambda i, *_: (0, 0))],
             scratch_shapes=[
                 pltpu.VMEM((kv_heads, keys, LANES), F32),
                 pltpu.VMEM((kv_heads, keys, LANES), F32),
                 pltpu.VMEM((kv_heads, group * bq, LANES), F32),
-            ],
+            ]
+            + scratch,
         ),
         out_shape=[
             jax.ShapeDtypeStruct((tokens, dq_width), dq_type),
-            jax.ShapeDtypeStruct(kv.shape, dkv_type),
+            jax.ShapeDtypeStruct((keys, kv_lanes), dkv_type),
         ],
         compiler_params=pltpu.CompilerParams(vmem_limit_bytes=48 << 20),
         cost_estimate=pl.CostEstimate(
@@ -415,12 +437,12 @@
     return copies
 
 
-def mix_kernel(count, att_ref, x_ref, gain_ref, *rest):
+def mix_kernel(count, shards, att_ref, x_ref, gain_ref, z_ref, *rest):
     chips = count // 2
     blocks, rest = rest[:chips], rest[chips:]
     (
-        n2_ref, mid_ref, other_ref, heads, rows_in, rows_out, others, a_send, a_recv, b_send, b_recv,
-        g_send, g_recv, local,
+        n2_ref, mid_ref, other_ref, z_full_ref, heads, rows_in, rows_out, others, a_send, a_recv,
+        b_send, b_recv, g_send, g_recv, z_send, z_recv, x_send, x_recv, local,
     ) = rest
     ranks = Ranks(count)
     own = rows_in.shape[0]
@@ -429,7 +451,56 @@
     fetch.start()
     mine = pltpu.make_async_copy(att_ref.at[mine_at], heads.at[0], local.at[1])
     mine.start()
-    ranks.barrier()
+    me = lax.axis_index("fsdp")
+    barrier = pltpu.get_barrier_semaphore()
+    for k, j in ranks.others():
+        pl.semaphore_signal(barrier, inc=1, device_id={"tp": ranks.peer(k, j)}, device_id_type=MESH)
+    for k in range(1, shards):
+        pl.semaphore_signal(
+            barrier, inc=1, device_id={"fsdp": lax.rem(me + k, shards)}, device_id_type=MESH
+        )
+    piece = lax.axis_index("ctx")
+    pl.semaphore_signal(barrier, inc=1, device_id={"ctx": 1 - piece}, device_id_type=MESH)
+    pl.semaphore_wait(barrier, count + shards - 1)
+    shard = z_ref.shape[0]
+    half = shard // 2
+    place = lambda s: z_full_ref.at[half_rows(s, piece, half)]
+
+    def along(s, step, own_block):
+        way = 0 if step > 0 else 1
+        src = z_ref.at[pl.ds(pl.multiple_of(piece * half, half), half)] if own_block else place(s)
+        return shard_copy(
+            src, place(s), z_send.at[way, s], z_recv.at[s], "fsdp",
+            lax.rem(me + step + shards, shards),
+        )
+
+    def across(s):
+        return shard_copy(place(s), place(s), x_send.at[s], x_recv.at[s], "ctx", 1 - piece)
+
+    def arrival(d):
+        for step in (1, -1):
+            s = me - step * d
+            there = (s >= 0) & (s <= shards - 1)
+            s = jnp.minimum(jnp.maximum(s, 0), shards - 1)
+
+            @pl.when(there)
+            def _():
+                along(s, step, False).wait_recv()
+                across(s).start()
+
+            @pl.when(there & ((me < shards - 1) if step > 0 else (me > 0)))
+            def _():
+                along(s, step, False).start()
+
+    keep_z = pltpu.make_async_copy(
+        z_ref, z_full_ref.at[pl.ds(pl.multiple_of(me * shard, shard), shard)], local.at[2 + chips]
+    )
+    keep_z.start()
+    for step, there in ((1, me < shards - 1), (-1, me > 0)):
+        @pl.when(there)
+        def _():
+            along(me, step, True).start()
+
     copies = {}
     for k, j in ranks.others()[::-1]:
         peer, slot = ranks.peer(k, j), 2 * k + j
@@ -456,11 +527,14 @@
             keeps[-1].start()
         copies[slot].wait_recv()
         mid_ref[...] += dot(heads[slot], others[k] if slot % 2 else blocks[k][...], NT)
+    arrival(1)
     mid = mid_ref[...]
     factor = lax.rsqrt(row_mean(mid * mid) + EPSILON)
     rows_out[...] = (mid * factor * gain_ref[...]).astype(BF16)
     gather = GatherRows(ranks, rows_out, n2_ref, g_send, g_recv, local.at[0])
     gather.start()
+    for d in range(2, shards):
+        arrival(d)
     for slot in range(1, count):
         copies[slot].wait_send()
     for copy in swaps:
@@ -468,9 +542,20 @@
     for copy in keeps:
         copy.wait()
     gather.finish()
-
-
-def mix(count, attended, layer_input, gain, blocks):
+    keep_z.wait()
+    for k in range(1, shards):
+        across(lax.rem(me + k, shards)).wait()
+    for s in range(shards):
+        @pl.when((me >= s) & (me < shards - 1))
+        def _():
+            along(s, 1, False).wait_send()
+
+        @pl.when((me <= s) & (me > 0))
+        def _():
+            along(s, -1, False).wait_send()
+
+
+def mix(count, shards, attended, layer_input, gain, along_z, blocks):
     tokens, model = layer_input.shape
     own = tokens // count
     chips = count // 2
@@ -478,13 +563,14 @@
     vmem, hbm = pl.BlockSpec(memory_space=pltpu.VMEM), pl.BlockSpec(memory_space=pl.ANY)
     sem = pltpu.SemaphoreType.DMA
     return pl.pallas_call(
-        functools.partial(mix_kernel, count),
-        in_specs=[hbm, hbm, vmem] + [vmem] * chips,
-        out_specs=[hbm, vmem, hbm],
+        functools.partial(mix_kernel, count, shards),
+        in_specs=[hbm, hbm, vmem, hbm] + [vmem] * chips,
+        out_specs=[hbm, vmem, hbm, hbm],
         out_shape=[
             jax.ShapeDtypeStruct((tokens, model), BF16),
             jax.ShapeDtypeStruct((own, model), F32),
             jax.ShapeDtypeStruct((chips, model, width), BF16),
+            jax.ShapeDtypeStruct((model, along_z.shape[1]), BF16),
         ],
         scratch_shapes=[
             pltpu.VMEM((count, own, width), BF16),
@@ -492,7 +578,7 @@
             pltpu.VMEM((own, model), BF16),
             pltpu.VMEM((chips, model, width), BF16),
             sem((count,)), sem((count,)), sem((chips,)), sem((chips,)), sem((2, chips)),
-            sem((2, chips)), sem((2 + chips,)),
+            sem((2, chips)), sem((2, shards)), sem((shards,)), sem((shards,)), sem((shards,)), sem((3 + chips,)),
         ],
         compiler_params=pltpu.CompilerParams(
             vmem_limit_bytes=40 << 20, collective_id=1, has_side_effects=True
@@ -501,7 +587,7 @@
             flops=2 * tokens * model * model, bytes_accessed=150 << 20, transcendentals=0
         ),
         name="mix_heads",
-    )(attended, layer_input, gain, *blocks)
+    )(attended, layer_input, gain, along_z, *blocks)
 
 
 def scatter_order(ranks, halves, own, i):
@@ -538,12 +624,12 @@
     pl.semaphore_wait(sem, count)
 
 
-def feedforward_kernel(count, n2_ref, cot_ref, mid_ref, gain_ref, other_ref, weight_ref, *rest):
-    blocks, rest = rest[: count // 2], rest[count // 2 :]
+def feedforward_kernel(count, n2_ref, cot_ref, mid_ref, gain_ref, other_in, weight_ref, z_ref, *rest):
+    blocks_in, rest = rest[: count // 2], rest[count // 2 :]
     (
         ffb_ref, mg_ref, bg_ref, gain_grad_ref, da_ref, grad_ref, grads_ref,
         gate_w, up_w, down_w, n2, fg, hid, gu, rows_in, ffb_out,
-        c_send, c_recv, y_send, y_recv, f_send, f_recv, heads,
+        c_send, c_recv, y_send, y_recv, f_send, f_recv, heads, other_ref, blocks,
         w_sem, in_sem, out_sem, cs, cr, ys, yr, fs, fr, hs, hr, local,
     ) = rest
     ranks = Ranks(count)
@@ -553,11 +639,21 @@
     steps = ranks.chips * halves
     width = gate_w.shape[1]
     model = n2.shape[1]
-    loads = [pltpu.make_async_copy(n2_ref, n2, w_sem.at[3])] + [
-        pltpu.make_async_copy(weight_ref.at[:, pl.ds(w * width, width)], full, w_sem.at[w])
-        for w, full in enumerate((gate_w, up_w, down_w))
+    cut = weight_ref.shape[1] - width
+    loads = [
+        pltpu.make_async_copy(n2_ref, n2, w_sem.at[3]),
+        pltpu.make_async_copy(weight_ref.at[:, pl.ds(0, width)], gate_w, w_sem.at[0]),
+        pltpu.make_async_copy(weight_ref.at[:, pl.ds(width, cut)], up_w.at[:, pl.ds(0, cut)], w_sem.at[1]),
+        pltpu.make_async_copy(
+            z_ref.at[:, pl.ds(0, width - cut)], up_w.at[:, pl.ds(cut, width - cut)], w_sem.at[4]
+        ),
+        pltpu.make_async_copy(z_ref.at[:, pl.ds(width - cut, width)], down_w, w_sem.at[2]),
     ]
-    for load in loads:
+    late = [pltpu.make_async_copy(other_in, other_ref, w_sem.at[5])] + [
+        pltpu.make_async_copy(block, blocks.at[k], w_sem.at[6 + k])
+        for k, block in enumerate(blocks_in)
+    ]
+    for load in loads + late:
         load.start()
 
     def read(at, slot):
@@ -579,8 +675,9 @@
         fg[here, :] = grad
         gate = dot(n, gate_w[...])
         ready(2)
+        ready(3)
         up = dot(n, up_w[...])
-        ready(3)
+        ready(4)
         back = dot(grad, down_w[...])
         sig = 1.0 / (1.0 + jnp.exp(-gate))
         act = gate * sig
@@ -697,15 +794,17 @@
             for copy in fetch(u + 1):
                 copy.start()
     gain_grad_ref[...] = gain_total
+    for load in late:
+        load.wait()
     back = []
     for k, j in ranks.others()[::-1]:
         slot, peer = 2 * k + j, ranks.peer(-k, j)
-        heads[slot] = dot(bg_ref[...], other_ref[k] if j else blocks[k][...]).astype(BF16)
+        heads[slot] = dot(bg_ref[...], other_ref[k] if j else blocks[k]).astype(BF16)
         back.append(
             remote(heads.at[slot], da_ref.at[pl.ds(mine_at, own)], hs.at[slot], hr.at[slot], peer)
         )
         back[-1].start()
-    heads[0] = dot(bg_ref[...], blocks[0][...]).astype(BF16)
+    heads[0] = dot(bg_ref[...], blocks[0]).astype(BF16)
     keep = pltpu.make_async_copy(heads.at[0], da_ref.at[pl.ds(mine_at, own)], local.at[0])
     keep.start()
     product(n2, gu[:, width:], up_w, grads_ref.at[:, pl.ds(0, width)], 1)
@@ -723,17 +822,17 @@
         copy.wait()
 
 
-def feedforward(count, n2, cotangent, middle, gain, weights, blocks, others):
+def feedforward(count, n2, cotangent, middle, gain, weights, along_z, blocks, others):
     tokens, model = n2.shape
     own = tokens // count
-    hidden = weights.shape[1] // 3
+    hidden = (weights.shape[1] + along_z.shape[1]) // 3
     width = blocks[0].shape[1]
     rows, steps = own // 2, count
     vmem, hbm = pl.BlockSpec(memory_space=pltpu.VMEM), pl.BlockSpec(memory_space=pl.ANY)
     sem = pltpu.SemaphoreType.DMA
     return pl.pallas_call(
         functools.partial(feedforward_kernel, count),
-        in_specs=[hbm, hbm, hbm, vmem, vmem, hbm] + [vmem] * (count // 2),
+        in_specs=[hbm, hbm, hbm, vmem, hbm, hbm, hbm] + [hbm] * (count // 2),
         out_specs=[hbm, vmem, vmem, vmem, hbm, hbm, hbm],
         out_shape=[
             jax.ShapeDtypeStruct((steps, rows, model), BF16),
@@ -758,7 +857,9 @@
         + [pltpu.VMEM((2, rows, model), BF16)] * 2
         + [
             pltpu.VMEM((count, own, width), BF16),
-            sem((4,)), sem((2,)), sem((4,)),
+            pltpu.VMEM(others.shape, BF16),
+            pltpu.VMEM(others.shape, BF16),
+            sem((6 + count // 2,)), sem((2,)), sem((4,)),
             sem((2,)), sem((2,)), sem((steps - 2,)), sem((steps - 2,)),
             sem((2,)), sem((2,)), sem((count,)), sem((count,)), sem((1,)),
         ],
@@ -770,7 +871,7 @@
             transcendentals=tokens * hidden,
         ),
         name="feed_forward",
-    )(n2, cotangent, middle, gain, others, weights, *blocks)
+    )(n2, cotangent, middle, gain, others, weights, along_z, *blocks)
 
 
 def shard_copy(src, dst, send, recv, axis, index):
@@ -781,9 +882,10 @@
 
 
 def begin_kernel(
-    shards, x_ref, qkv_ref, wo_ref, gains_ref, n_ref, qkv_full_ref, wo_full_ref, gain_out_ref,
+    shards, x_ref, qkv_ref, wo_ref, gains_ref, order_ref, n_ref, qkv_full_ref, wo_full_ref, gain_out_ref,
     qkv_full, wo_full, normed, rows_in, gain_buf, zs, zr, xs, xr, gs, gr, own_sem, in_sem, out_sem,
 ):
+    del order_ref
     me, piece = lax.axis_index("fsdp"), lax.axis_index("ctx")
     fulls, sources = (qkv_full, wo_full), (qkv_ref, wo_ref)
     shard = qkv_ref.shape[0]
@@ -910,14 +1012,14 @@
         copy.wait()
 
 
-def begin(shards, x, qkv, wo, gains):
+def begin(shards, x, qkv, wo, gains, order):
     tokens, model = x.shape
     rows = math.gcd(tokens, 256)
     vmem, hbm = pl.BlockSpec(memory_space=pltpu.VMEM), pl.BlockSpec(memory_space=pl.ANY)
     sem = pltpu.SemaphoreType.DMA
     return pl.pallas_call(
         functools.partial(begin_kernel, shards),
-        in_specs=[hbm, vmem, vmem, vmem],
+        in_specs=[hbm, vmem, vmem, vmem, hbm],
         out_specs=[hbm, hbm, hbm, vmem],
         out_shape=[
             jax.ShapeDtypeStruct((tokens, model), BF16),
@@ -939,11 +1041,12 @@
         ),
         cost_estimate=pl.CostEstimate(flops=0, bytes_accessed=120 << 20, transcendentals=0),
         name="norm_and_gather",
-    )(x, qkv, wo, gains)
+    )(x, qkv, wo, gains, order)
 
 
 def project_kernel(
-    q_heads, n_ref, qkv_ref, spread_ref, cos_ref, sin_ref, krow_ref, vrow_ref, q_ref, kv_ref, wide
+    q_heads, n_ref, qkv_ref, spread_ref, cos_ref, sin_ref, krow_ref, vrow_ref, pick_ref, q_ref, kv_ref,
+    dense_ref, wide
 ):
     @pl.when(pl.program_id(0) == 0)
     def _():
@@ -955,6 +1058,7 @@
     kv_heads = kv_ref.shape[1] // LANES // 2
     cos, sin = cos_ref[...], sin_ref[...]
     out = dot(n_ref[...], wide[...])
+    plain = []
     for h in range(q_heads + 2 * kv_heads):
         part = out[:, h * LANES : (h + 1) * LANES]
         if h < q_heads + kv_heads:
@@ -962,11 +1066,13 @@
         if h < q_heads:
             q_ref[:, h * LANES : (h + 1) * LANES] = part.astype(BF16)
         else:
+            plain.append(part.astype(BF16))
             part = part + (krow_ref[...] if h < q_heads + kv_heads else vrow_ref[...])
             kv_ref[:, (h - q_heads) * LANES : (h - q_heads + 1) * LANES] = part.astype(BF16)
-
-
-def project(normed, qkv, spread, cos, sin, krow, vrow, q_heads, kv_heads):
+    dense_ref[...] = dot(jnp.concatenate(plain, axis=1), pick_ref[...]).astype(BF16)
+
+
+def project(normed, qkv, spread, cos, sin, krow, vrow, pick, q_heads, kv_heads):
     tokens, model = normed.shape
     wide = spread.shape[1]
     bm = math.gcd(tokens, 256)
@@ -975,11 +1081,13 @@
     return pl.pallas_call(
         functools.partial(project_kernel, q_heads),
         grid=(tokens // bm,),
-        in_specs=[row(model), whole(qkv), whole(spread), row(LANES), row(LANES), whole(krow), whole(vrow)],
-        out_specs=[row(q_heads * LANES), row(2 * kv_heads * LANES)],
+        in_specs=[row(model), whole(qkv), whole(spread), row(LANES), row(LANES), whole(krow), whole(vrow),
+            whole(pick)],
+        out_specs=[row(q_heads * LANES), row(2 * kv_heads * LANES), row(pick.shape[1])],
         out_shape=[
             jax.ShapeDtypeStruct((tokens, q_heads * LANES), BF16),
             jax.ShapeDtypeStruct((tokens, 2 * kv_heads * LANES), BF16),
+            jax.ShapeDtypeStruct((tokens, pick.shape[1]), BF16),
         ],
         scratch_shapes=[pltpu.VMEM((model, wide), BF16)],
         compiler_params=pltpu.CompilerParams(vmem_limit_bytes=40 << 20),
@@ -987,7 +1095,7 @@
             flops=2 * tokens * model * wide, bytes_accessed=16 << 20, transcendentals=0
         ),
         name="project_qkv",
-    )(normed, qkv, spread, cos, sin, krow, vrow)
+    )(normed, qkv, spread, cos, sin, krow, vrow, pick)
 
 
 def dense_kernel(
@@ -1313,55 +1421,64 @@
         )
         return pair.astype(F32)
 
-    ff_half = half_of(jnp.concatenate([gate_weight, up_weight, down_weight.T], axis=1))
+    cut = up_weight.shape[1] // 2
+    ff_half = half_of(jnp.concatenate([gate_weight, up_weight[:, :cut]], axis=1))
+    ff_later = jnp.concatenate([up_weight[:, cut:], down_weight.T], axis=1)
     gain_shard = jnp.stack([attention_gain, feedforward_gain]).astype(F32)
     gain_shard = jnp.pad(gain_shard, ((0, 6), (0, 0)))
     qkv_shard = jnp.concatenate([query_weight, key_matrix, value_matrix], axis=1)
     positions = doc_positions(doc_lengths[0], piece * tokens, tokens)
     cos, sin = rotary_lanes(positions, head_dim)
-    lane = lax.broadcasted_iota(jnp.int32, (1, LANES), 1)
-    krow = jnp.where((lane >= head_dim // 2) & (lane < head_dim // 2 + 3), -1.0, 0.0)
-    vrow = jnp.where((lane >= head_dim) & (lane < head_dim + 3), 1.0, 0.0)
-    spread = jnp.zeros((q_width + 2 * kv_width, (q_heads + 2 * kv_heads) * LANES), BF16)
+    lane = np.arange(LANES)[None, :]
+    half_dim = head_dim // 2
+    krow = np.where((lane >= half_dim) & (lane < half_dim + 3), -1.0, 0.0).astype(np.float32)
+    vrow = np.where((lane >= head_dim) & (lane < head_dim + 3), 1.0, 0.0).astype(np.float32)
     rot_q, rot_k = select_rotary(q_heads, head_dim), select_rotary(kv_heads, head_dim)
     val_q, val_k = select_value(q_heads, head_dim), select_value(kv_heads, head_dim)
-    spread = spread.at[:q_width, : q_heads * LANES].set(rot_q.T)
-    spread = spread.at[q_width : q_width + kv_width, q_heads * LANES : (q_heads + kv_heads) * LANES].set(rot_k.T)
-    spread = spread.at[q_width + kv_width :, (q_heads + kv_heads) * LANES :].set(val_k.T)
-
+    val_q_wide = np.ascontiguousarray(val_q.T)
+    spread = np.zeros((q_width + 2 * kv_width, (q_heads + 2 * kv_heads) * LANES), rot_q.dtype)
+    at_key, at_value = q_heads * LANES, (q_heads + kv_heads) * LANES
+    spread[:q_width, :at_key] = rot_q.T
+    spread[q_width : q_width + kv_width, at_key:at_value] = rot_k.T
+    spread[q_width + kv_width :, at_value:] = val_k.T
     normed_one, qkv_full, out_own, gains_full = begin(
-        shards, layer_input, qkv_shard, output_weight.T, gain_shard
-    )
-    queries, keys_values = project(
-        normed_one, qkv_full, spread, cos, sin, krow, vrow, q_heads, kv_heads
+        shards, layer_input, qkv_shard, output_weight.T, gain_shard, ff_half
+    )
+    widen_kv = np.ascontiguousarray(spread[q_width:, at_key:])
+    marks = np.concatenate([krow] * kv_heads + [vrow] * kv_heads, axis=1)
+    queries, keys_values, dense_kv = project(
+        normed_one, qkv_full, spread, cos, sin, krow, vrow, np.ascontiguousarray(widen_kv.T), q_heads, kv_heads
     )
     ff_half, gains_full = lax.optimization_barrier((ff_half, gains_full))
     ff_full = lax.all_gather(ff_half, both_axes, axis=0, tiled=True)
     gain_one, gain_two = gains_full[0:1], gains_full[1:2]
-    before = lax.ppermute(keys_values, "ctx", [(0, 1)])
+    before = lax.ppermute(dense_kv, "ctx", [(0, 1)])
     base = -(piece - 1) * tokens
     ends = jnp.cumsum(doc_lengths[0]).astype(jnp.int32) + base
     base = base.astype(jnp.int32).reshape(1)
     state = attention_forward(ends, base, queries, keys_values, head_dim, tokens)
     attended, marked = attention_forward(
-        ends, base, queries, before, head_dim, 0, state, val_q
+        ends, base, queries, before, head_dim, 0, state, (widen_kv, marks, val_q)
     )
     wo = [out_own] + [lax.ppermute(out_own, "tp", chip_shift(k)) for k in range(1, chips)]
-    normed_two, middle, wo_others = mix(ranks, attended, layer_input, gain_two, wo)
+    normed_two, middle, wo_others, ff_rest = mix(
+        ranks, shards, attended, layer_input, gain_two, ff_later, wo
+    )
     (
         feed_sums, middle_grad, branch_grad, gain_two_grad, attended_grad, gate_part, feed_part,
     ) = feedforward(
-        ranks, normed_two, output_cotangent, middle, gain_two, ff_full, wo, wo_others
+        ranks, normed_two, output_cotangent, middle, gain_two, ff_full, ff_rest, wo, wo_others
     )
     gate_own, feed_own = reduce_fsdp(gate_part), reduce_fsdp(feed_part)
     cut = feed_sums.reshape(chips, own, model)
     feed_sums = [lax.ppermute(cut[k - 1], "tp", chip_shift(k)) for k in range(1, chips)]
     dq_part, dkv_before = attention_backward(
-        ends, base, marked, attended_grad, attended, before, val_q.T, head_dim, 0
+        ends, base, marked, attended_grad, attended, before, val_q_wide, head_dim, 0,
+        extra=(widen_kv, marks),
     )
     after = lax.ppermute(dkv_before, "ctx", [(1, 0)])
     dq, dkv = attention_backward(
-        ends, base, marked, attended_grad, attended, keys_values, val_q.T, head_dim, tokens,
+        ends, base, marked, attended_grad, attended, keys_values, val_q_wide, head_dim, tokens,
         (dq_part, cos, sin, rot_q),
     )
 

time: 526 us -> 528 us (level)
  Pallas kernels: 330 us -> 358 us
  waiting for transfers between devices: 102 us -> 75.5 us
    pallas_call x1, Pallas kernels: 48 us -> 76 us  [mix(): pl.pallas_call(functools.partial(mix_kernel, count, shards), in_specs=[hb...]
    all_gather x1, waiting for transfers between devices: 22 us -> 0.01 us  [per_device(): ff_full = lax.all_gather(ff_half, both_axes, axis=0, tiled=True)]
    pallas_call x1, Pallas kernels: 93.8 us -> 88.1 us  [close(): pl.pallas_call(functools.partial(close_kernel, count, shards), in_specs=[...]
    unnamed x79 -> x113, local copies, waits for them, and re-layouts: 27.3 us -> 29.3 us
  transfers between devices with their start and end apart: 12 -> 12, of which waited for: 6 -> 6; matrix products, arithmetic and copies ran while one was open for 6% -> 6% of each run, Pallas kernels for 40% -> 45%
where the time goes in v3:
time: 528 us; the launch traced here: 519 us
  Pallas kernels  358 us (68%)
  waiting for transfers between devices  75.5 us (14%)
  local copies, waits for them, and re-layouts  36.2 us (7%)
  other arithmetic  22.7 us (4%)
  between operations  14.6 us (3%)
  starting transfers between devices  11.6 us (2%)
    pallas_call x1, Pallas kernels, close(): pl.pallas_call(functools.partial(close_kernel, count, shards), in_specs=[...  88.1 us
    pallas_call x1, Pallas kernels, feedforward(): pl.pallas_call(functools.partial(feedforward_kernel, count), in_specs=[hb...  78.6 us
    pallas_call x1, Pallas kernels, mix(): pl.pallas_call(functools.partial(mix_kernel, count, shards), in_specs=[hb...  76 us
    pallas_call x1, Pallas kernels, begin(): pl.pallas_call(functools.partial(begin_kernel, shards), in_specs=[hbm, vm...  45.4 us
    pallas_call x2, Pallas kernels, attention_backward(): pl.pallas_call(functools.partial(attention_backward_kernel, rest is None,...  29.8 us
    unnamed x113, local copies, waits for them, and re-layouts  29.3 us
    reduce_scatter x3, waiting for transfers between devices, reduce_fsdp(): return lax.psum_scatter(part, 'fsdp', scatter_dimension=0, tiled=True)  28 us
    ppermute x2, waiting for transfers between devices, from_chips(): lax.ppermute(rows, 'tp', chip_shift(k))  24.7 us
  transfers between devices with their start and end apart: 12, of which 6 were waited for; matrix products, arithmetic and copies ran while one was open for 6% of the time, Pallas kernels for 45%

profile of v3, /device:TPU:0, one launch (start us, length us, event | category | flops | bytes accessed | tf_op | source)
XLA Modules:
  0.0 519.0 jit_solution(17465651121580516030)
XLA Ops:
  7.3 2.0 fusion.13
  10.4 45.4 %norm_and_gather.1 = (bf16[1536,1536]{1,0:T(8,128)(2,1)}, bf16[1536,768]{1,0:T(8,128)(2,1)S(1)}, bf16[1536,384]{1,0:T(8,128)(2,1)}, f32[8,1536]{1,0:T(8,128)S(1)}) custom-call(f32[1536,1536]{1,0:T(8,128)} %x_ref.5, bf16[384,768]{1,0:T(8,128)(2,1)S(1)} %pad_maximum_fusion.5.qkv_ref, bf16[384,384]{1,0:T(8,128)(2,1)S(1)} %bitcast.17, ...), custom_call_target="tpu_custom_call" | custom-call | bytes 125829120 | tf_op jit(solution)/shard_map/norm_and_gather/pallas_call | solution.py:1020
  56.4 2.8 fusion.6
  60.7 12.2 %project_qkv.1 = (bf16[1536,512]{1,0:T(8,128)(2,1)S(1)}, bf16[1536,512]{1,0:T(8,128)(2,1)S(1)}, bf16[1536,384]{1,0:T(8,128)(2,1)}) custom-call(bf16[1536,1536]{1,0:T(8,128)(2,1)} %get-tuple-element.50.n_ref, bf16[1536,768]{1,0:T(8,128)(2,1)S(1)} %get-tuple-element.51.qkv_ref.w_ref, bf16[768,1024]{1,0:T(8,128)(2,1)S(1)} %copy-done.17, ...), custom_call_target="tpu_custom_call" | custom-call | flops 4831838208 | bytes 16777216 | tf_op jit(solution)/shard_map/project_qkv/pallas_call | solution.py:1081
  75.2 2.6 collective-permute-start
  79.5 2.3 copy.45
  84.9 9.1 %attention_forward.2 = (f32[3,2,1,1024]{3,2,1,0:T(1,128)S(1)}, f32[3,2,128,1024]{3,2,1,0:T(8,128)S(1)}) custom-call(s32[3]{0:T(128)S(1)} %get-tuple-element.131.ends_ref, s32[1]{0:T(128)} %bitcast.2.base_ref, bf16[1536,512]{1,0:T(8,128)(2,1)S(1)} %copy-done.33, bf16[1536,512]{1,0:T(8,128)(2,1)S(1)} %copy-done.31), custom_call_target="tpu_custom_call" | custom-call | flops 4831838208 | bytes 8388608 | tf_op jit(solution)/shard_map/attention_forward/pallas_call | solution.py:210
  94.0 18.9 %collective-permute-done.kv_ref = bf16[1536,384]{1,0:T(8,128)(2,1)S(1)} collective-permute-done((bf16[1536,384]{1,0:T(8,128)(2,1)}, bf16[1536,384]{1,0:T(8,128)(2,1)S(1)}, u32[]{:S(2)}, u32[]{:S(2)}) %collective-permute-start) | collective-permute-done | bytes 1179680 | tf_op jit(solution)/shard_map/ppermute | solution.py:1455
  113.0 5.6 %attention_forward.3 = (bf16[1536,384]{1,0:T(8,128)(2,1)S(1)}, bf16[1536,512]{1,0:T(8,128)(2,1)S(1)}) custom-call(s32[3]{0:T(128)S(1)} %get-tuple-element.131.ends_ref, s32[1]{0:T(128)} %bitcast.2.base_ref, bf16[1536,512]{1,0:T(8,128)(2,1)S(1)} %copy-done.33, bf16[1536,384]{1,0:T(8,128)(2,1)S(1)} %collective-permute-done.kv_ref, ...), custom_call_target="tpu_custom_call" | custom-call | flops 4831838208 | bytes 8388608 | tf_op jit(solution)/shard_map/attention_forward/pallas_call | solution.py:210
  119.8 76.0 %mix_heads.1 = (bf16[1536,1536]{1,0:T(8,128)(2,1)S(1)}, f32[384,1536]{1,0:T(8,128)S(1)}, bf16[2,1536,384]{2,1,0:T(8,128)(2,1)S(1)}, bf16[1536,1536]{1,0:T(8,128)(2,1)}) custom-call(bf16[1536,384]{1,0:T(8,128)(2,1)S(1)} %get-tuple-element.57.att_ref.o_ref, f32[1536,1536]{1,0:T(8,128)} %x_ref.5, f32[1,1536]{1,0:T(1,128)S(1)} %get-tuple-element.126.gain_ref, ...), custom_call_target="tpu_custom_call" | custom-call | flops 7247757312 | bytes 157286400 | tf_op jit(solution)/shard_map/mix_heads/pallas_call | solution.py:565
  198.4 2.2 copy-done.34
  202.0 78.6 %feed_forward.1 = (bf16[4,192,1536]{2,1,0:T(8,128)(2,1)}, f32[384,1536]{1,0:T(8,128)}, bf16[384,1536]{1,0:T(8,128)(2,1)}, f32[1,1536]{1,0:T(1,128)}, bf16[1536,3...) custom-call(bf16[1536,1536]{1,0:T(8,128)(2,1)} %copy-done.34, f32[1536,1536]{1,0:T(8,128)} %cot_ref.1, ...), custom_call_target="tpu_custom_call" | custom-call | flops 43486543872 | bytes 293601280 | tf_op jit(solution)/shard_map/feed_forward/pallas_call | solution.py:833
  285.2 6.2 %attention_backward.2 = (f32[1536,512]{1,0:T(8,128)}, bf16[1536,512]{1,0:T(8,128)(2,1)S(1)}) custom-call(s32[3]{0:T(128)S(1)} %get-tuple-element.131.ends_ref, s32[1]{0:T(128)} %bitcast.2.base_ref, bf16[1536,512]{1,0:T(8,128)(2,1)} %copy-done.36, bf16[1536,384]{1,0:T(8,128)(2,1)S(1)} %copy-done.37, bf16[1536,384]{1,0:T(8,128)(2,1)S(1)} %copy-done.29, ...), custom_call_target="tpu_custom_call" | custom-call | flops 12079595520 | bytes 12582912 | tf_op jit(solution)/shard_map/attention_backward/pallas_call | solution.py:336
  293.6 23.6 %attention_backward.3 = (bf16[1536,384]{1,0:T(8,128)(2,1)S(1)}, f32[1536,512]{1,0:T(8,128)}) custom-call(s32[3]{0:T(128)S(1)} %get-tuple-element.131.ends_ref, s32[1]{0:T(128)} %bitcast.2.base_ref, bf16[1536,512]{1,0:T(8,128)(2,1)} %copy-done.36, bf16[1536,384]{1,0:T(8,128)(2,1)S(1)} %copy-done.37, bf16[1536,384]{1,0:T(8,128)(2,1)S(1)} %copy-done.29, ...), custom_call_target="tpu_custom_call" | custom-call | flops 12079595520 | bytes 12582912 | tf_op jit(solution)/shard_map/attention_backward/pallas_call | solution.py:336
  321.3 16.7 %collective-permute-done.4.rest_1_ = bf16[384,1536]{1,0:T(8,128)(2,1)} collective-permute-done((bf16[384,1536]{1,0:T(8,128)(2,1)S(1)}, bf16[384,1536]{1,0:T(8,128)(2,1)}, u32[]{:S(2)}, u32[]{:S(2)}) %collective-permute-start.4) | collective-permute-done | bytes 1179680 | tf_op jit(solution)/shard_map/ppermute | solution.py:1492
  339.2 13.5 %dense_gradients.1 = (bf16[1536,768]{1,0:T(8,128)(2,1)}, bf16[1536,1152]{1,0:T(8,128)(2,1)}) custom-call(bf16[1536,384]{1,0:T(8,128)(2,1)S(1)} %get-tuple-element.71.dq_ref, f32[1536,512]{1,0:T(8,128)} %get-tuple-element.72.dkv_ref, bf16[1536,512]{1,0:T(8,128)(2,1)} %copy-done.49, f32[1536,128]{1,0:T(8,128)S(1)} %copy-done.10, f32[1536,128]{1,0:T(8,128)S(1)} %copy-done.8, ...), custom_call_target="tpu_custom_call" | custom-call | flops 5435817984 | bytes 25165824 | tf_op jit(solution)/shard_map/dense_gradients/pallas_call | solution.py:1147
  352.7 8.0 %collective-permute-done.5.rest_1_ = bf16[384,1536]{1,0:T(8,128)(2,1)S(1)} collective-permute-done((bf16[384,1536]{1,0:T(8,128)(2,1)S(1)}, bf16[384,1536]{1,0:T(8,128)(2,1)S(1)}, u32[]{:S(2)}, u32[]{:S(2)}) %collective-permute-start.5) | collective-permute-done | bytes 1179680 | tf_op jit(solution)/shard_map/ppermute | solution.py:1492
  364.1 88.1 %close_layer.1 = (bf16[1536,1536]{1,0:T(8,128)(2,1)}, f32[8,1536]{1,0:T(8,128)S(1)}, bf16[768,1152]{1,0:T(8,128)(2,1)}, bf16[1536,1536]{1,0:T(8,128)(2,1)}, f32[384,1024]{1,0:T(8,128)S(1)}) custom-call(bf16[1536,768]{1,0:T(8,128)(2,1)} %get-tuple-element.75.dense_ref, bf16[1536,768]{1,0:T(8,128)(2,1)} %copy-done.1, f32[1536,1536]{1,0:T(8,128)} %x_ref.5, ...), custom_call_target="tpu_custom_call" | custom-call | flops 3623878656 | bytes 209715200 | tf_op jit(solution)/shard_map/close_layer/pallas_call | solution.py:1324
  455.6 7.6 %convert_element_type.46 = f32[1536,1536]{1,0:T(8,128)} convert(bf16[1536,1536]{1,0:T(8,128)(2,1)} %get-tuple-element.81) | non-fusion elementwise | flops 2359296 | bytes 14155776 | tf_op jit(solution)/shard_map/convert_element_type | solution.py:1504
  463.2 5.1 convert_element_type.47
  468.9 26.2 %reduce-scatter.8.cloned.1.call-done = bf16[192,1152]{1,0:T(8,128)(2,1)} async-done(((bf16[768,1152]{1,0:T(8,128)(2,1)}), bf16[192,1152]{1,0:T(8,128)(2,1)}) %reduce-scatter.8.cloned.1.call-update) | async-done | bytes 442384 | tf_op jit(solution)/shard_map/reduce_scatter | solution.py:1412
  496.6 2.5 convert_add_fusion
  501.0 3.1 copy.49
  504.0 3.0 collective-permute-done.6
  (156 shorter events, 43.0 us)
Async XLA Ops:
  7.2 194.7 %all-gather.2.cloned.1.call-start = ((), (), s32[]{:S(2)}) async-start(), calls=%async_computation.3 | async-start | bytes 5308416 | tf_op jit(solution)/shard_map/all_gather | solution.py:1453
  10.0 45.9 %copy-start = (bf16[192,1536]{1,0:T(8,128)(2,1)}, bf16[192,1536]{1,0:T(8,128)(2,1)S(1)}, u32[]{:S(2)}) copy-start(bf16[192,1536]{1,0:T(8,128)(2,1)S(1)} %fusion.5.order_ref) | copy-start | bytes 1769476
  10.4 45.5 %copy-start.48 = (s32[1,3]{1,0:T(1,128)S(1)}, s32[1,3]{1,0:T(1,128)}, u32[]{:S(2)}) copy-start(s32[1,3]{1,0:T(1,128)} %param.24) | copy-start | bytes 40
  55.9 305.8 %reduce-scatter.4.cloned.1.call-start = ((), (), s32[]{:S(2)}) async-start(), calls=%async_computation.4 | async-start | bytes 3932160 | tf_op jit(solution)/shard_map/reduce_scatter | solution.py:1412
  60.2 12.8 %copy-start.7 = (f32[1536,128]{1,0:T(8,128)}, f32[1536,128]{1,0:T(8,128)S(1)}, u32[]{:S(2)}) copy-start(f32[1536,128]{1,0:T(8,128)S(1)} %get-tuple-element.123.sin_ref.rest_2_) | copy-start | bytes 2359300
  75.2 37.7 %collective-permute-start = (bf16[1536,384]{1,0:T(8,128)(2,1)}, bf16[1536,384]{1,0:T(8,128)(2,1)S(1)}, u32[]{:S(2)}, u32[]{:S(2)}) collective-permute-start(bf16[1536,384]{1,0:T(8,128)(2,1)} %get-tuple-element.53), channel_id=1, source_target_pairs={{0,4},{1,5},{2,6},{3,7},{8,12},{9,13},{10,14},{11,15},{16,20},{17,... | collective-permute-start | bytes 3538952 | tf_op jit(solution)/shard_map/ppermute | solution.py:1455
  77.9 41.9 %collective-permute-start.1 = (bf16[1536,384]{1,0:T(8,128)(2,1)}, bf16[1536,384]{1,0:T(8,128)(2,1)S(1)}, u32[]{:S(2)}, u32[]{:S(2)}) collective-permute-start(bf16[1536,384]{1,0:T(8,128)(2,1)} %get-tuple-element.60.rest_0_), channel_id=1, source_target_pairs={{0,2},{1,3},{2,0},{3,1},{4,6},{5,7},{6,4},{7,5},{8,10},{9,11},{10,... | collective-permute-start | bytes 3538952 | tf_op jit(solution)/shard_map/ppermute | solution.py:1463
  79.5 40.3 %copy-start.12 = (f32[1,1536]{1,0:T(1,128)}, f32[1,1536]{1,0:T(1,128)S(1)}, u32[]{:S(2)}) copy-start(f32[1,1536]{1,0:T(1,128)S(1)} %get-tuple-element.126.gain_ref) | copy-start | bytes 18436
  84.9 28.0 %copy-start.20 = (bf16[384,512]{1,0:T(8,128)(2,1)S(1)}, bf16[384,512]{1,0:T(8,128)(2,1)}, u32[]{:S(2)}) copy-start(bf16[384,512]{1,0:T(8,128)(2,1)} %constant.63.clone.rest_0_) | copy-start | bytes 1179652
  84.9 28.0 %copy-start.21 = (bf16[512,384]{1,0:T(8,128)(2,1)S(1)}, bf16[512,384]{1,0:T(8,128)(2,1)}, u32[]{:S(2)}) copy-start(bf16[512,384]{1,0:T(8,128)(2,1)} %constant.65.clone.rest_2_) | copy-start | bytes 1179652
  84.9 28.0 %copy-start.25 = (f32[1,512]{1,0:T(1,128)S(1)}, f32[1,512]{1,0:T(1,128)}, u32[]{:S(2)}) copy-start(f32[1,512]{1,0:T(1,128)} %constant.64.clone.rest_1_) | copy-start | bytes 6148
  119.8 76.1 %copy-start.16 = (bf16[1536,384]{1,0:T(8,128)(2,1)}, bf16[1536,384]{1,0:T(8,128)(2,1)S(1)}, u32[]{:S(2)}) copy-start(bf16[1536,384]{1,0:T(8,128)(2,1)S(1)} %collective-permute-done.1.rest_1_) | copy-start | bytes 3538948
  280.6 173.4 %reduce-scatter.6.cloned.1.call-start = ((), (), s32[]{:S(2)}) async-start(), calls=%async_computation.5 | async-start | bytes 7864320 | tf_op jit(solution)/shard_map/reduce_scatter | solution.py:1412
  281.3 213.8 %reduce-scatter.8.cloned.1.call-start = ((), (), s32[]{:S(2)}) async-start(), calls=%async_computation.6 | async-start | bytes 2211840 | tf_op jit(solution)/shard_map/reduce_scatter | solution.py:1412
  283.5 33.7 %collective-permute-start.2 = (bf16[384,1536]{1,0:T(8,128)(2,1)}, bf16[384,1536]{1,0:T(8,128)(2,1)S(1)}, u32[]{:S(2)}, u32[]{:S(2)}) collective-permute-start(bf16[384,1536]{1,0:T(8,128)(2,1)} %bitcast.6), channel_id=1, source_target_pairs={{0,2},{1,3},{2,0},{3,1},{4,6},{5,7},{6,4},{7,5},{8,10},{9,11},{10,... | collective-permute-start | bytes 3538952 | tf_op jit(solution)/shard_map/ppermute | solution.py:1474
  291.4 46.7 %collective-permute-start.3 = (bf16[1536,512]{1,0:T(8,128)(2,1)S(1)}, bf16[1536,512]{1,0:T(8,128)(2,1)S(1)}, u32[]{:S(2)}, u32[]{:S(2)}) collective-permute-start(bf16[1536,512]{1,0:T(8,128)(2,1)S(1)} %get-tuple-element.73), channel_id=1, source_target_pairs={{4,0},{5,1},{6,2},{7,3},{12,8},{13,9},{14,10},{15,11},{20,16},{21,... | collective-permute-start | bytes 4718600 | tf_op jit(solution)/shard_map/ppermute | solution.py:1479
  292.7 45.4 %collective-permute-start.4 = (bf16[384,1536]{1,0:T(8,128)(2,1)S(1)}, bf16[384,1536]{1,0:T(8,128)(2,1)}, u32[]{:S(2)}, u32[]{:S(2)}) collective-permute-start(bf16[384,1536]{1,0:T(8,128)(2,1)S(1)} %copy-done.13), channel_id=1, source_target_pairs={{0,2},{1,3},{2,0},{3,1},{4,6},{5,7},{6,4},{7,5},{8,10},{9,11},{10,... | collective-permute-start | bytes 3538952 | tf_op jit(solution)/shard_map/ppermute | solution.py:1492
  293.6 24.7 %copy-start.3 = (f32[384,1536]{1,0:T(8,128)S(1)}, f32[384,1536]{1,0:T(8,128)}, u32[]{:S(2)}) copy-start(f32[384,1536]{1,0:T(8,128)} %copy-done.2) | copy-start | bytes 7077892
  318.3 20.9 %copy-start.23 = (bf16[256,192]{1,0:T(8,128)(2,1)S(1)}, bf16[256,192]{1,0:T(8,128)(2,1)}, u32[]{:S(2)}) copy-start(bf16[256,192]{1,0:T(8,128)(2,1)} %constant.68.clone.rotk_ref) | copy-start | bytes 294916
  318.3 20.9 %copy-start.24 = (bf16[256,192]{1,0:T(8,128)(2,1)S(1)}, bf16[256,192]{1,0:T(8,128)(2,1)}, u32[]{:S(2)}) copy-start(bf16[256,192]{1,0:T(8,128)(2,1)} %constant.69.clone.valk_ref) | copy-start | bytes 294916
  320.0 40.6 %collective-permute-start.5 = (bf16[384,1536]{1,0:T(8,128)(2,1)S(1)}, bf16[384,1536]{1,0:T(8,128)(2,1)S(1)}, u32[]{:S(2)}, u32[]{:S(2)}) collective-permute-start(bf16[384,1536]{1,0:T(8,128)(2,1)S(1)} %fusion.1.rest_0_), channel_id=1, source_target_pairs={{0,2},{1,3},{2,0},{3,1},{4,6},{5,7},{6,4},{7,5},{8,10},{9,11},{10,... | collective-permute-start | bytes 3538952 | tf_op jit(solution)/shard_map/ppermute | solution.py:1492
  339.2 22.5 %copy-start.11 = (f32[1,1536]{1,0:T(1,128)S(1)}, f32[1,1536]{1,0:T(1,128)}, u32[]{:S(2)}) copy-start(f32[1,1536]{1,0:T(1,128)} %get-tuple-element.77.gain_two_ref) | copy-start | bytes 18436
  454.0 42.6 %collective-permute-start.7 = (bf16[384,2048]{1,0:T(8,128)(2,1)}, bf16[384,2048]{1,0:T(8,128)(2,1)}, u32[]{:S(2)}, u32[]{:S(2)}) collective-permute-start(bf16[384,2048]{1,0:T(8,128)(2,1)} %reduce-scatter.6.cloned.1.call-done), channel_id=1, source_target_pairs={{0,4},{4,0},{1,5},{5,1},{2,6},{6,2},{3,7},{7,3},{8,12},{12,8},{9,1... | collective-permute-start | bytes 4718600 | tf_op jit(solution)/shard_map/ppermute | solution.py:1415
  495.1 11.9 %collective-permute-start.6 = (bf16[192,1152]{1,0:T(8,128)(2,1)}, bf16[192,1152]{1,0:T(8,128)(2,1)S(1)}, u32[]{:S(2)}, u32[]{:S(2)}) collective-permute-start(bf16[192,1152]{1,0:T(8,128)(2,1)} %reduce-scatter.8.cloned.1.call-done), channel_id=1, source_target_pairs={{0,4},{4,0},{1,5},{5,1},{2,6},{6,2},{3,7},{7,3},{8,12},{12,8},{9,1... | collective-permute-start | bytes 1327112 | tf_op jit(solution)/shard_map/ppermute | solution.py:1418
  (40 other events, 129.2 us)
Sparse Core Ops, SparseCore 0:
  56.0 81.4 all-gather.1
  280.7 56.9 reduce-scatter.3
  340.1 113.9 reduce-scatter.5
  456.2 38.8 reduce-scatter.7

commit v4 on v3

--- a/solution.py
+++ b/solution.py
@@ -437,12 +437,12 @@
     return copies
 
 
-def mix_kernel(count, shards, att_ref, x_ref, gain_ref, z_ref, *rest):
+def mix_kernel(count, att_ref, x_ref, gain_ref, *rest):
     chips = count // 2
     blocks, rest = rest[:chips], rest[chips:]
     (
-        n2_ref, mid_ref, other_ref, z_full_ref, heads, rows_in, rows_out, others, a_send, a_recv,
-        b_send, b_recv, g_send, g_recv, z_send, z_recv, x_send, x_recv, local,
+        n2_ref, mid_ref, other_ref, heads, rows_in, rows_out, others, a_send, a_recv, b_send, b_recv,
+        g_send, g_recv, local,
     ) = rest
     ranks = Ranks(count)
     own = rows_in.shape[0]
@@ -451,56 +451,7 @@
     fetch.start()
     mine = pltpu.make_async_copy(att_ref.at[mine_at], heads.at[0], local.at[1])
     mine.start()
-    me = lax.axis_index("fsdp")
-    barrier = pltpu.get_barrier_semaphore()
-    for k, j in ranks.others():
-        pl.semaphore_signal(barrier, inc=1, device_id={"tp": ranks.peer(k, j)}, device_id_type=MESH)
-    for k in range(1, shards):
-        pl.semaphore_signal(
-            barrier, inc=1, device_id={"fsdp": lax.rem(me + k, shards)}, device_id_type=MESH
-        )
-    piece = lax.axis_index("ctx")
-    pl.semaphore_signal(barrier, inc=1, device_id={"ctx": 1 - piece}, device_id_type=MESH)
-    pl.semaphore_wait(barrier, count + shards - 1)
-    shard = z_ref.shape[0]
-    half = shard // 2
-    place = lambda s: z_full_ref.at[half_rows(s, piece, half)]
-
-    def along(s, step, own_block):
-        way = 0 if step > 0 else 1
-        src = z_ref.at[pl.ds(pl.multiple_of(piece * half, half), half)] if own_block else place(s)
-        return shard_copy(
-            src, place(s), z_send.at[way, s], z_recv.at[s], "fsdp",
-            lax.rem(me + step + shards, shards),
-        )
-
-    def across(s):
-        return shard_copy(place(s), place(s), x_send.at[s], x_recv.at[s], "ctx", 1 - piece)
-
-    def arrival(d):
-        for step in (1, -1):
-            s = me - step * d
-            there = (s >= 0) & (s <= shards - 1)
-            s = jnp.minimum(jnp.maximum(s, 0), shards - 1)
-
-            @pl.when(there)
-            def _():
-                along(s, step, False).wait_recv()
-                across(s).start()
-
-            @pl.when(there & ((me < shards - 1) if step > 0 else (me > 0)))
-            def _():
-                along(s, step, False).start()
-
-    keep_z = pltpu.make_async_copy(
-        z_ref, z_full_ref.at[pl.ds(pl.multiple_of(me * shard, shard), shard)], local.at[2 + chips]
-    )
-    keep_z.start()
-    for step, there in ((1, me < shards - 1), (-1, me > 0)):
-        @pl.when(there)
-        def _():
-            along(me, step, True).start()
-
+    ranks.barrier()
     copies = {}
     for k, j in ranks.others()[::-1]:
         peer, slot = ranks.peer(k, j), 2 * k + j
@@ -527,14 +478,11 @@
             keeps[-1].start()
         copies[slot].wait_recv()
         mid_ref[...] += dot(heads[slot], others[k] if slot % 2 else blocks[k][...], NT)
-    arrival(1)
     mid = mid_ref[...]
     factor = lax.rsqrt(row_mean(mid * mid) + EPSILON)
     rows_out[...] = (mid * factor * gain_ref[...]).astype(BF16)
     gather = GatherRows(ranks, rows_out, n2_ref, g_send, g_recv, local.at[0])
     gather.start()
-    for d in range(2, shards):
-        arrival(d)
     for slot in range(1, count):
         copies[slot].wait_send()
     for copy in swaps:
@@ -542,20 +490,9 @@
     for copy in keeps:
         copy.wait()
     gather.finish()
-    keep_z.wait()
-    for k in range(1, shards):
-        across(lax.rem(me + k, shards)).wait()
-    for s in range(shards):
-        @pl.when((me >= s) & (me < shards - 1))
-        def _():
-            along(s, 1, False).wait_send()
-
-        @pl.when((me <= s) & (me > 0))
-        def _():
-            along(s, -1, False).wait_send()
-
-
-def mix(count, shards, attended, layer_input, gain, along_z, blocks):
+
+
+def mix(count, attended, layer_input, gain, blocks):
     tokens, model = layer_input.shape
     own = tokens // count
     chips = count // 2
@@ -563,14 +500,13 @@
     vmem, hbm = pl.BlockSpec(memory_space=pltpu.VMEM), pl.BlockSpec(memory_space=pl.ANY)
     sem = pltpu.SemaphoreType.DMA
     return pl.pallas_call(
-        functools.partial(mix_kernel, count, shards),
-        in_specs=[hbm, hbm, vmem, hbm] + [vmem] * chips,
-        out_specs=[hbm, vmem, hbm, hbm],
+        functools.partial(mix_kernel, count),
+        in_specs=[hbm, hbm, vmem] + [vmem] * chips,
+        out_specs=[hbm, vmem, hbm],
         out_shape=[
             jax.ShapeDtypeStruct((tokens, model), BF16),
             jax.ShapeDtypeStruct((own, model), F32),
             jax.ShapeDtypeStruct((chips, model, width), BF16),
-            jax.ShapeDtypeStruct((model, along_z.shape[1]), BF16),
         ],
         scratch_shapes=[
             pltpu.VMEM((count, own, width), BF16),
@@ -578,7 +514,7 @@
             pltpu.VMEM((own, model), BF16),
             pltpu.VMEM((chips, model, width), BF16),
             sem((count,)), sem((count,)), sem((chips,)), sem((chips,)), sem((2, chips)),
-            sem((2, chips)), sem((2, shards)), sem((shards,)), sem((shards,)), sem((shards,)), sem((3 + chips,)),
+            sem((2, chips)), sem((2 + chips,)),
         ],
         compiler_params=pltpu.CompilerParams(
             vmem_limit_bytes=40 << 20, collective_id=1, has_side_effects=True
@@ -587,7 +523,7 @@
             flops=2 * tokens * model * model, bytes_accessed=150 << 20, transcendentals=0
         ),
         name="mix_heads",
-    )(attended, layer_input, gain, along_z, *blocks)
+    )(attended, layer_input, gain, *blocks)
 
 
 def scatter_order(ranks, halves, own, i):
@@ -624,7 +560,7 @@
     pl.semaphore_wait(sem, count)
 
 
-def feedforward_kernel(count, n2_ref, cot_ref, mid_ref, gain_ref, other_in, weight_ref, z_ref, *rest):
+def feedforward_kernel(count, n2_ref, cot_ref, mid_ref, gain_ref, other_in, weight_ref, *rest):
     blocks_in, rest = rest[: count // 2], rest[count // 2 :]
     (
         ffb_ref, mg_ref, bg_ref, gain_grad_ref, da_ref, grad_ref, grads_ref,
@@ -639,18 +575,12 @@
     steps = ranks.chips * halves
     width = gate_w.shape[1]
     model = n2.shape[1]
-    cut = weight_ref.shape[1] - width
-    loads = [
-        pltpu.make_async_copy(n2_ref, n2, w_sem.at[3]),
-        pltpu.make_async_copy(weight_ref.at[:, pl.ds(0, width)], gate_w, w_sem.at[0]),
-        pltpu.make_async_copy(weight_ref.at[:, pl.ds(width, cut)], up_w.at[:, pl.ds(0, cut)], w_sem.at[1]),
-        pltpu.make_async_copy(
-            z_ref.at[:, pl.ds(0, width - cut)], up_w.at[:, pl.ds(cut, width - cut)], w_sem.at[4]
-        ),
-        pltpu.make_async_copy(z_ref.at[:, pl.ds(width - cut, width)], down_w, w_sem.at[2]),
+    loads = [pltpu.make_async_copy(n2_ref, n2, w_sem.at[3])] + [
+        pltpu.make_async_copy(weight_ref.at[:, pl.ds(w * width, width)], full, w_sem.at[w])
+        for w, full in enumerate((gate_w, up_w, down_w))
     ]
-    late = [pltpu.make_async_copy(other_in, other_ref, w_sem.at[5])] + [
-        pltpu.make_async_copy(block, blocks.at[k], w_sem.at[6 + k])
+    late = [pltpu.make_async_copy(other_in, other_ref, w_sem.at[4])] + [
+        pltpu.make_async_copy(block, blocks.at[k], w_sem.at[5 + k])
         for k, block in enumerate(blocks_in)
     ]
     for load in loads + late:
@@ -675,9 +605,8 @@
         fg[here, :] = grad
         gate = dot(n, gate_w[...])
         ready(2)
+        up = dot(n, up_w[...])
         ready(3)
-        up = dot(n, up_w[...])
-        ready(4)
         back = dot(grad, down_w[...])
         sig = 1.0 / (1.0 + jnp.exp(-gate))
         act = gate * sig
@@ -822,17 +751,17 @@
         copy.wait()
 
 
-def feedforward(count, n2, cotangent, middle, gain, weights, along_z, blocks, others):
+def feedforward(count, n2, cotangent, middle, gain, weights, blocks, others):
     tokens, model = n2.shape
     own = tokens // count
-    hidden = (weights.shape[1] + along_z.shape[1]) // 3
+    hidden = weights.shape[1] // 3
     width = blocks[0].shape[1]
     rows, steps = own // 2, count
     vmem, hbm = pl.BlockSpec(memory_space=pltpu.VMEM), pl.BlockSpec(memory_space=pl.ANY)
     sem = pltpu.SemaphoreType.DMA
     return pl.pallas_call(
         functools.partial(feedforward_kernel, count),
-        in_specs=[hbm, hbm, hbm, vmem, hbm, hbm, hbm] + [hbm] * (count // 2),
+        in_specs=[hbm, hbm, hbm, vmem, hbm, hbm] + [hbm] * (count // 2),
         out_specs=[hbm, vmem, vmem, vmem, hbm, hbm, hbm],
         out_shape=[
             jax.ShapeDtypeStruct((steps, rows, model), BF16),
@@ -859,7 +788,7 @@
             pltpu.VMEM((count, own, width), BF16),
             pltpu.VMEM(others.shape, BF16),
             pltpu.VMEM(others.shape, BF16),
-            sem((6 + count // 2,)), sem((2,)), sem((4,)),
+            sem((5 + count // 2,)), sem((2,)), sem((4,)),
             sem((2,)), sem((2,)), sem((steps - 2,)), sem((steps - 2,)),
             sem((2,)), sem((2,)), sem((count,)), sem((count,)), sem((1,)),
         ],
@@ -871,7 +800,7 @@
             transcendentals=tokens * hidden,
         ),
         name="feed_forward",
-    )(n2, cotangent, middle, gain, others, weights, along_z, *blocks)
+    )(n2, cotangent, middle, gain, others, weights, *blocks)
 
 
 def shard_copy(src, dst, send, recv, axis, index):
@@ -1421,9 +1350,7 @@
         )
         return pair.astype(F32)
 
-    cut = up_weight.shape[1] // 2
-    ff_half = half_of(jnp.concatenate([gate_weight, up_weight[:, :cut]], axis=1))
-    ff_later = jnp.concatenate([up_weight[:, cut:], down_weight.T], axis=1)
+    ff_half = half_of(jnp.concatenate([gate_weight, up_weight, down_weight.T], axis=1))
     gain_shard = jnp.stack([attention_gain, feedforward_gain]).astype(F32)
     gain_shard = jnp.pad(gain_shard, ((0, 6), (0, 0)))
     qkv_shard = jnp.concatenate([query_weight, key_matrix, value_matrix], axis=1)
@@ -1461,13 +1388,11 @@
         ends, base, queries, before, head_dim, 0, state, (widen_kv, marks, val_q)
     )
     wo = [out_own] + [lax.ppermute(out_own, "tp", chip_shift(k)) for k in range(1, chips)]
-    normed_two, middle, wo_others, ff_rest = mix(
-        ranks, shards, attended, layer_input, gain_two, ff_later, wo
-    )
+    normed_two, middle, wo_others = mix(ranks, attended, layer_input, gain_two, wo)
     (
         feed_sums, middle_grad, branch_grad, gain_two_grad, attended_grad, gate_part, feed_part,
     ) = feedforward(
-        ranks, normed_two, output_cotangent, middle, gain_two, ff_full, ff_rest, wo, wo_others
+        ranks, normed_two, output_cotangent, middle, gain_two, ff_full, wo, wo_others
     )
     gate_own, feed_own = reduce_fsdp(gate_part), reduce_fsdp(feed_part)
     cut = feed_sums.reshape(chips, own, model)

time: 528 us -> 525 us (level)
  Pallas kernels: 358 us -> 335 us
  waiting for transfers between devices: 75.5 us -> 97.3 us
    all_gather x1, waiting for transfers between devices: 0.01 us -> 29.4 us  [per_device(): ff_full = lax.all_gather(ff_half, both_axes, axis=0, tiled=True)]
    pallas_call x1, Pallas kernels: 76 us -> 48 us  [mix(): pl.pallas_call(functools.partial(mix_kernel, count), in_specs=[hbm, hbm,...]
    ppermute x1, waiting for transfers between devices: 18.9 us -> 11.1 us  [per_device(): before = lax.ppermute(dense_kv, 'ctx', [(0, 1)])]
    unnamed x113 -> x117, local copies, waits for them, and re-layouts: 29.3 us -> 29.7 us
  transfers between devices with their start and end apart: 12 -> 12, of which waited for: 6 -> 7; matrix products, arithmetic and copies ran while one was open for 6% -> 6% of each run, Pallas kernels for 45% -> 41%
where the time goes in v4:
time: 525 us; the launch traced here: 516 us
  Pallas kernels  335 us (64%)
  waiting for transfers between devices  97.3 us (19%)
  local copies, waits for them, and re-layouts  35.5 us (7%)
  other arithmetic  22.1 us (4%)
  between operations  14.6 us (3%)
  starting transfers between devices  12.2 us (2%)
    pallas_call x1, Pallas kernels, close(): pl.pallas_call(functools.partial(close_kernel, count, shards), in_specs=[...  84.8 us
    pallas_call x1, Pallas kernels, feedforward(): pl.pallas_call(functools.partial(feedforward_kernel, count), in_specs=[hb...  78.9 us
    pallas_call x1, Pallas kernels, mix(): pl.pallas_call(functools.partial(mix_kernel, count), in_specs=[hbm, hbm,...  48 us
    pallas_call x1, Pallas kernels, begin(): pl.pallas_call(functools.partial(begin_kernel, shards), in_specs=[hbm, vm...  44.7 us
    pallas_call x2, Pallas kernels, attention_backward(): pl.pallas_call(functools.partial(attention_backward_kernel, rest is None,...  35 us
    reduce_scatter x3, waiting for transfers between devices, reduce_fsdp(): return lax.psum_scatter(part, 'fsdp', scatter_dimension=0, tiled=True)  31.9 us
    unnamed x117, local copies, waits for them, and re-layouts  29.7 us
    all_gather x1, waiting for transfers between devices, per_device(): ff_full = lax.all_gather(ff_half, both_axes, axis=0, tiled=True)  29.4 us
  transfers between devices with their start and end apart: 12, of which 7 were waited for; matrix products, arithmetic and copies ran while one was open for 6% of the time, Pallas kernels for 41%

profile of v4, /device:TPU:0, one launch (start us, length us, event | category | flops | bytes accessed | tf_op | source)
XLA Modules:
  0.0 516.4 jit_solution(13232317044567706354)
XLA Ops:
  14.5 44.7 %norm_and_gather.1 = (bf16[1536,1536]{1,0:T(8,128)(2,1)}, bf16[1536,768]{1,0:T(8,128)(2,1)S(1)}, bf16[1536,384]{1,0:T(8,128)(2,1)S(1)}, f32[8,1536]{1,0:T(8,128)S(1)}) custom-call(f32[1536,1536]{1,0:T(8,128)} %x_ref.5, bf16[384,768]{1,0:T(8,128)(2,1)S(1)} %copy-done.2, bf16[384,384]{1,0:T(8,128)(2,1)S(1)} %bitcast.17, f32[8,384]{1,0:T(8,128)S(1)} %fusion.11.gains_ref, ...), custom_call_target="tpu_custom_call" | custom-call | bytes 125829120 | tf_op jit(solution)/shard_map/norm_and_gather/pallas_call | solution.py:949
  61.3 2.8 fusion.7
  65.7 11.7 %project_qkv.1 = (bf16[1536,512]{1,0:T(8,128)(2,1)S(1)}, bf16[1536,512]{1,0:T(8,128)(2,1)S(1)}, bf16[1536,384]{1,0:T(8,128)(2,1)S(1)}) custom-call(bf16[1536,1536]{1,0:T(8,128)(2,1)} %get-tuple-element.49.n_ref, bf16[1536,768]{1,0:T(8,128)(2,1)S(1)} %get-tuple-element.50.qkv_ref.w_ref, bf16[768,1024]{1,0:T(8,128)(2,1)S(1)} %copy-done.22, ...), custom_call_target="tpu_custom_call" | custom-call | flops 4831838208 | bytes 16777216 | tf_op jit(solution)/shard_map/project_qkv/pallas_call | solution.py:1010
  77.4 2.9 collective-permute-start
  82.9 12.7 %attention_forward.2 = (f32[3,2,1,1024]{3,2,1,0:T(1,128)S(1)}, f32[3,2,128,1024]{3,2,1,0:T(8,128)S(1)}) custom-call(s32[3]{0:T(128)S(1)} %get-tuple-element.127.ends_ref, s32[1]{0:T(128)} %bitcast.2.base_ref, bf16[1536,512]{1,0:T(8,128)(2,1)S(1)} %get-tuple-element.51.q_ref, bf16[1536,512]{1,0:T(8,128)(2,1)S(1)} %get-tuple-element.53.kv_ref), custom_call_target="tpu_custom_call" | custom-call | flops 4831838208 | bytes 8388608 | tf_op jit(solution)/shard_map/attention_forward/pallas_call | solution.py:210
  95.6 11.1 %collective-permute-done.kv_ref = bf16[1536,384]{1,0:T(8,128)(2,1)S(1)} collective-permute-done((bf16[1536,384]{1,0:T(8,128)(2,1)S(1)}, bf16[1536,384]{1,0:T(8,128)(2,1)S(1)}, u32[]{:S(2)}, u32[]{:S(2)}) %collective-permute-start) | collective-permute-done | bytes 1179680 | tf_op jit(solution)/shard_map/ppermute | solution.py:1382
  106.7 5.4 %attention_forward.3 = (bf16[1536,384]{1,0:T(8,128)(2,1)S(1)}, bf16[1536,512]{1,0:T(8,128)(2,1)S(1)}) custom-call(s32[3]{0:T(128)S(1)} %get-tuple-element.127.ends_ref, s32[1]{0:T(128)} %bitcast.2.base_ref, bf16[1536,512]{1,0:T(8,128)(2,1)S(1)} %get-tuple-element.51.q_ref, bf16[1536,384]{1,0:T(8,128)(2,1)S(1)} %collective-permute-done.kv_ref, ...), custom_call_target="tpu_custom_call" | custom-call | flops 4831838208 | bytes 8388608 | tf_op jit(solution)/shard_map/attention_forward/pallas_call | solution.py:210
  113.3 48.0 %mix_heads.1 = (bf16[1536,1536]{1,0:T(8,128)(2,1)S(1)}, f32[384,1536]{1,0:T(8,128)S(1)}, bf16[2,1536,384]{2,1,0:T(8,128)(2,1)S(1)}) custom-call(bf16[1536,384]{1,0:T(8,128)(2,1)S(1)} %get-tuple-element.56.att_ref.o_ref, f32[1536,1536]{1,0:T(8,128)} %x_ref.5, f32[1,1536]{1,0:T(1,128)S(1)} %get-tuple-element.122.gain_ref, bf16[1536,384]{1,0:T(8,128)(2,1)S(1)} %copy-done.17, ...), custom_call_target="tpu_custom_call" | custom-call | flops 7247757312 | bytes 157286400 | tf_op jit(solution)/shard_map/mix_heads/pallas_call | solution.py:502
  164.9 2.2 copy-done.37
  168.5 29.4 %all-gather.2.cloned.1.call-done.weight_ref = bf16[1536,3072]{1,0:T(8,128)(2,1)} async-done(((bf16[192,3072]{1,0:T(8,128)(2,1)}), bf16[1536,3072]{1,0:T(8,128)(2,1)}) %all-gather.2.cloned.1.call-update) | async-done | bytes 9437200 | tf_op jit(solution)/shard_map/all_gather | solution.py:1380
  197.8 78.9 %feed_forward.1 = (bf16[4,192,1536]{2,1,0:T(8,128)(2,1)}, f32[384,1536]{1,0:T(8,128)}, bf16[384,1536]{1,0:T(8,128)(2,1)}, f32[1,1536]{1,0:T(1,128)}, bf16[1536,3...) custom-call(bf16[1536,1536]{1,0:T(8,128)(2,1)} %copy-done.37, f32[1536,1536]{1,0:T(8,128)} %cot_ref.1, ...), custom_call_target="tpu_custom_call" | custom-call | flops 43486543872 | bytes 293601280 | tf_op jit(solution)/shard_map/feed_forward/pallas_call | solution.py:762
  281.5 6.2 %attention_backward.2 = (f32[1536,512]{1,0:T(8,128)}, bf16[1536,512]{1,0:T(8,128)(2,1)S(1)}) custom-call(s32[3]{0:T(128)S(1)} %get-tuple-element.127.ends_ref, s32[1]{0:T(128)} %bitcast.2.base_ref, bf16[1536,512]{1,0:T(8,128)(2,1)} %copy-done.38, bf16[1536,384]{1,0:T(8,128)(2,1)S(1)} %copy-done.40, bf16[1536,384]{1,0:T(8,128)(2,1)S(1)} %copy-done.35, ...), custom_call_target="tpu_custom_call" | custom-call | flops 12079595520 | bytes 12582912 | tf_op jit(solution)/shard_map/attention_backward/pallas_call | solution.py:336
  290.2 28.9 %attention_backward.3 = (bf16[1536,384]{1,0:T(8,128)(2,1)S(1)}, f32[1536,512]{1,0:T(8,128)}) custom-call(s32[3]{0:T(128)S(1)} %get-tuple-element.127.ends_ref, s32[1]{0:T(128)} %bitcast.2.base_ref, bf16[1536,512]{1,0:T(8,128)(2,1)} %copy-done.38, bf16[1536,384]{1,0:T(8,128)(2,1)S(1)} %copy-done.40, bf16[1536,384]{1,0:T(8,128)(2,1)S(1)} %copy-done.35, ...), custom_call_target="tpu_custom_call" | custom-call | flops 12079595520 | bytes 12582912 | tf_op jit(solution)/shard_map/attention_backward/pallas_call | solution.py:336
  321.8 12.4 %collective-permute-done.4.rest_1_ = bf16[384,1536]{1,0:T(8,128)(2,1)} collective-permute-done((bf16[384,1536]{1,0:T(8,128)(2,1)S(1)}, bf16[384,1536]{1,0:T(8,128)(2,1)}, u32[]{:S(2)}, u32[]{:S(2)}) %collective-permute-start.4) | collective-permute-done | bytes 1179680 | tf_op jit(solution)/shard_map/ppermute | solution.py:1417
  335.4 13.4 %dense_gradients.1 = (bf16[1536,768]{1,0:T(8,128)(2,1)}, bf16[1536,1152]{1,0:T(8,128)(2,1)}) custom-call(bf16[1536,384]{1,0:T(8,128)(2,1)S(1)} %get-tuple-element.69.dq_ref, f32[1536,512]{1,0:T(8,128)} %get-tuple-element.70.dkv_ref, bf16[1536,512]{1,0:T(8,128)(2,1)} %copy-done.51, f32[1536,128]{1,0:T(8,128)S(1)} %copy-done.12, f32[1536,128]{1,0:T(8,128)S(1)} %copy-done.10, ...), custom_call_target="tpu_custom_call" | custom-call | flops 5435817984 | bytes 25165824 | tf_op jit(solution)/shard_map/dense_gradients/pallas_call | solution.py:1076
  348.8 8.7 %collective-permute-done.5.rest_1_ = bf16[384,1536]{1,0:T(8,128)(2,1)S(1)} collective-permute-done((bf16[384,1536]{1,0:T(8,128)(2,1)S(1)}, bf16[384,1536]{1,0:T(8,128)(2,1)S(1)}, u32[]{:S(2)}, u32[]{:S(2)}) %collective-permute-start.5) | collective-permute-done | bytes 1179680 | tf_op jit(solution)/shard_map/ppermute | solution.py:1417
  360.9 84.8 %close_layer.1 = (bf16[1536,1536]{1,0:T(8,128)(2,1)}, f32[8,1536]{1,0:T(8,128)S(1)}, bf16[768,1152]{1,0:T(8,128)(2,1)}, bf16[1536,1536]{1,0:T(8,128)(2,1)}, f32[384,1024]{1,0:T(8,128)S(1)}) custom-call(bf16[1536,768]{1,0:T(8,128)(2,1)} %get-tuple-element.73.dense_ref, bf16[1536,768]{1,0:T(8,128)(2,1)} %copy-done.1, f32[1536,1536]{1,0:T(8,128)} %x_ref.5, ...), custom_call_target="tpu_custom_call" | custom-call | flops 3623878656 | bytes 209715200 | tf_op jit(solution)/shard_map/close_layer/pallas_call | solution.py:1253
  445.7 5.7 %reduce-scatter.6.cloned.1.call-done = bf16[384,2048]{1,0:T(8,128)(2,1)} async-done(((bf16[1536,2048]{1,0:T(8,128)(2,1)}), bf16[384,2048]{1,0:T(8,128)(2,1)}) %reduce-scatter.6.cloned.1.call-update) | async-done | bytes 1572880 | tf_op jit(solution)/shard_map/reduce_scatter | solution.py:1341
  452.9 7.6 %convert_element_type.46 = f32[1536,1536]{1,0:T(8,128)} convert(bf16[1536,1536]{1,0:T(8,128)(2,1)} %get-tuple-element.79) | non-fusion elementwise | flops 2359296 | bytes 14155776 | tf_op jit(solution)/shard_map/convert_element_type | solution.py:1429
  460.5 5.1 convert_element_type.47
  466.2 26.2 %reduce-scatter.8.cloned.1.call-done = bf16[192,1152]{1,0:T(8,128)(2,1)} async-done(((bf16[768,1152]{1,0:T(8,128)(2,1)}), bf16[192,1152]{1,0:T(8,128)(2,1)}) %reduce-scatter.8.cloned.1.call-update) | async-done | bytes 442384 | tf_op jit(solution)/shard_map/reduce_scatter | solution.py:1341
  493.9 2.5 convert_add_fusion
  498.3 3.1 copy.49
  501.4 3.0 collective-permute-done.6
  (158 shorter events, 44.5 us)
Async XLA Ops:
  7.2 190.6 %all-gather.2.cloned.1.call-start = ((), (), s32[]{:S(2)}) async-start(), calls=%async_computation.3 | async-start | bytes 10616832 | tf_op jit(solution)/shard_map/all_gather | solution.py:1380
  12.0 47.1 %copy-start = (bf16[192,3072]{1,0:T(8,128)(2,1)}, bf16[192,3072]{1,0:T(8,128)(2,1)S(1)}, u32[]{:S(2)}) copy-start(bf16[192,3072]{1,0:T(8,128)(2,1)S(1)} %fusion.3.order_ref) | copy-start | bytes 3538948
  14.5 46.4 %copy-start.50 = (s32[1,3]{1,0:T(1,128)S(1)}, s32[1,3]{1,0:T(1,128)}, u32[]{:S(2)}) copy-start(s32[1,3]{1,0:T(1,128)} %param.24) | copy-start | bytes 40
  60.9 297.7 %reduce-scatter.4.cloned.1.call-start = ((), (), s32[]{:S(2)}) async-start(), calls=%async_computation.4 | async-start | bytes 3932160 | tf_op jit(solution)/shard_map/reduce_scatter | solution.py:1341
  65.7 14.6 %copy-start.17 = (bf16[1536,384]{1,0:T(8,128)(2,1)S(1)}, bf16[1536,384]{1,0:T(8,128)(2,1)}, u32[]{:S(2)}) copy-start(bf16[1536,384]{1,0:T(8,128)(2,1)} %copy-done.16) | copy-start | bytes 3538948
  77.4 18.2 %copy-start.36 = (bf16[1536,512]{1,0:T(8,128)(2,1)}, bf16[1536,512]{1,0:T(8,128)(2,1)S(1)}, u32[]{:S(2)}) copy-start(bf16[1536,512]{1,0:T(8,128)(2,1)S(1)} %get-tuple-element.53.kv_ref) | copy-start | bytes 4718596
  77.4 29.3 %collective-permute-start = (bf16[1536,384]{1,0:T(8,128)(2,1)S(1)}, bf16[1536,384]{1,0:T(8,128)(2,1)S(1)}, u32[]{:S(2)}, u32[]{:S(2)}) collective-permute-start(bf16[1536,384]{1,0:T(8,128)(2,1)S(1)} %get-tuple-element.52), channel_id=1, source_target_pairs={{0,4},{1,5},{2,6},{3,7},{8,12},{9,13},{10,14},{11,15},{16,20},{17,... | collective-permute-start | bytes 3538952 | tf_op jit(solution)/shard_map/ppermute | solution.py:1382
  80.3 33.0 %collective-permute-start.1 = (bf16[1536,384]{1,0:T(8,128)(2,1)S(1)}, bf16[1536,384]{1,0:T(8,128)(2,1)S(1)}, u32[]{:S(2)}, u32[]{:S(2)}) collective-permute-start(bf16[1536,384]{1,0:T(8,128)(2,1)S(1)} %copy-done.17), channel_id=1, source_target_pairs={{0,2},{1,3},{2,0},{3,1},{4,6},{5,7},{6,4},{7,5},{8,10},{9,11},{10,... | collective-permute-start | bytes 3538952 | tf_op jit(solution)/shard_map/ppermute | solution.py:1390
  82.8 30.5 %copy-start.14 = (f32[1,1536]{1,0:T(1,128)}, f32[1,1536]{1,0:T(1,128)S(1)}, u32[]{:S(2)}) copy-start(f32[1,1536]{1,0:T(1,128)S(1)} %get-tuple-element.122.gain_ref) | copy-start | bytes 18436
  82.8 23.9 %copy-start.25 = (bf16[384,512]{1,0:T(8,128)(2,1)S(1)}, bf16[384,512]{1,0:T(8,128)(2,1)}, u32[]{:S(2)}) copy-start(bf16[384,512]{1,0:T(8,128)(2,1)} %constant.63.clone.rest_0_) | copy-start | bytes 1179652
  82.9 23.9 %copy-start.27 = (bf16[512,384]{1,0:T(8,128)(2,1)S(1)}, bf16[512,384]{1,0:T(8,128)(2,1)}, u32[]{:S(2)}) copy-start(bf16[512,384]{1,0:T(8,128)(2,1)} %constant.65.clone.rest_2_) | copy-start | bytes 1179652
  82.9 23.9 %copy-start.31 = (f32[1,512]{1,0:T(1,128)S(1)}, f32[1,512]{1,0:T(1,128)}, u32[]{:S(2)}) copy-start(f32[1,512]{1,0:T(1,128)} %constant.64.clone.rest_1_) | copy-start | bytes 6148
  276.8 174.6 %reduce-scatter.6.cloned.1.call-start = ((), (), s32[]{:S(2)}) async-start(), calls=%async_computation.5 | async-start | bytes 7864320 | tf_op jit(solution)/shard_map/reduce_scatter | solution.py:1341
  277.5 215.0 %reduce-scatter.8.cloned.1.call-start = ((), (), s32[]{:S(2)}) async-start(), calls=%async_computation.6 | async-start | bytes 2211840 | tf_op jit(solution)/shard_map/reduce_scatter | solution.py:1341
  279.8 39.3 %collective-permute-start.2 = (bf16[384,1536]{1,0:T(8,128)(2,1)}, bf16[384,1536]{1,0:T(8,128)(2,1)}, u32[]{:S(2)}, u32[]{:S(2)}) collective-permute-start(bf16[384,1536]{1,0:T(8,128)(2,1)} %bitcast.6), channel_id=1, source_target_pairs={{0,2},{1,3},{2,0},{3,1},{4,6},{5,7},{6,4},{7,5},{8,10},{9,11},{10,... | collective-permute-start | bytes 3538952 | tf_op jit(solution)/shard_map/ppermute | solution.py:1399
  287.7 46.5 %collective-permute-start.3 = (bf16[1536,512]{1,0:T(8,128)(2,1)S(1)}, bf16[1536,512]{1,0:T(8,128)(2,1)S(1)}, u32[]{:S(2)}, u32[]{:S(2)}) collective-permute-start(bf16[1536,512]{1,0:T(8,128)(2,1)S(1)} %get-tuple-element.71), channel_id=1, source_target_pairs={{4,0},{5,1},{6,2},{7,3},{12,8},{13,9},{14,10},{15,11},{20,16},{21,... | collective-permute-start | bytes 4718600 | tf_op jit(solution)/shard_map/ppermute | solution.py:1404
  289.0 45.2 %collective-permute-start.4 = (bf16[384,1536]{1,0:T(8,128)(2,1)S(1)}, bf16[384,1536]{1,0:T(8,128)(2,1)}, u32[]{:S(2)}, u32[]{:S(2)}) collective-permute-start(bf16[384,1536]{1,0:T(8,128)(2,1)S(1)} %copy-done.18), channel_id=1, source_target_pairs={{0,2},{1,3},{2,0},{3,1},{4,6},{5,7},{6,4},{7,5},{8,10},{9,11},{10,... | collective-permute-start | bytes 3538952 | tf_op jit(solution)/shard_map/ppermute | solution.py:1417
  290.2 28.9 %copy-start.4 = (f32[384,1536]{1,0:T(8,128)S(1)}, f32[384,1536]{1,0:T(8,128)}, u32[]{:S(2)}) copy-start(f32[384,1536]{1,0:T(8,128)} %copy-done.3) | copy-start | bytes 7077892
  319.1 16.3 %copy-start.29 = (bf16[256,192]{1,0:T(8,128)(2,1)S(1)}, bf16[256,192]{1,0:T(8,128)(2,1)}, u32[]{:S(2)}) copy-start(bf16[256,192]{1,0:T(8,128)(2,1)} %constant.68.clone.rotk_ref) | copy-start | bytes 294916
  319.1 16.3 %copy-start.30 = (bf16[256,192]{1,0:T(8,128)(2,1)S(1)}, bf16[256,192]{1,0:T(8,128)(2,1)}, u32[]{:S(2)}) copy-start(bf16[256,192]{1,0:T(8,128)(2,1)} %constant.69.clone.valk_ref) | copy-start | bytes 294916
  320.9 36.7 %collective-permute-start.5 = (bf16[384,1536]{1,0:T(8,128)(2,1)S(1)}, bf16[384,1536]{1,0:T(8,128)(2,1)S(1)}, u32[]{:S(2)}, u32[]{:S(2)}) collective-permute-start(bf16[384,1536]{1,0:T(8,128)(2,1)S(1)} %fusion.1.rest_0_), channel_id=1, source_target_pairs={{0,2},{1,3},{2,0},{3,1},{4,6},{5,7},{6,4},{7,5},{8,10},{9,11},{10,... | collective-permute-start | bytes 3538952 | tf_op jit(solution)/shard_map/ppermute | solution.py:1417
  335.4 23.1 %copy-start.13 = (f32[1,1536]{1,0:T(1,128)S(1)}, f32[1,1536]{1,0:T(1,128)}, u32[]{:S(2)}) copy-start(f32[1,1536]{1,0:T(1,128)} %get-tuple-element.75.gain_two_ref) | copy-start | bytes 18436
  451.4 42.5 %collective-permute-start.7 = (bf16[384,2048]{1,0:T(8,128)(2,1)}, bf16[384,2048]{1,0:T(8,128)(2,1)}, u32[]{:S(2)}, u32[]{:S(2)}) collective-permute-start(bf16[384,2048]{1,0:T(8,128)(2,1)} %reduce-scatter.6.cloned.1.call-done), channel_id=1, source_target_pairs={{0,4},{4,0},{1,5},{5,1},{2,6},{6,2},{3,7},{7,3},{8,12},{12,8},{9,1... | collective-permute-start | bytes 4718600 | tf_op jit(solution)/shard_map/ppermute | solution.py:1344
  492.5 11.9 %collective-permute-start.6 = (bf16[192,1152]{1,0:T(8,128)(2,1)}, bf16[192,1152]{1,0:T(8,128)(2,1)S(1)}, u32[]{:S(2)}, u32[]{:S(2)}) collective-permute-start(bf16[192,1152]{1,0:T(8,128)(2,1)} %reduce-scatter.8.cloned.1.call-done), channel_id=1, source_target_pairs={{0,4},{4,0},{1,5},{5,1},{2,6},{6,2},{3,7},{7,3},{8,12},{12,8},{9,1... | collective-permute-start | bytes 1327112 | tf_op jit(solution)/shard_map/ppermute | solution.py:1347
  (42 other events, 153.9 us)
Sparse Core Ops, SparseCore 0:
  61.0 136.7 all-gather.1
  276.9 58.1 reduce-scatter.3
  337.4 113.9 reduce-scatter.5
  453.5 38.8 reduce-scatter.7

commit v5 on v4

--- a/solution.py
+++ b/solution.py
@@ -560,7 +560,7 @@
     pl.semaphore_wait(sem, count)
 
 
-def feedforward_kernel(count, n2_ref, cot_ref, mid_ref, gain_ref, other_in, weight_ref, *rest):
+def feedforward_kernel(count, n2_ref, cot_ref, mid_ref, gain_ref, other_in, weight_ref, ff_ref, *rest):
     blocks_in, rest = rest[: count // 2], rest[count // 2 :]
     (
         ffb_ref, mg_ref, bg_ref, gain_grad_ref, da_ref, grad_ref, grads_ref,
@@ -575,12 +575,18 @@
     steps = ranks.chips * halves
     width = gate_w.shape[1]
     model = n2.shape[1]
-    loads = [pltpu.make_async_copy(n2_ref, n2, w_sem.at[3])] + [
-        pltpu.make_async_copy(weight_ref.at[:, pl.ds(w * width, width)], full, w_sem.at[w])
-        for w, full in enumerate((gate_w, up_w, down_w))
+    cut = width - ff_ref.shape[1]
+    loads = [
+        pltpu.make_async_copy(n2_ref, n2, w_sem.at[0]),
+        pltpu.make_async_copy(weight_ref.at[:, pl.ds(0, width)], gate_w, w_sem.at[1]),
+        pltpu.make_async_copy(weight_ref.at[:, pl.ds(width, width)], up_w, w_sem.at[2]),
+        pltpu.make_async_copy(
+            weight_ref.at[:, pl.ds(2 * width, cut)], down_w.at[:, pl.ds(0, cut)], w_sem.at[3]
+        ),
+        pltpu.make_async_copy(ff_ref, down_w.at[:, pl.ds(cut, width - cut)], w_sem.at[4]),
     ]
-    late = [pltpu.make_async_copy(other_in, other_ref, w_sem.at[4])] + [
-        pltpu.make_async_copy(block, blocks.at[k], w_sem.at[5 + k])
+    late = [pltpu.make_async_copy(other_in, other_ref, w_sem.at[5])] + [
+        pltpu.make_async_copy(block, blocks.at[k], w_sem.at[6 + k])
         for k, block in enumerate(blocks_in)
     ]
     for load in loads + late:
@@ -607,6 +613,7 @@
         ready(2)
         up = dot(n, up_w[...])
         ready(3)
+        ready(4)
         back = dot(grad, down_w[...])
         sig = 1.0 / (1.0 + jnp.exp(-gate))
         act = gate * sig
@@ -751,17 +758,17 @@
         copy.wait()
 
 
-def feedforward(count, n2, cotangent, middle, gain, weights, blocks, others):
+def feedforward(count, n2, cotangent, middle, gain, weights, first, blocks, others):
     tokens, model = n2.shape
     own = tokens // count
-    hidden = weights.shape[1] // 3
+    hidden = (weights.shape[1] + first.shape[1]) // 3
     width = blocks[0].shape[1]
     rows, steps = own // 2, count
     vmem, hbm = pl.BlockSpec(memory_space=pltpu.VMEM), pl.BlockSpec(memory_space=pl.ANY)
     sem = pltpu.SemaphoreType.DMA
     return pl.pallas_call(
         functools.partial(feedforward_kernel, count),
-        in_specs=[hbm, hbm, hbm, vmem, hbm, hbm] + [hbm] * (count // 2),
+        in_specs=[hbm, hbm, hbm, vmem, hbm, hbm, hbm] + [hbm] * (count // 2),
         out_specs=[hbm, vmem, vmem, vmem, hbm, hbm, hbm],
         out_shape=[
             jax.ShapeDtypeStruct((steps, rows, model), BF16),
@@ -788,7 +795,7 @@
             pltpu.VMEM((count, own, width), BF16),
             pltpu.VMEM(others.shape, BF16),
             pltpu.VMEM(others.shape, BF16),
-            sem((5 + count // 2,)), sem((2,)), sem((4,)),
+            sem((6 + count // 2,)), sem((2,)), sem((4,)),
             sem((2,)), sem((2,)), sem((steps - 2,)), sem((steps - 2,)),
             sem((2,)), sem((2,)), sem((count,)), sem((count,)), sem((1,)),
         ],
@@ -800,7 +807,7 @@
             transcendentals=tokens * hidden,
         ),
         name="feed_forward",
-    )(n2, cotangent, middle, gain, others, weights, *blocks)
+    )(n2, cotangent, middle, gain, others, weights, first, *blocks)
 
 
 def shard_copy(src, dst, send, recv, axis, index):
@@ -811,12 +818,13 @@
 
 
 def begin_kernel(
-    shards, x_ref, qkv_ref, wo_ref, gains_ref, order_ref, n_ref, qkv_full_ref, wo_full_ref, gain_out_ref,
-    qkv_full, wo_full, normed, rows_in, gain_buf, zs, zr, xs, xr, gs, gr, own_sem, in_sem, out_sem,
+    shards, x_ref, qkv_ref, wo_ref, ff_ref, gains_ref, order_ref, n_ref, qkv_full_ref, wo_full_ref,
+    ff_full_ref, gain_out_ref, qkv_full, wo_full, ff_full, normed, rows_in, gain_buf, zs, zr, xs, xr, gs, gr, own_sem, in_sem, out_sem,
 ):
     del order_ref
     me, piece = lax.axis_index("fsdp"), lax.axis_index("ctx")
-    fulls, sources = (qkv_full, wo_full), (qkv_ref, wo_ref)
+    fulls, sources = (qkv_full, wo_full, ff_full), (qkv_ref, wo_ref, ff_ref)
+    arrays = range(len(fulls))
     shard = qkv_ref.shape[0]
     half = shard // 2
     tokens = normed.shape[0]
@@ -835,7 +843,7 @@
     ]
     for copy in keeps:
         copy.start()
-    keep_gain = pltpu.make_async_copy(gains_ref, gain_buf.at[me], own_sem.at[2])
+    keep_gain = pltpu.make_async_copy(gains_ref, gain_buf.at[me], own_sem.at[3])
     keep_gain.start()
     barrier = pltpu.get_barrier_semaphore()
     for k in range(1, shards):
@@ -872,7 +880,7 @@
     ]
     for copy in gain_copies:
         copy.start()
-    for a in range(2):
+    for a in arrays:
         for step, there in ((1, me < shards - 1), (-1, me > 0)):
             @pl.when(there)
             def _():
@@ -900,13 +908,13 @@
 
         @pl.when(there)
         def _():
-            for a in range(2):
+            for a in arrays:
                 along(a, s, step, False).wait_recv()
                 across(a, s).start()
 
         @pl.when(there & onward)
         def _():
-            for a in range(2):
+            for a in arrays:
                 along(a, s, step, False).start()
 
     for d in range(1, shards):
@@ -916,15 +924,16 @@
         copy.wait()
     for k in range(1, shards):
         s = lax.rem(me + k, shards)
-        for a in range(2):
+        for a in arrays:
             across(a, s).wait_recv()
     writes = [
         pltpu.make_async_copy(qkv_full, qkv_full_ref, out_sem.at[1]),
         pltpu.make_async_copy(wo_full, wo_full_ref, out_sem.at[2]),
+        pltpu.make_async_copy(ff_full, ff_full_ref, out_sem.at[3]),
     ]
     for copy in writes:
         copy.start()
-    for a in range(2):
+    for a in arrays:
         for s in range(shards):
             @pl.when((me >= s) & (me < shards - 1))
             def _():
@@ -941,36 +950,38 @@
         copy.wait()
 
 
-def begin(shards, x, qkv, wo, gains, order):
+def begin(shards, x, qkv, wo, ff, gains, order):
     tokens, model = x.shape
     rows = math.gcd(tokens, 256)
     vmem, hbm = pl.BlockSpec(memory_space=pltpu.VMEM), pl.BlockSpec(memory_space=pl.ANY)
     sem = pltpu.SemaphoreType.DMA
     return pl.pallas_call(
         functools.partial(begin_kernel, shards),
-        in_specs=[hbm, vmem, vmem, vmem, hbm],
-        out_specs=[hbm, hbm, hbm, vmem],
+        in_specs=[hbm, vmem, vmem, vmem, vmem, hbm],
+        out_specs=[hbm, hbm, hbm, hbm, vmem],
         out_shape=[
             jax.ShapeDtypeStruct((tokens, model), BF16),
             jax.ShapeDtypeStruct((model, qkv.shape[1]), BF16),
             jax.ShapeDtypeStruct((model, wo.shape[1]), BF16),
+            jax.ShapeDtypeStruct((model, ff.shape[1]), BF16),
             jax.ShapeDtypeStruct((gains.shape[0], model), F32),
         ],
         scratch_shapes=[
             pltpu.VMEM((model, qkv.shape[1]), BF16),
             pltpu.VMEM((model, wo.shape[1]), BF16),
+            pltpu.VMEM((model, ff.shape[1]), BF16),
             pltpu.VMEM((tokens, model), BF16),
             pltpu.VMEM((2, rows, model), F32),
             pltpu.VMEM((shards,) + gains.shape, F32),
-            sem((2, 2, shards)), sem((2, shards)), sem((2, shards)), sem((2, shards)),
-            sem((shards,)), sem((shards,)), sem((3,)), sem((2,)), sem((3,)),
+            sem((3, 2, shards)), sem((3, shards)), sem((3, shards)), sem((3, shards)),
+            sem((shards,)), sem((shards,)), sem((4,)), sem((2,)), sem((4,)),
         ],
         compiler_params=pltpu.CompilerParams(
             vmem_limit_bytes=48 << 20, collective_id=4, has_side_effects=True
         ),
         cost_estimate=pl.CostEstimate(flops=0, bytes_accessed=120 << 20, transcendentals=0),
         name="norm_and_gather",
-    )(x, qkv, wo, gains, order)
+    )(x, qkv, wo, ff, gains, order)
 
 
 def project_kernel(
@@ -1350,7 +1361,9 @@
         )
         return pair.astype(F32)
 
-    ff_half = half_of(jnp.concatenate([gate_weight, up_weight, down_weight.T], axis=1))
+    cut = down_weight.shape[0] // 2
+    down_columns = down_weight.T
+    ff_half = half_of(jnp.concatenate([gate_weight, up_weight, down_columns[:, :cut]], axis=1))
     gain_shard = jnp.stack([attention_gain, feedforward_gain]).astype(F32)
     gain_shard = jnp.pad(gain_shard, ((0, 6), (0, 0)))
     qkv_shard = jnp.concatenate([query_weight, key_matrix, value_matrix], axis=1)
@@ -1368,8 +1381,8 @@
     spread[:q_width, :at_key] = rot_q.T
     spread[q_width : q_width + kv_width, at_key:at_value] = rot_k.T
     spread[q_width + kv_width :, at_value:] = val_k.T
-    normed_one, qkv_full, out_own, gains_full = begin(
-        shards, layer_input, qkv_shard, output_weight.T, gain_shard, ff_half
+    normed_one, qkv_full, out_own, ff_first, gains_full = begin(
+        shards, layer_input, qkv_shard, output_weight.T, down_columns[:, cut:], gain_shard, ff_half
     )
     widen_kv = np.ascontiguousarray(spread[q_width:, at_key:])
     marks = np.concatenate([krow] * kv_heads + [vrow] * kv_heads, axis=1)
@@ -1392,7 +1405,7 @@
     (
         feed_sums, middle_grad, branch_grad, gain_two_grad, attended_grad, gate_part, feed_part,
     ) = feedforward(
-        ranks, normed_two, output_cotangent, middle, gain_two, ff_full, wo, wo_others
+        ranks, normed_two, output_cotangent, middle, gain_two, ff_full, ff_first, wo, wo_others
     )
     gate_own, feed_own = reduce_fsdp(gate_part), reduce_fsdp(feed_part)
     cut = feed_sums.reshape(chips, own, model)

time: 525 us -> 518 us (0.987)
  waiting for transfers between devices: 97.3 us -> 73.1 us
  Pallas kernels: 335 us -> 358 us
    all_gather x1, waiting for transfers between devices: 29.4 us -> 12.1 us  [per_device(): ff_full = lax.all_gather(ff_half, both_axes, axis=0, tiled=True)]
    pallas_call x1, Pallas kernels: 44.7 us -> 58.7 us  [begin(): pl.pallas_call(functools.partial(begin_kernel, shards), in_specs=[hbm, vm...]
    ppermute x1, waiting for transfers between devices: 0.01 us -> 11.1 us  [per_device(): after = lax.ppermute(dkv_before, 'ctx', [(1, 0)])]
    ppermute x2, waiting for transfers between devices: 21.1 us -> 12.1 us  [from_chips(): lax.ppermute(rows, 'tp', chip_shift(k))]
    pallas_call x1, Pallas kernels: 84.8 us -> 92.8 us  [close(): pl.pallas_call(functools.partial(close_kernel, count, shards), in_specs=[...]
    reduce_scatter x3, waiting for transfers between devices: 31.9 us -> 25.5 us  [reduce_fsdp(): return lax.psum_scatter(part, 'fsdp', scatter_dimension=0, tiled=True)]
    unnamed x117 -> x105, local copies, waits for them, and re-layouts: 29.7 us -> 25.6 us
  transfers between devices with their start and end apart: 12 -> 12, of which waited for: 7 -> 6; matrix products, arithmetic and copies ran while one was open for 6% -> 6% of each run, Pallas kernels for 41% -> 43%
where the time goes in v5:
time: 518 us; the launch traced here: 511 us
  Pallas kernels  358 us (69%)
  waiting for transfers between devices  73.1 us (14%)
  local copies, waits for them, and re-layouts  31.3 us (6%)
  other arithmetic  23.3 us (4%)
  between operations  14.7 us (3%)
  starting transfers between devices  10.9 us (2%)
    pallas_call x1, Pallas kernels, close(): pl.pallas_call(functools.partial(close_kernel, count, shards), in_specs=[...  92.8 us
    pallas_call x1, Pallas kernels, feedforward(): pl.pallas_call(functools.partial(feedforward_kernel, count), in_specs=[hb...  79 us
    pallas_call x1, Pallas kernels, begin(): pl.pallas_call(functools.partial(begin_kernel, shards), in_specs=[hbm, vm...  58.7 us
    pallas_call x1, Pallas kernels, mix(): pl.pallas_call(functools.partial(mix_kernel, count), in_specs=[hbm, hbm,...  48 us
    pallas_call x2, Pallas kernels, attention_backward(): pl.pallas_call(functools.partial(attention_backward_kernel, rest is None,...  35.7 us
    unnamed x105, local copies, waits for them, and re-layouts  25.6 us
    reduce_scatter x3, waiting for transfers between devices, reduce_fsdp(): return lax.psum_scatter(part, 'fsdp', scatter_dimension=0, tiled=True)  25.5 us
    pallas_call x2, Pallas kernels, attention_forward(): pl.pallas_call(functools.partial(attention_forward_kernel, state is None,...  18.4 us
  transfers between devices with their start and end apart: 12, of which 6 were waited for; matrix products, arithmetic and copies ran while one was open for 6% of the time, Pallas kernels for 43%

profile of v5, /device:TPU:0, one launch (start us, length us, event | category | flops | bytes accessed | tf_op | source)
XLA Modules:
  0.0 511.2 jit_solution(4173681474197855234)
XLA Ops:
  11.7 58.7 %norm_and_gather.1 = (bf16[1536,1536]{1,0:T(8,128)(2,1)}, bf16[1536,768]{1,0:T(8,128)(2,1)}, bf16[1536,384]{1,0:T(8,128)(2,1)S(1)}, bf16[1536,512]{1,0:T(8,128)(2,1)S(1)}, f32[8,1536]{1,0:T(8,128)S(1)}) custom-call(f32[1536,1536]{1,0:T(8,128)} %x_ref.5, bf16[384,768]{1,0:T(8,128)(2,1)S(1)} %pad_maximum_fusion.4.qkv_ref, bf16[384,384]{1,0:T(8,128)(2,1)S(1)} %bitcast.17, ...), custom_call_target="tpu_custom_call" | custom-call | bytes 125829120 | tf_op jit(solution)/shard_map/norm_and_gather/pallas_call | solution.py:958
  73.1 2.8 fusion.7
  78.5 11.6 %project_qkv.1 = (bf16[1536,512]{1,0:T(8,128)(2,1)S(1)}, bf16[1536,512]{1,0:T(8,128)(2,1)S(1)}, bf16[1536,384]{1,0:T(8,128)(2,1)S(1)}) custom-call(bf16[1536,1536]{1,0:T(8,128)(2,1)} %get-tuple-element.50.n_ref, bf16[1536,768]{1,0:T(8,128)(2,1)S(1)} %copy-done.1, bf16[768,1024]{1,0:T(8,128)(2,1)S(1)} %copy-done.18, ...), custom_call_target="tpu_custom_call" | custom-call | flops 4831838208 | bytes 16777216 | tf_op jit(solution)/shard_map/project_qkv/pallas_call | solution.py:1021
  90.1 2.9 collective-permute-start
  94.7 13.0 %attention_forward.2 = (f32[3,2,1,1024]{3,2,1,0:T(1,128)S(1)}, f32[3,2,128,1024]{3,2,1,0:T(8,128)S(1)}) custom-call(s32[3]{0:T(128)S(1)} %get-tuple-element.131.ends_ref, s32[1]{0:T(128)} %bitcast.2.base_ref, bf16[1536,512]{1,0:T(8,128)(2,1)S(1)} %get-tuple-element.52.q_ref, bf16[1536,512]{1,0:T(8,128)(2,1)S(1)} %get-tuple-element.54.kv_ref), custom_call_target="tpu_custom_call" | custom-call | flops 4831838208 | bytes 8388608 | tf_op jit(solution)/shard_map/attention_forward/pallas_call | solution.py:210
  107.7 8.5 %collective-permute-done.kv_ref = bf16[1536,384]{1,0:T(8,128)(2,1)S(1)} collective-permute-done((bf16[1536,384]{1,0:T(8,128)(2,1)S(1)}, bf16[1536,384]{1,0:T(8,128)(2,1)S(1)}, u32[]{:S(2)}, u32[]{:S(2)}) %collective-permute-start) | collective-permute-done | bytes 1179680 | tf_op jit(solution)/shard_map/ppermute | solution.py:1395
  116.2 5.4 %attention_forward.3 = (bf16[1536,384]{1,0:T(8,128)(2,1)S(1)}, bf16[1536,512]{1,0:T(8,128)(2,1)S(1)}) custom-call(s32[3]{0:T(128)S(1)} %get-tuple-element.131.ends_ref, s32[1]{0:T(128)} %bitcast.2.base_ref, bf16[1536,512]{1,0:T(8,128)(2,1)S(1)} %get-tuple-element.52.q_ref, bf16[1536,384]{1,0:T(8,128)(2,1)S(1)} %collective-permute-done.kv_ref, ...), custom_call_target="tpu_custom_call" | custom-call | flops 4831838208 | bytes 8388608 | tf_op jit(solution)/shard_map/attention_forward/pallas_call | solution.py:210
  122.8 48.0 %mix_heads.1 = (bf16[1536,1536]{1,0:T(8,128)(2,1)S(1)}, f32[384,1536]{1,0:T(8,128)S(1)}, bf16[2,1536,384]{2,1,0:T(8,128)(2,1)S(1)}) custom-call(bf16[1536,384]{1,0:T(8,128)(2,1)S(1)} %get-tuple-element.57.att_ref.o_ref, f32[1536,1536]{1,0:T(8,128)} %x_ref.5, f32[1,1536]{1,0:T(1,128)S(1)} %get-tuple-element.126.gain_ref, bf16[1536,384]{1,0:T(8,128)(2,1)S(1)} %copy-done.13, ...), custom_call_target="tpu_custom_call" | custom-call | flops 7247757312 | bytes 157286400 | tf_op jit(solution)/shard_map/mix_heads/pallas_call | solution.py:502
  174.3 2.2 copy-done.33
  177.9 12.1 %all-gather.2.cloned.1.call-done.weight_ref = bf16[1536,2560]{1,0:T(8,128)(2,1)} async-done(((bf16[192,2560]{1,0:T(8,128)(2,1)}), bf16[1536,2560]{1,0:T(8,128)(2,1)}) %all-gather.2.cloned.1.call-update) | async-done | bytes 7864336 | tf_op jit(solution)/shard_map/all_gather | solution.py:1393
  190.0 79.0 %feed_forward.1 = (bf16[4,192,1536]{2,1,0:T(8,128)(2,1)}, f32[384,1536]{1,0:T(8,128)}, bf16[384,1536]{1,0:T(8,128)(2,1)}, f32[1,1536]{1,0:T(1,128)}, bf16[1536,3...) custom-call(bf16[1536,1536]{1,0:T(8,128)(2,1)} %copy-done.33, f32[1536,1536]{1,0:T(8,128)} %cot_ref.1, ...), custom_call_target="tpu_custom_call" | custom-call | flops 43486543872 | bytes 293601280 | tf_op jit(solution)/shard_map/feed_forward/pallas_call | solution.py:769
  269.9 1.9 fusion.12
  273.1 6.0 %attention_backward.2 = (f32[1536,512]{1,0:T(8,128)}, bf16[1536,512]{1,0:T(8,128)(2,1)S(1)}) custom-call(s32[3]{0:T(128)S(1)} %get-tuple-element.131.ends_ref, s32[1]{0:T(128)} %bitcast.2.base_ref, bf16[1536,512]{1,0:T(8,128)(2,1)} %copy-done.34, bf16[1536,384]{1,0:T(8,128)(2,1)S(1)} %copy-done.36, bf16[1536,384]{1,0:T(8,128)(2,1)S(1)} %copy-done.31, ...), custom_call_target="tpu_custom_call" | custom-call | flops 12079595520 | bytes 12582912 | tf_op jit(solution)/shard_map/attention_backward/pallas_call | solution.py:336
  281.4 29.7 %attention_backward.3 = (bf16[1536,384]{1,0:T(8,128)(2,1)S(1)}, f32[1536,512]{1,0:T(8,128)}) custom-call(s32[3]{0:T(128)S(1)} %get-tuple-element.131.ends_ref, s32[1]{0:T(128)} %bitcast.2.base_ref, bf16[1536,512]{1,0:T(8,128)(2,1)} %copy-done.34, bf16[1536,384]{1,0:T(8,128)(2,1)S(1)} %copy-done.36, bf16[1536,384]{1,0:T(8,128)(2,1)S(1)} %copy-done.31, ...), custom_call_target="tpu_custom_call" | custom-call | flops 12079595520 | bytes 12582912 | tf_op jit(solution)/shard_map/attention_backward/pallas_call | solution.py:336
  314.1 12.1 %collective-permute-done.4.rest_1_ = bf16[384,1536]{1,0:T(8,128)(2,1)} collective-permute-done((bf16[384,1536]{1,0:T(8,128)(2,1)S(1)}, bf16[384,1536]{1,0:T(8,128)(2,1)}, u32[]{:S(2)}, u32[]{:S(2)}) %collective-permute-start.4) | collective-permute-done | bytes 1179680 | tf_op jit(solution)/shard_map/ppermute | solution.py:1430
  326.1 11.1 %collective-permute-done.3.after_ref = bf16[1536,512]{1,0:T(8,128)(2,1)S(1)} collective-permute-done((bf16[1536,512]{1,0:T(8,128)(2,1)S(1)}, bf16[1536,512]{1,0:T(8,128)(2,1)S(1)}, u32[]{:S(2)}, u32[]{:S(2)}) %collective-permute-start.3) | collective-permute-done | bytes 1572896 | tf_op jit(solution)/shard_map/ppermute | solution.py:1417
  338.4 13.8 %dense_gradients.1 = (bf16[1536,768]{1,0:T(8,128)(2,1)}, bf16[1536,1152]{1,0:T(8,128)(2,1)}) custom-call(bf16[1536,384]{1,0:T(8,128)(2,1)S(1)} %get-tuple-element.71.dq_ref, f32[1536,512]{1,0:T(8,128)} %get-tuple-element.72.dkv_ref, bf16[1536,512]{1,0:T(8,128)(2,1)} %copy-done.45, f32[1536,128]{1,0:T(8,128)S(1)} %copy-done.8, ...), custom_call_target="tpu_custom_call" | custom-call | flops 5435817984 | bytes 25165824 | tf_op jit(solution)/shard_map/dense_gradients/pallas_call | solution.py:1087
  355.6 92.8 %close_layer.1 = (bf16[1536,1536]{1,0:T(8,128)(2,1)}, f32[8,1536]{1,0:T(8,128)S(1)}, bf16[768,1152]{1,0:T(8,128)(2,1)}, bf16[1536,1536]{1,0:T(8,128)(2,1)}, f32[384,1024]{1,0:T(8,128)S(1)}) custom-call(bf16[1536,768]{1,0:T(8,128)(2,1)} %get-tuple-element.75.dense_ref, bf16[1536,768]{1,0:T(8,128)(2,1)} %get-tuple-element.51.qkv_ref.w_ref, ...), custom_call_target="tpu_custom_call" | custom-call | flops 3623878656 | bytes 209715200 | tf_op jit(solution)/shard_map/close_layer/pallas_call | solution.py:1264
  448.6 7.6 %convert_element_type.46 = f32[1536,1536]{1,0:T(8,128)} convert(bf16[1536,1536]{1,0:T(8,128)(2,1)} %get-tuple-element.81) | non-fusion elementwise | flops 2359296 | bytes 14155776 | tf_op jit(solution)/shard_map/convert_element_type | solution.py:1442
  456.1 5.1 convert_element_type.47
  461.9 25.5 %reduce-scatter.8.cloned.1.call-done = bf16[192,1152]{1,0:T(8,128)(2,1)} async-done(((bf16[768,1152]{1,0:T(8,128)(2,1)}), bf16[192,1152]{1,0:T(8,128)(2,1)}) %reduce-scatter.8.cloned.1.call-update) | async-done | bytes 442384 | tf_op jit(solution)/shard_map/reduce_scatter | solution.py:1352
  488.8 2.5 convert_add_fusion
  493.2 3.1 copy.49
  496.2 3.0 collective-permute-done.6
  (147 shorter events, 38.2 us)
Async XLA Ops:
  7.2 182.8 %all-gather.2.cloned.1.call-start = ((), (), s32[]{:S(2)}) async-start(), calls=%async_computation.3 | async-start | bytes 8847360 | tf_op jit(solution)/shard_map/all_gather | solution.py:1393
  11.6 58.8 %copy-start = (bf16[192,2560]{1,0:T(8,128)(2,1)}, bf16[192,2560]{1,0:T(8,128)(2,1)S(1)}, u32[]{:S(2)}) copy-start(bf16[192,2560]{1,0:T(8,128)(2,1)S(1)} %fusion.3.order_ref) | copy-start | bytes 2949124
  11.6 61.0 %copy-start.44 = (s32[1,3]{1,0:T(1,128)S(1)}, s32[1,3]{1,0:T(1,128)}, u32[]{:S(2)}) copy-start(s32[1,3]{1,0:T(1,128)} %param.24) | copy-start | bytes 40
  72.6 280.6 %reduce-scatter.4.cloned.1.call-start = ((), (), s32[]{:S(2)}) async-start(), calls=%async_computation.4 | async-start | bytes 3932160 | tf_op jit(solution)/shard_map/reduce_scatter | solution.py:1352
  78.5 14.6 %copy-start.13 = (bf16[1536,384]{1,0:T(8,128)(2,1)S(1)}, bf16[1536,384]{1,0:T(8,128)(2,1)}, u32[]{:S(2)}) copy-start(bf16[1536,384]{1,0:T(8,128)(2,1)} %copy-done.12) | copy-start | bytes 3538948
  90.1 17.6 %copy-start.32 = (bf16[1536,512]{1,0:T(8,128)(2,1)}, bf16[1536,512]{1,0:T(8,128)(2,1)S(1)}, u32[]{:S(2)}) copy-start(bf16[1536,512]{1,0:T(8,128)(2,1)S(1)} %get-tuple-element.54.kv_ref) | copy-start | bytes 4718596
  90.1 26.1 %collective-permute-start = (bf16[1536,384]{1,0:T(8,128)(2,1)S(1)}, bf16[1536,384]{1,0:T(8,128)(2,1)S(1)}, u32[]{:S(2)}, u32[]{:S(2)}) collective-permute-start(bf16[1536,384]{1,0:T(8,128)(2,1)S(1)} %get-tuple-element.53), channel_id=1, source_target_pairs={{0,4},{1,5},{2,6},{3,7},{8,12},{9,13},{10,14},{11,15},{16,20},{17,... | collective-permute-start | bytes 3538952 | tf_op jit(solution)/shard_map/ppermute | solution.py:1395
  93.0 29.8 %collective-permute-start.1 = (bf16[1536,384]{1,0:T(8,128)(2,1)S(1)}, bf16[1536,384]{1,0:T(8,128)(2,1)S(1)}, u32[]{:S(2)}, u32[]{:S(2)}) collective-permute-start(bf16[1536,384]{1,0:T(8,128)(2,1)S(1)} %copy-done.13), channel_id=1, source_target_pairs={{0,2},{1,3},{2,0},{3,1},{4,6},{5,7},{6,4},{7,5},{8,10},{9,11},{10,... | collective-permute-start | bytes 3538952 | tf_op jit(solution)/shard_map/ppermute | solution.py:1403
  94.6 28.2 %copy-start.10 = (f32[1,1536]{1,0:T(1,128)}, f32[1,1536]{1,0:T(1,128)S(1)}, u32[]{:S(2)}) copy-start(f32[1,1536]{1,0:T(1,128)S(1)} %get-tuple-element.126.gain_ref) | copy-start | bytes 18436
  94.6 21.6 %copy-start.21 = (bf16[384,512]{1,0:T(8,128)(2,1)S(1)}, bf16[384,512]{1,0:T(8,128)(2,1)}, u32[]{:S(2)}) copy-start(bf16[384,512]{1,0:T(8,128)(2,1)} %constant.63.clone.rest_0_) | copy-start | bytes 1179652
  94.6 21.6 %copy-start.23 = (bf16[512,384]{1,0:T(8,128)(2,1)S(1)}, bf16[512,384]{1,0:T(8,128)(2,1)}, u32[]{:S(2)}) copy-start(bf16[512,384]{1,0:T(8,128)(2,1)} %constant.65.clone.rest_2_) | copy-start | bytes 1179652
  94.7 21.6 %copy-start.27 = (f32[1,512]{1,0:T(1,128)S(1)}, f32[1,512]{1,0:T(1,128)}, u32[]{:S(2)}) copy-start(f32[1,512]{1,0:T(1,128)} %constant.64.clone.rest_1_) | copy-start | bytes 6148
  269.0 179.4 %reduce-scatter.6.cloned.1.call-start = ((), (), s32[]{:S(2)}) async-start(), calls=%async_computation.5 | async-start | bytes 7864320 | tf_op jit(solution)/shard_map/reduce_scatter | solution.py:1352
  269.8 217.6 %reduce-scatter.8.cloned.1.call-start = ((), (), s32[]{:S(2)}) async-start(), calls=%async_computation.6 | async-start | bytes 2211840 | tf_op jit(solution)/shard_map/reduce_scatter | solution.py:1352
  271.8 39.3 %collective-permute-start.2 = (bf16[384,1536]{1,0:T(8,128)(2,1)S(1)}, bf16[384,1536]{1,0:T(8,128)(2,1)}, u32[]{:S(2)}, u32[]{:S(2)}) collective-permute-start(bf16[384,1536]{1,0:T(8,128)(2,1)S(1)} %bitcast.21), channel_id=1, source_target_pairs={{0,2},{1,3},{2,0},{3,1},{4,6},{5,7},{6,4},{7,5},{8,10},{9,11},{10,... | collective-permute-start | bytes 3538952 | tf_op jit(solution)/shard_map/ppermute | solution.py:1412
  279.1 58.1 %collective-permute-start.3 = (bf16[1536,512]{1,0:T(8,128)(2,1)S(1)}, bf16[1536,512]{1,0:T(8,128)(2,1)S(1)}, u32[]{:S(2)}, u32[]{:S(2)}) collective-permute-start(bf16[1536,512]{1,0:T(8,128)(2,1)S(1)} %get-tuple-element.73), channel_id=1, source_target_pairs={{4,0},{5,1},{6,2},{7,3},{12,8},{13,9},{14,10},{15,11},{20,16},{21,... | collective-permute-start | bytes 4718600 | tf_op jit(solution)/shard_map/ppermute | solution.py:1417
  280.4 45.7 %collective-permute-start.4 = (bf16[384,1536]{1,0:T(8,128)(2,1)S(1)}, bf16[384,1536]{1,0:T(8,128)(2,1)}, u32[]{:S(2)}, u32[]{:S(2)}) collective-permute-start(bf16[384,1536]{1,0:T(8,128)(2,1)S(1)} %copy-done.14), channel_id=1, source_target_pairs={{0,2},{1,3},{2,0},{3,1},{4,6},{5,7},{6,4},{7,5},{8,10},{9,11},{10,... | collective-permute-start | bytes 3538952 | tf_op jit(solution)/shard_map/ppermute | solution.py:1430
  281.4 29.7 %copy-start.3 = (f32[384,1536]{1,0:T(8,128)S(1)}, f32[384,1536]{1,0:T(8,128)}, u32[]{:S(2)}) copy-start(f32[384,1536]{1,0:T(8,128)} %copy-done.2) | copy-start | bytes 7077892
  311.1 27.3 %copy-start.25 = (bf16[256,192]{1,0:T(8,128)(2,1)S(1)}, bf16[256,192]{1,0:T(8,128)(2,1)}, u32[]{:S(2)}) copy-start(bf16[256,192]{1,0:T(8,128)(2,1)} %constant.68.clone.rotk_ref) | copy-start | bytes 294916
  311.1 27.3 %copy-start.26 = (bf16[256,192]{1,0:T(8,128)(2,1)S(1)}, bf16[256,192]{1,0:T(8,128)(2,1)}, u32[]{:S(2)}) copy-start(bf16[256,192]{1,0:T(8,128)(2,1)} %constant.69.clone.valk_ref) | copy-start | bytes 294916
  312.9 39.3 %collective-permute-start.5 = (bf16[384,1536]{1,0:T(8,128)(2,1)S(1)}, bf16[384,1536]{1,0:T(8,128)(2,1)S(1)}, u32[]{:S(2)}, u32[]{:S(2)}) collective-permute-start(bf16[384,1536]{1,0:T(8,128)(2,1)S(1)} %fusion.1.rest_0_), channel_id=1, source_target_pairs={{0,2},{1,3},{2,0},{3,1},{4,6},{5,7},{6,4},{7,5},{8,10},{9,11},{10,... | collective-permute-start | bytes 3538952 | tf_op jit(solution)/shard_map/ppermute | solution.py:1430
  338.4 14.8 %copy-start.9 = (f32[1,1536]{1,0:T(1,128)S(1)}, f32[1,1536]{1,0:T(1,128)}, u32[]{:S(2)}) copy-start(f32[1,1536]{1,0:T(1,128)} %get-tuple-element.77.gain_two_ref) | copy-start | bytes 18436
  448.5 40.3 %collective-permute-start.7 = (bf16[384,2048]{1,0:T(8,128)(2,1)}, bf16[384,2048]{1,0:T(8,128)(2,1)}, u32[]{:S(2)}, u32[]{:S(2)}) collective-permute-start(bf16[384,2048]{1,0:T(8,128)(2,1)} %reduce-scatter.6.cloned.1.call-done), channel_id=1, source_target_pairs={{0,4},{4,0},{1,5},{5,1},{2,6},{6,2},{3,7},{7,3},{8,12},{12,8},{9,1... | collective-permute-start | bytes 4718600 | tf_op jit(solution)/shard_map/ppermute | solution.py:1355
  487.3 12.0 %collective-permute-start.6 = (bf16[192,1152]{1,0:T(8,128)(2,1)}, bf16[192,1152]{1,0:T(8,128)(2,1)S(1)}, u32[]{:S(2)}, u32[]{:S(2)}) collective-permute-start(bf16[192,1152]{1,0:T(8,128)(2,1)} %reduce-scatter.8.cloned.1.call-done), channel_id=1, source_target_pairs={{0,4},{4,0},{1,5},{5,1},{2,6},{6,2},{3,7},{7,3},{8,12},{12,8},{9,1... | collective-permute-start | bytes 1327112 | tf_op jit(solution)/shard_map/ppermute | solution.py:1358
  (36 other events, 114.9 us)
Sparse Core Ops, SparseCore 0:
  72.7 117.1 all-gather.1
  269.1 60.2 reduce-scatter.3
  331.7 113.9 reduce-scatter.5
  448.6 38.7 reduce-scatter.7

commit v6 on v5

--- a/solution.py
+++ b/solution.py
@@ -564,7 +564,7 @@
     blocks_in, rest = rest[: count // 2], rest[count // 2 :]
     (
         ffb_ref, mg_ref, bg_ref, gain_grad_ref, da_ref, grad_ref, grads_ref,
-        gate_w, up_w, down_w, n2, fg, hid, gu, rows_in, ffb_out,
+        both_w, down_w, n2, fg, hid, gu, rows_in, ffb_out,
         c_send, c_recv, y_send, y_recv, f_send, f_recv, heads, other_ref, blocks,
         w_sem, in_sem, out_sem, cs, cr, ys, yr, fs, fr, hs, hr, local,
     ) = rest
@@ -573,13 +573,12 @@
     halves = 2
     rows = own // halves
     steps = ranks.chips * halves
-    width = gate_w.shape[1]
+    width = down_w.shape[1]
     model = n2.shape[1]
     cut = width - ff_ref.shape[1]
     loads = [
         pltpu.make_async_copy(n2_ref, n2, w_sem.at[0]),
-        pltpu.make_async_copy(weight_ref.at[:, pl.ds(0, width)], gate_w, w_sem.at[1]),
-        pltpu.make_async_copy(weight_ref.at[:, pl.ds(width, width)], up_w, w_sem.at[2]),
+        pltpu.make_async_copy(weight_ref.at[:, pl.ds(0, 2 * width)], both_w, w_sem.at[1]),
         pltpu.make_async_copy(
             weight_ref.at[:, pl.ds(2 * width, cut)], down_w.at[:, pl.ds(0, cut)], w_sem.at[3]
         ),
@@ -609,11 +608,10 @@
         n = n2[here, :]
         grad = rows_in[slot].astype(BF16)
         fg[here, :] = grad
-        gate = dot(n, gate_w[...])
+        gate = dot(n, both_w[:, :width])
+        up = dot(n, both_w[:, width:])
         ready(2)
-        up = dot(n, up_w[...])
         ready(3)
-        ready(4)
         back = dot(grad, down_w[...])
         sig = 1.0 / (1.0 + jnp.exp(-gate))
         act = gate * sig
@@ -623,7 +621,8 @@
         gu[here, :width] = gg
         ug = (back * act).astype(BF16)
         gu[here, width:] = ug
-        return dot(gg, gate_w[...], NT) + dot(ug, up_w[...], NT), dot(hidden, down_w[...], NT)
+        grad = dot(gg, both_w[:, :width], NT) + dot(ug, both_w[:, width:], NT)
+        return grad, dot(hidden, down_w[...], NT)
 
     read(scatter_order(ranks, halves, own, 0)[3], 0).start()
     ranks.barrier()
@@ -694,18 +693,21 @@
     ]
     for copy in fetch(0):
         copy.start()
-    cols = math.gcd(model, 384)
+    cols = math.gcd(model, 256)
     writes = []
 
-    def product(left, right, full, dst, n):
+    def product(left, right, full):
         for d in range(model // cols):
             full[d * cols : (d + 1) * cols, :] = dot(
                 left[:, d * cols : (d + 1) * cols], right, TN
             ).astype(BF16)
-        writes.append(pltpu.make_async_copy(full, dst, out_sem.at[1 + n]))
+
+    def write(src, dst):
+        writes.append(pltpu.make_async_copy(src, dst, out_sem.at[1 + len(writes)]))
         writes[-1].start()
 
-    product(n2, gu[:, :width], gate_w, grad_ref, 0)
+    product(fg, hid[...], down_w)
+    write(down_w, grads_ref.at[:, pl.ds(width, width)])
     gain = gain_ref[...]
     gain_total = None
     for u in range(halves):
@@ -743,8 +745,9 @@
     heads[0] = dot(bg_ref[...], blocks[0]).astype(BF16)
     keep = pltpu.make_async_copy(heads.at[0], da_ref.at[pl.ds(mine_at, own)], local.at[0])
     keep.start()
-    product(n2, gu[:, width:], up_w, grads_ref.at[:, pl.ds(0, width)], 1)
-    product(fg, hid[...], down_w, grads_ref.at[:, pl.ds(width, width)], 2)
+    product(n2, gu[...], both_w)
+    write(both_w.at[:, pl.ds(0, width)], grad_ref)
+    write(both_w.at[:, pl.ds(width, width)], grads_ref.at[:, pl.ds(0, width)])
     for i in (steps - 2, steps - 1):
         for copy in to_core(i):
             copy.wait_send()
@@ -779,7 +782,7 @@
             jax.ShapeDtypeStruct((model, hidden), BF16),
             jax.ShapeDtypeStruct((model, 2 * hidden), BF16),
         ],
-        scratch_shapes=[pltpu.VMEM((model, hidden), BF16)] * 3
+        scratch_shapes=[pltpu.VMEM((model, 2 * hidden), BF16), pltpu.VMEM((model, hidden), BF16)]
         + [
             pltpu.VMEM((tokens, model), BF16),
             pltpu.VMEM((tokens, model), BF16),

time: 518 us -> 519 us (level)
  Pallas kernels: 358 us -> 349 us
    ppermute x1, waiting for transfers between devices: 11.1 us -> 0.01 us  [per_device(): after = lax.ppermute(dkv_before, 'ctx', [(1, 0)])]
    ppermute x2, waiting for transfers between devices: 12.1 us -> 21.4 us  [from_chips(): lax.ppermute(rows, 'tp', chip_shift(k))]
    pallas_call x1, Pallas kernels: 92.8 us -> 85.2 us  [close(): pl.pallas_call(functools.partial(close_kernel, count, shards), in_specs=[...]
    reduce_scatter x3, waiting for transfers between devices: 25.5 us -> 31.7 us  [reduce_fsdp(): return lax.psum_scatter(part, 'fsdp', scatter_dimension=0, tiled=True)]
  transfers between devices with their start and end apart: 12 -> 12, of which waited for: 6 -> 7; matrix products, arithmetic and copies ran while one was open for 6% -> 6% of each run, Pallas kernels for 43% -> 42%
where the time goes in v6:
time: 519 us; the launch traced here: 509 us
  Pallas kernels  349 us (67%)
  waiting for transfers between devices  77.9 us (15%)
  local copies, waits for them, and re-layouts  31.3 us (6%)
  other arithmetic  23.3 us (4%)
  between operations  14.6 us (3%)
  starting transfers between devices  12.6 us (2%)
    pallas_call x1, Pallas kernels, close(): pl.pallas_call(functools.partial(close_kernel, count, shards), in_specs=[...  85.2 us
    pallas_call x1, Pallas kernels, feedforward(): pl.pallas_call(functools.partial(feedforward_kernel, count), in_specs=[hb...  79 us
    pallas_call x1, Pallas kernels, begin(): pl.pallas_call(functools.partial(begin_kernel, shards), in_specs=[hbm, vm...  58.7 us
    pallas_call x1, Pallas kernels, mix(): pl.pallas_call(functools.partial(mix_kernel, count), in_specs=[hbm, hbm,...  48 us
    pallas_call x2, Pallas kernels, attention_backward(): pl.pallas_call(functools.partial(attention_backward_kernel, rest is None,...  35 us
    reduce_scatter x3, waiting for transfers between devices, reduce_fsdp(): return lax.psum_scatter(part, 'fsdp', scatter_dimension=0, tiled=True)  31.7 us
    unnamed x105, local copies, waits for them, and re-layouts  25.6 us
    ppermute x2, waiting for transfers between devices, from_chips(): lax.ppermute(rows, 'tp', chip_shift(k))  21.4 us
  transfers between devices with their start and end apart: 12, of which 7 were waited for; matrix products, arithmetic and copies ran while one was open for 6% of the time, Pallas kernels for 42%

profile of v6, /device:TPU:0, one launch (start us, length us, event | category | flops | bytes accessed | tf_op | source)
XLA Modules:
  0.0 508.9 jit_solution(9489514780257976162)
XLA Ops:
  11.7 58.7 %norm_and_gather.1 = (bf16[1536,1536]{1,0:T(8,128)(2,1)}, bf16[1536,768]{1,0:T(8,128)(2,1)}, bf16[1536,384]{1,0:T(8,128)(2,1)S(1)}, bf16[1536,512]{1,0:T(8,128)(2,1)S(1)}, f32[8,1536]{1,0:T(8,128)S(1)}) custom-call(f32[1536,1536]{1,0:T(8,128)} %x_ref.5, bf16[384,768]{1,0:T(8,128)(2,1)S(1)} %pad_maximum_fusion.4.qkv_ref, bf16[384,384]{1,0:T(8,128)(2,1)S(1)} %bitcast.17, ...), custom_call_target="tpu_custom_call" | custom-call | bytes 125829120 | tf_op jit(solution)/shard_map/norm_and_gather/pallas_call | solution.py:961
  73.1 2.8 fusion.7
  78.5 11.6 %project_qkv.1 = (bf16[1536,512]{1,0:T(8,128)(2,1)S(1)}, bf16[1536,512]{1,0:T(8,128)(2,1)S(1)}, bf16[1536,384]{1,0:T(8,128)(2,1)S(1)}) custom-call(bf16[1536,1536]{1,0:T(8,128)(2,1)} %get-tuple-element.50.n_ref, bf16[1536,768]{1,0:T(8,128)(2,1)S(1)} %copy-done.1, bf16[768,1024]{1,0:T(8,128)(2,1)S(1)} %copy-done.18, ...), custom_call_target="tpu_custom_call" | custom-call | flops 4831838208 | bytes 16777216 | tf_op jit(solution)/shard_map/project_qkv/pallas_call | solution.py:1024
  90.1 2.9 collective-permute-start
  94.7 12.7 %attention_forward.2 = (f32[3,2,1,1024]{3,2,1,0:T(1,128)S(1)}, f32[3,2,128,1024]{3,2,1,0:T(8,128)S(1)}) custom-call(s32[3]{0:T(128)S(1)} %get-tuple-element.131.ends_ref, s32[1]{0:T(128)} %bitcast.2.base_ref, bf16[1536,512]{1,0:T(8,128)(2,1)S(1)} %get-tuple-element.52.q_ref, bf16[1536,512]{1,0:T(8,128)(2,1)S(1)} %get-tuple-element.54.kv_ref), custom_call_target="tpu_custom_call" | custom-call | flops 4831838208 | bytes 8388608 | tf_op jit(solution)/shard_map/attention_forward/pallas_call | solution.py:210
  107.4 8.8 %collective-permute-done.kv_ref = bf16[1536,384]{1,0:T(8,128)(2,1)S(1)} collective-permute-done((bf16[1536,384]{1,0:T(8,128)(2,1)S(1)}, bf16[1536,384]{1,0:T(8,128)(2,1)S(1)}, u32[]{:S(2)}, u32[]{:S(2)}) %collective-permute-start) | collective-permute-done | bytes 1179680 | tf_op jit(solution)/shard_map/ppermute | solution.py:1398
  116.2 5.4 %attention_forward.3 = (bf16[1536,384]{1,0:T(8,128)(2,1)S(1)}, bf16[1536,512]{1,0:T(8,128)(2,1)S(1)}) custom-call(s32[3]{0:T(128)S(1)} %get-tuple-element.131.ends_ref, s32[1]{0:T(128)} %bitcast.2.base_ref, bf16[1536,512]{1,0:T(8,128)(2,1)S(1)} %get-tuple-element.52.q_ref, bf16[1536,384]{1,0:T(8,128)(2,1)S(1)} %collective-permute-done.kv_ref, ...), custom_call_target="tpu_custom_call" | custom-call | flops 4831838208 | bytes 8388608 | tf_op jit(solution)/shard_map/attention_forward/pallas_call | solution.py:210
  122.8 48.0 %mix_heads.1 = (bf16[1536,1536]{1,0:T(8,128)(2,1)S(1)}, f32[384,1536]{1,0:T(8,128)S(1)}, bf16[2,1536,384]{2,1,0:T(8,128)(2,1)S(1)}) custom-call(bf16[1536,384]{1,0:T(8,128)(2,1)S(1)} %get-tuple-element.57.att_ref.o_ref, f32[1536,1536]{1,0:T(8,128)} %x_ref.5, f32[1,1536]{1,0:T(1,128)S(1)} %get-tuple-element.126.gain_ref, bf16[1536,384]{1,0:T(8,128)(2,1)S(1)} %copy-done.13, ...), custom_call_target="tpu_custom_call" | custom-call | flops 7247757312 | bytes 157286400 | tf_op jit(solution)/shard_map/mix_heads/pallas_call | solution.py:502
  174.3 2.2 copy-done.33
  177.9 12.1 %all-gather.2.cloned.1.call-done.weight_ref = bf16[1536,2560]{1,0:T(8,128)(2,1)} async-done(((bf16[192,2560]{1,0:T(8,128)(2,1)}), bf16[1536,2560]{1,0:T(8,128)(2,1)}) %all-gather.2.cloned.1.call-update) | async-done | bytes 7864336 | tf_op jit(solution)/shard_map/all_gather | solution.py:1396
  190.0 79.0 %feed_forward.1 = (bf16[4,192,1536]{2,1,0:T(8,128)(2,1)}, f32[384,1536]{1,0:T(8,128)}, bf16[384,1536]{1,0:T(8,128)(2,1)}, f32[1,1536]{1,0:T(1,128)}, bf16[1536,3...) custom-call(bf16[1536,1536]{1,0:T(8,128)(2,1)} %copy-done.33, f32[1536,1536]{1,0:T(8,128)} %cot_ref.1, ...), custom_call_target="tpu_custom_call" | custom-call | flops 43486543872 | bytes 293601280 | tf_op jit(solution)/shard_map/feed_forward/pallas_call | solution.py:772
  273.4 6.2 %attention_backward.2 = (f32[1536,512]{1,0:T(8,128)}, bf16[1536,512]{1,0:T(8,128)(2,1)S(1)}) custom-call(s32[3]{0:T(128)S(1)} %get-tuple-element.131.ends_ref, s32[1]{0:T(128)} %bitcast.2.base_ref, bf16[1536,512]{1,0:T(8,128)(2,1)} %copy-done.34, bf16[1536,384]{1,0:T(8,128)(2,1)S(1)} %copy-done.36, bf16[1536,384]{1,0:T(8,128)(2,1)S(1)} %copy-done.31, ...), custom_call_target="tpu_custom_call" | custom-call | flops 12079595520 | bytes 12582912 | tf_op jit(solution)/shard_map/attention_backward/pallas_call | solution.py:336
  282.2 28.8 %attention_backward.3 = (bf16[1536,384]{1,0:T(8,128)(2,1)S(1)}, f32[1536,512]{1,0:T(8,128)}) custom-call(s32[3]{0:T(128)S(1)} %get-tuple-element.131.ends_ref, s32[1]{0:T(128)} %bitcast.2.base_ref, bf16[1536,512]{1,0:T(8,128)(2,1)} %copy-done.34, bf16[1536,384]{1,0:T(8,128)(2,1)S(1)} %copy-done.36, bf16[1536,384]{1,0:T(8,128)(2,1)S(1)} %copy-done.31, ...), custom_call_target="tpu_custom_call" | custom-call | flops 12079595520 | bytes 12582912 | tf_op jit(solution)/shard_map/attention_backward/pallas_call | solution.py:336
  313.6 12.5 %collective-permute-done.4.rest_1_ = bf16[384,1536]{1,0:T(8,128)(2,1)} collective-permute-done((bf16[384,1536]{1,0:T(8,128)(2,1)S(1)}, bf16[384,1536]{1,0:T(8,128)(2,1)}, u32[]{:S(2)}, u32[]{:S(2)}) %collective-permute-start.4) | collective-permute-done | bytes 1179680 | tf_op jit(solution)/shard_map/ppermute | solution.py:1433
  327.3 13.5 %dense_gradients.1 = (bf16[1536,768]{1,0:T(8,128)(2,1)}, bf16[1536,1152]{1,0:T(8,128)(2,1)}) custom-call(bf16[1536,384]{1,0:T(8,128)(2,1)S(1)} %get-tuple-element.71.dq_ref, f32[1536,512]{1,0:T(8,128)} %get-tuple-element.72.dkv_ref, bf16[1536,512]{1,0:T(8,128)(2,1)} %copy-done.45, f32[1536,128]{1,0:T(8,128)S(1)} %copy-done.8, ...), custom_call_target="tpu_custom_call" | custom-call | flops 5435817984 | bytes 25165824 | tf_op jit(solution)/shard_map/dense_gradients/pallas_call | solution.py:1090
  340.8 8.9 %collective-permute-done.5.rest_1_ = bf16[384,1536]{1,0:T(8,128)(2,1)S(1)} collective-permute-done((bf16[384,1536]{1,0:T(8,128)(2,1)S(1)}, bf16[384,1536]{1,0:T(8,128)(2,1)S(1)}, u32[]{:S(2)}, u32[]{:S(2)}) %collective-permute-start.5) | collective-permute-done | bytes 1179680 | tf_op jit(solution)/shard_map/ppermute | solution.py:1433
  353.1 85.2 %close_layer.1 = (bf16[1536,1536]{1,0:T(8,128)(2,1)}, f32[8,1536]{1,0:T(8,128)S(1)}, bf16[768,1152]{1,0:T(8,128)(2,1)}, bf16[1536,1536]{1,0:T(8,128)(2,1)}, f32[384,1024]{1,0:T(8,128)S(1)}) custom-call(bf16[1536,768]{1,0:T(8,128)(2,1)} %get-tuple-element.75.dense_ref, bf16[1536,768]{1,0:T(8,128)(2,1)} %get-tuple-element.51.qkv_ref.w_ref, ...), custom_call_target="tpu_custom_call" | custom-call | flops 3623878656 | bytes 209715200 | tf_op jit(solution)/shard_map/close_layer/pallas_call | solution.py:1267
  438.4 5.5 %reduce-scatter.6.cloned.1.call-done = bf16[384,2048]{1,0:T(8,128)(2,1)} async-done(((bf16[1536,2048]{1,0:T(8,128)(2,1)}), bf16[384,2048]{1,0:T(8,128)(2,1)}) %reduce-scatter.6.cloned.1.call-update) | async-done | bytes 1572880 | tf_op jit(solution)/shard_map/reduce_scatter | solution.py:1355
  445.4 7.6 %convert_element_type.46 = f32[1536,1536]{1,0:T(8,128)} convert(bf16[1536,1536]{1,0:T(8,128)(2,1)} %get-tuple-element.81) | non-fusion elementwise | flops 2359296 | bytes 14155776 | tf_op jit(solution)/shard_map/convert_element_type | solution.py:1445
  453.0 5.1 convert_element_type.47
  458.7 26.2 %reduce-scatter.8.cloned.1.call-done = bf16[192,1152]{1,0:T(8,128)(2,1)} async-done(((bf16[768,1152]{1,0:T(8,128)(2,1)}), bf16[192,1152]{1,0:T(8,128)(2,1)}) %reduce-scatter.8.cloned.1.call-update) | async-done | bytes 442384 | tf_op jit(solution)/shard_map/reduce_scatter | solution.py:1355
  486.4 2.5 convert_add_fusion
  490.8 3.1 copy.49
  493.9 3.0 collective-permute-done.6
  (147 shorter events, 41.9 us)
Async XLA Ops:
  7.2 182.8 %all-gather.2.cloned.1.call-start = ((), (), s32[]{:S(2)}) async-start(), calls=%async_computation.3 | async-start | bytes 8847360 | tf_op jit(solution)/shard_map/all_gather | solution.py:1396
  11.6 58.8 %copy-start = (bf16[192,2560]{1,0:T(8,128)(2,1)}, bf16[192,2560]{1,0:T(8,128)(2,1)S(1)}, u32[]{:S(2)}) copy-start(bf16[192,2560]{1,0:T(8,128)(2,1)S(1)} %fusion.3.order_ref) | copy-start | bytes 2949124
  11.6 61.0 %copy-start.44 = (s32[1,3]{1,0:T(1,128)S(1)}, s32[1,3]{1,0:T(1,128)}, u32[]{:S(2)}) copy-start(s32[1,3]{1,0:T(1,128)} %param.24) | copy-start | bytes 40
  72.6 278.1 %reduce-scatter.4.cloned.1.call-start = ((), (), s32[]{:S(2)}) async-start(), calls=%async_computation.4 | async-start | bytes 3932160 | tf_op jit(solution)/shard_map/reduce_scatter | solution.py:1355
  78.5 14.6 %copy-start.13 = (bf16[1536,384]{1,0:T(8,128)(2,1)S(1)}, bf16[1536,384]{1,0:T(8,128)(2,1)}, u32[]{:S(2)}) copy-start(bf16[1536,384]{1,0:T(8,128)(2,1)} %copy-done.12) | copy-start | bytes 3538948
  90.1 17.3 %copy-start.32 = (bf16[1536,512]{1,0:T(8,128)(2,1)}, bf16[1536,512]{1,0:T(8,128)(2,1)S(1)}, u32[]{:S(2)}) copy-start(bf16[1536,512]{1,0:T(8,128)(2,1)S(1)} %get-tuple-element.54.kv_ref) | copy-start | bytes 4718596
  90.1 26.1 %collective-permute-start = (bf16[1536,384]{1,0:T(8,128)(2,1)S(1)}, bf16[1536,384]{1,0:T(8,128)(2,1)S(1)}, u32[]{:S(2)}, u32[]{:S(2)}) collective-permute-start(bf16[1536,384]{1,0:T(8,128)(2,1)S(1)} %get-tuple-element.53), channel_id=1, source_target_pairs={{0,4},{1,5},{2,6},{3,7},{8,12},{9,13},{10,14},{11,15},{16,20},{17,... | collective-permute-start | bytes 3538952 | tf_op jit(solution)/shard_map/ppermute | solution.py:1398
  93.0 29.8 %collective-permute-start.1 = (bf16[1536,384]{1,0:T(8,128)(2,1)S(1)}, bf16[1536,384]{1,0:T(8,128)(2,1)S(1)}, u32[]{:S(2)}, u32[]{:S(2)}) collective-permute-start(bf16[1536,384]{1,0:T(8,128)(2,1)S(1)} %copy-done.13), channel_id=1, source_target_pairs={{0,2},{1,3},{2,0},{3,1},{4,6},{5,7},{6,4},{7,5},{8,10},{9,11},{10,... | collective-permute-start | bytes 3538952 | tf_op jit(solution)/shard_map/ppermute | solution.py:1406
  94.6 28.2 %copy-start.10 = (f32[1,1536]{1,0:T(1,128)}, f32[1,1536]{1,0:T(1,128)S(1)}, u32[]{:S(2)}) copy-start(f32[1,1536]{1,0:T(1,128)S(1)} %get-tuple-element.126.gain_ref) | copy-start | bytes 18436
  94.6 21.6 %copy-start.21 = (bf16[384,512]{1,0:T(8,128)(2,1)S(1)}, bf16[384,512]{1,0:T(8,128)(2,1)}, u32[]{:S(2)}) copy-start(bf16[384,512]{1,0:T(8,128)(2,1)} %constant.63.clone.rest_0_) | copy-start | bytes 1179652
  94.6 21.6 %copy-start.23 = (bf16[512,384]{1,0:T(8,128)(2,1)S(1)}, bf16[512,384]{1,0:T(8,128)(2,1)}, u32[]{:S(2)}) copy-start(bf16[512,384]{1,0:T(8,128)(2,1)} %constant.65.clone.rest_2_) | copy-start | bytes 1179652
  94.7 21.6 %copy-start.27 = (f32[1,512]{1,0:T(1,128)S(1)}, f32[1,512]{1,0:T(1,128)}, u32[]{:S(2)}) copy-start(f32[1,512]{1,0:T(1,128)} %constant.64.clone.rest_1_) | copy-start | bytes 6148
  269.0 174.9 %reduce-scatter.6.cloned.1.call-start = ((), (), s32[]{:S(2)}) async-start(), calls=%async_computation.5 | async-start | bytes 7864320 | tf_op jit(solution)/shard_map/reduce_scatter | solution.py:1355
  269.7 215.3 %reduce-scatter.8.cloned.1.call-start = ((), (), s32[]{:S(2)}) async-start(), calls=%async_computation.6 | async-start | bytes 2211840 | tf_op jit(solution)/shard_map/reduce_scatter | solution.py:1355
  271.8 39.2 %collective-permute-start.2 = (bf16[384,1536]{1,0:T(8,128)(2,1)S(1)}, bf16[384,1536]{1,0:T(8,128)(2,1)}, u32[]{:S(2)}, u32[]{:S(2)}) collective-permute-start(bf16[384,1536]{1,0:T(8,128)(2,1)S(1)} %bitcast.21), channel_id=1, source_target_pairs={{0,2},{1,3},{2,0},{3,1},{4,6},{5,7},{6,4},{7,5},{8,10},{9,11},{10,... | collective-permute-start | bytes 3538952 | tf_op jit(solution)/shard_map/ppermute | solution.py:1415
  279.5 46.6 %collective-permute-start.3 = (bf16[1536,512]{1,0:T(8,128)(2,1)S(1)}, bf16[1536,512]{1,0:T(8,128)(2,1)S(1)}, u32[]{:S(2)}, u32[]{:S(2)}) collective-permute-start(bf16[1536,512]{1,0:T(8,128)(2,1)S(1)} %get-tuple-element.73), channel_id=1, source_target_pairs={{4,0},{5,1},{6,2},{7,3},{12,8},{13,9},{14,10},{15,11},{20,16},{21,... | collective-permute-start | bytes 4718600 | tf_op jit(solution)/shard_map/ppermute | solution.py:1420
  280.8 45.3 %collective-permute-start.4 = (bf16[384,1536]{1,0:T(8,128)(2,1)S(1)}, bf16[384,1536]{1,0:T(8,128)(2,1)}, u32[]{:S(2)}, u32[]{:S(2)}) collective-permute-start(bf16[384,1536]{1,0:T(8,128)(2,1)S(1)} %copy-done.14), channel_id=1, source_target_pairs={{0,2},{1,3},{2,0},{3,1},{4,6},{5,7},{6,4},{7,5},{8,10},{9,11},{10,... | collective-permute-start | bytes 3538952 | tf_op jit(solution)/shard_map/ppermute | solution.py:1433
  282.2 28.8 %copy-start.3 = (f32[384,1536]{1,0:T(8,128)S(1)}, f32[384,1536]{1,0:T(8,128)}, u32[]{:S(2)}) copy-start(f32[384,1536]{1,0:T(8,128)} %copy-done.2) | copy-start | bytes 7077892
  311.0 16.3 %copy-start.25 = (bf16[256,192]{1,0:T(8,128)(2,1)S(1)}, bf16[256,192]{1,0:T(8,128)(2,1)}, u32[]{:S(2)}) copy-start(bf16[256,192]{1,0:T(8,128)(2,1)} %constant.68.clone.rotk_ref) | copy-start | bytes 294916
  311.0 16.2 %copy-start.26 = (bf16[256,192]{1,0:T(8,128)(2,1)S(1)}, bf16[256,192]{1,0:T(8,128)(2,1)}, u32[]{:S(2)}) copy-start(bf16[256,192]{1,0:T(8,128)(2,1)} %constant.69.clone.valk_ref) | copy-start | bytes 294916
  312.8 36.9 %collective-permute-start.5 = (bf16[384,1536]{1,0:T(8,128)(2,1)S(1)}, bf16[384,1536]{1,0:T(8,128)(2,1)S(1)}, u32[]{:S(2)}, u32[]{:S(2)}) collective-permute-start(bf16[384,1536]{1,0:T(8,128)(2,1)S(1)} %fusion.1.rest_0_), channel_id=1, source_target_pairs={{0,2},{1,3},{2,0},{3,1},{4,6},{5,7},{6,4},{7,5},{8,10},{9,11},{10,... | collective-permute-start | bytes 3538952 | tf_op jit(solution)/shard_map/ppermute | solution.py:1433
  327.3 23.4 %copy-start.9 = (f32[1,1536]{1,0:T(1,128)S(1)}, f32[1,1536]{1,0:T(1,128)}, u32[]{:S(2)}) copy-start(f32[1,1536]{1,0:T(1,128)} %get-tuple-element.77.gain_two_ref) | copy-start | bytes 18436
  443.9 42.6 %collective-permute-start.7 = (bf16[384,2048]{1,0:T(8,128)(2,1)}, bf16[384,2048]{1,0:T(8,128)(2,1)}, u32[]{:S(2)}, u32[]{:S(2)}) collective-permute-start(bf16[384,2048]{1,0:T(8,128)(2,1)} %reduce-scatter.6.cloned.1.call-done), channel_id=1, source_target_pairs={{0,4},{4,0},{1,5},{5,1},{2,6},{6,2},{3,7},{7,3},{8,12},{12,8},{9,1... | collective-permute-start | bytes 4718600 | tf_op jit(solution)/shard_map/ppermute | solution.py:1358
  485.0 11.9 %collective-permute-start.6 = (bf16[192,1152]{1,0:T(8,128)(2,1)}, bf16[192,1152]{1,0:T(8,128)(2,1)S(1)}, u32[]{:S(2)}, u32[]{:S(2)}) collective-permute-start(bf16[192,1152]{1,0:T(8,128)(2,1)} %reduce-scatter.8.cloned.1.call-done), channel_id=1, source_target_pairs={{0,4},{4,0},{1,5},{5,1},{2,6},{6,2},{3,7},{7,3},{8,12},{12,8},{9,1... | collective-permute-start | bytes 1327112 | tf_op jit(solution)/shard_map/ppermute | solution.py:1361
  (36 other events, 119.0 us)
Sparse Core Ops, SparseCore 0:
  72.7 117.1 all-gather.1
  269.1 58.4 reduce-scatter.3
  329.9 113.8 reduce-scatter.5
  446.0 38.9 reduce-scatter.7
